TPU v7x, 512 devices: a whole 4x4x16 slice. The times are simulated.
512 devices in a mesh: pipe: 16 (over y, x_hi, core), expert: 32 (over z, x_lo).
Axes of the slice: x: 4 (x_hi: 2, x_lo: 2; x = x_hi * 2 + x_lo), y: 4, z: 16, core: 2. Of those that a mesh axis runs over, the one named last changes fastest.
Arguments:
- tokens: bfloat16 [16, 4096, 3584], P('pipe', 'expert'), may hold values from -6 to 6
- expert_ids: int32 [16, 4096, 8], P('pipe', 'expert'), may hold values from 0 to 255, as said below
- gates: float32 [16, 4096, 8], P('pipe', 'expert'), may hold values from 0.1 to 1
- loss_weight: float32 [16, 4096], P('pipe', 'expert'), may hold values from 0.25 to 4
- w_gate: bfloat16 [16, 3584, 4096], P('pipe', None, 'expert'), may hold values from -0.09375 to 0.09375
- w_up: bfloat16 [16, 3584, 4096], P('pipe', None, 'expert'), may hold values from -0.09375 to 0.09375
- w_down: bfloat16 [16, 4096, 3584], P('pipe', 'expert'), may hold values from -0.1875 to 0.1875
Outputs:
- mixed: bfloat16 [16, 4096, 3584], P('pipe', 'expert')
- down_grad: bfloat16 [16, 4096, 1792], P('pipe', 'expert')
Inputs may be any that keep to these rules, and one draw needn't show every extreme that they name: `expert_ids`: each token names 8 different experts. In every block of 128 tokens of one section slot, each expert below 4 is named by 1 to 16 tokens; for each section slot one of these experts is named by exactly 16 tokens in every block.
All inputs are finite; a program needn't handle non-finite values.
Results may differ from a plain program's by a relative error of at most 0.0074.
Values may be sent and summed in bfloat16 or wider, within the bound.
No kernel may reach another device: no remote copies, remote signals or barrier semaphores. Data moves between devices by JAX's collectives and lax.ppermute only.
A program may use at most 64 MiB of HBM per device.

v0:
```python
import jax
import jax.numpy as jnp
from jax import lax
from jax.sharding import PartitionSpec as P

SPLIT = 8
CAP = 16


def partner_2(block, axis, distance):
    count = lax.axis_size(axis)
    route = []
    for low in range(count):
        high = low | 1 << distance
        if high != low and high < count:
            route += [(low, high), (high, low)]
    return lax.ppermute(block, axis, route)


def routing(routed, gate_vals, window):
    experts = jnp.arange(window, dtype=jnp.int32)
    hits = routed[:, :, None] == experts[None, None, :]
    member = jnp.any(hits, axis=1)
    weights = jnp.sum(jnp.where(hits, gate_vals[:, :, None], jnp.float32(0.0)), axis=1)
    ranking = jnp.cumsum(member.astype(jnp.int32), axis=0) - 1
    slot_ids = jnp.arange(CAP, dtype=jnp.int32)
    matched = member[:, :, None] & (ranking[:, :, None] == slot_ids[None, None, :])
    return (matched, weights)


def per_device(tokens, expert_ids, gates, loss_weight, w_gate, w_up, w_down):
    tok_rows = tokens[0]
    weighting = loss_weight[0]
    gate_cols = w_gate[0]
    up_cols = w_up[0]
    down_rows = w_down[0]
    tok_count = tok_rows.shape[0]
    model_width = tok_rows.shape[1]
    window = lax.axis_size("expert") // SPLIT
    matched, weights = routing(expert_ids[0], gates[0], window)
    selector = matched.reshape(tok_count, window * CAP)
    picker = selector.astype(jnp.bfloat16).T
    picked = jnp.dot(picker, tok_rows, preferred_element_type=jnp.float32).astype(jnp.bfloat16)
    outbound = jnp.repeat(picked.reshape(window, CAP, model_width), SPLIT, axis=0)
    inbound = lax.all_to_all(outbound, "expert", split_axis=0, concat_axis=0, tiled=True)
    gate_act = jnp.einsum("rcd,dh->rch", inbound, gate_cols, preferred_element_type=jnp.float32)
    up_act = jnp.einsum("rcd,dh->rch", inbound, up_cols, preferred_element_type=jnp.float32)
    hidden = (jax.nn.silu(gate_act) * up_act).astype(jnp.bfloat16)
    partial_value = jnp.einsum(
        "rch,hd->rcd", hidden, down_rows, preferred_element_type=jnp.float32
    ).astype(jnp.bfloat16)
    hidden, partial_value = (hidden, partial_value)
    returned = lax.all_to_all(partial_value, "expert", split_axis=0, concat_axis=0, tiled=True)
    summed = jnp.sum(returned.reshape(window, SPLIT, CAP, model_width).astype(jnp.float32), axis=1)
    summed = summed.reshape(window * CAP, model_width)
    spread = jnp.where(selector, jnp.repeat(weights, CAP, axis=1), jnp.float32(0.0))
    mixed = jnp.dot(
        spread, summed, precision=lax.Precision.HIGHEST, preferred_element_type=jnp.float32
    )
    output = mixed.astype(jnp.bfloat16)
    slope = weighting[:, None] * output.astype(jnp.float32)
    cotan = jnp.dot(
        spread.T, slope, precision=lax.Precision.HIGHEST, preferred_element_type=jnp.float32
    )
    cotan = cotan.astype(jnp.bfloat16).reshape(window, CAP, model_width)
    inbound_cotan = lax.all_to_all(
        jnp.repeat(cotan, SPLIT, axis=0), "expert", split_axis=0, concat_axis=0, tiled=True
    )
    grads = jnp.einsum("rch,rcd->hd", hidden, inbound_cotan, preferred_element_type=jnp.float32)
    pipe_count = lax.axis_size("pipe")
    partner_bit = pipe_count.bit_length() - 2
    side = lax.axis_index("pipe") // (pipe_count // 2)
    width_half = model_width // 2
    partner = partner_2(grads, "pipe", partner_bit)
    total = grads + partner
    share = lax.dynamic_slice_in_dim(total, side * width_half, width_half, 1)
    return (output[None], share.astype(jnp.bfloat16)[None])


def solution(mesh):
    in_specs = (
        P("pipe", "expert", None),
        P("pipe", "expert", None),
        P("pipe", "expert", None),
        P("pipe", "expert"),
        P("pipe", None, "expert"),
        P("pipe", None, "expert"),
        P("pipe", "expert", None),
    )
    out_specs = (P("pipe", "expert", None), P("pipe", "expert", None))
    return jax.shard_map(
        per_device, mesh=mesh, in_specs=in_specs, out_specs=out_specs, check_vma=False
    )
```

profile of v0, /device:TPU:2, one launch (start us, length us, event | category | flops | bytes accessed | tf_op | source)
XLA Modules:
  0.0 588.7 jit_solution(4684130852146520814)
XLA Ops:
  0.6 0.0 copy-start
  0.6 0.8 fusion.17
  1.4 0.1 copy.21
  1.6 0.2 reduce_window_sum.11
  1.7 0.1 copy.22
  1.8 1.5 convolution_convert_fusion.1
  3.3 0.4 broadcast_in_dim.44
  3.7 0.0 copy-start.2
  3.7 184.1 %all_to_all.15 = bf16[32,16,3584]{2,1,0:T(8,128)(2,1)S(1)} all-to-all(bf16[32,16,3584]{2,1,0:T(8,128)(2,1)S(1)} %bitcast.53), channel_id=1, replica_groups=mesh['pipe'=16,'expert'=32] {'expert'}, dimensions={0} | all-to-all | bytes 7340032 | tf_op jit(solution)/shard_map/all_to_all | solution.py:45
  187.9 0.0 copy-done.2
  187.9 1.1 fusion.7
  189.0 0.1 copy-done.6
  189.0 1.1 fusion.3
  190.2 0.0 copy-done
  190.2 2.9 convolution_convert_fusion
  193.1 5.1 all-to-all-start.1
  198.2 0.0 copy-start.5
  198.2 0.1 eq.56
  198.3 0.0 copy-done.3
  198.3 0.0 copy-done.4
  198.3 0.1 bitcast_select_fusion
  198.4 166.2 %all-to-all-done.1 = bf16[32,16,3584]{2,1,0:T(8,128)(2,1)} async-done(((bf16[32,16,3584]{2,1,0:T(8,128)(2,1)}), bf16[32,16,3584]{2,1,0:T(8,128)(2,1)}, u32[]{:S(2)}, u32[]{:S(2)}) %all-to-all-start.1) | async-done | bytes 3670048 | tf_op jit(solution)/shard_map/all_to_all | solution.py:53
  364.6 2.6 convert_reduce_fusion
  367.3 1.6 fusion
  368.9 0.0 copy-start.1
  369.0 1.3 convolution_convert_fusion.2
  370.3 0.4 broadcast_in_dim.47
  370.7 170.9 %all_to_all.16 = bf16[32,16,3584]{2,1,0:T(8,128)(2,1)S(1)} all-to-all(bf16[32,16,3584]{2,1,0:T(8,128)(2,1)S(1)} %bitcast.54), channel_id=1, replica_groups=mesh['pipe'=16,'expert'=32] {'expert'}, dimensions={0} | all-to-all | bytes 7340032 | tf_op jit(solution)/shard_map/all_to_all | solution.py:66
  541.6 0.7 convolution_bitcast_fusion
  542.3 5.1 collective-permute-start
  547.4 39.3 %collective-permute-done = f32[128,3584]{1,0:T(8,128)} collective-permute-done((f32[128,3584]{1,0:T(8,128)S(1)}, f32[128,3584]{1,0:T(8,128)}, u32[]{:S(2)}, u32[]{:S(2)}) %collective-permute-start) | collective-permute-done | bytes 1835040 | tf_op jit(solution)/shard_map/ppermute | solution.py:17
  586.7 2.0 fusion.11
  (10 shorter events, 0.1 us)
Async XLA Ops:
  0.6 189.5 %copy-start = (bf16[1,128,3584]{2,1,0:T(8,128)(2,1)S(1)}, bf16[1,128,3584]{2,1,0:T(8,128)(2,1)}, u32[]{:S(2)}) copy-start(bf16[1,128,3584]{2,1,0:T(8,128)(2,1)} %param.13) | copy-start | bytes 2752516
  3.7 184.1 %copy-start.2 = (bf16[1,3584,128]{2,1,0:T(8,128)(2,1)S(1)}, bf16[1,3584,128]{2,1,0:T(8,128)(2,1)}, u32[]{:S(2)}) copy-start(bf16[1,3584,128]{2,1,0:T(8,128)(2,1)} %param.11) | copy-start | bytes 2752516
  187.9 1.2 copy-start.6
  193.1 5.2 copy-start.3
  193.1 5.2 copy-start.4
  193.1 171.5 %all-to-all-start.1 = ((bf16[32,16,3584]{2,1,0:T(8,128)(2,1)}), bf16[32,16,3584]{2,1,0:T(8,128)(2,1)}, u32[]{:S(2)}, u32[]{:S(2)}) async-start(bf16[32,16,3584]{2,1,0:T(8,128)(2,1)} %convolution_convert_fusion), calls=%async_computation.1 | async-start | bytes 7340032 | tf_op jit(solution)/shard_map/all_to_all | solution.py:53
  198.2 170.8 %copy-start.5 = (f32[1,128]{1,0:T(1,128)S(1)}, f32[1,128]{1,0:T(1,128)}, u32[]{:S(2)}) copy-start(f32[1,128]{1,0:T(1,128)} %param.10) | copy-start | bytes 1540
  368.9 1.3 copy-start.1
  542.3 44.5 %collective-permute-start = (f32[128,3584]{1,0:T(8,128)S(1)}, f32[128,3584]{1,0:T(8,128)}, u32[]{:S(2)}, u32[]{:S(2)}) collective-permute-start(f32[128,3584]{1,0:T(8,128)S(1)} %convolution_bitcast_fusion), channel_id=1, source_target_pairs={{0,256},{256,0},{32,288},{288,32},{64,320},{320,64},{96,352},{352,... | collective-permute-start | bytes 5505032 | tf_op jit(solution)/shard_map/ppermute | solution.py:17
where the time goes:
time: 589 us
  blocking collectives  355 us (60%)
  waiting for transfers between devices  206 us (35%)
  matrix products  10.2 us (2%)
  starting transfers between devices  10.2 us (2%)
    all_to_all x1, blocking collectives, per_device(): lax.all_to_all(outbound, 'expert', split_axis=0, concat_axis=0, tiled=True)  184 us
    all_to_all x1, blocking collectives, per_device(): lax.all_to_all(jnp.repeat(cotan, SPLIT, axis=0), 'expert', split_axis=0,...  171 us
    all_to_all x1, waiting for transfers between devices, per_device(): lax.all_to_all(partial_value, 'expert', split_axis=0, concat_axis=0, tile...  166 us
    ppermute x1, waiting for transfers between devices, partner_2(): return lax.ppermute(block, axis, route)  39.3 us
  transfers between devices with their start and end apart: 2, of which 2 were waited for; matrix products, arithmetic and copies ran while one was open for 0% of the time, Pallas kernels for 0%

commit v1 on v0

v1 whole, which is shorter than its diff:
```python
import jax
import jax.numpy as jnp
from jax import lax
from jax.sharding import PartitionSpec as P

SPLIT = 8
CAP = 16
QUADS = 4
BF16 = jnp.bfloat16
F32 = jnp.float32


def segment_shift(block, distance):
    count = lax.axis_size("expert")
    step = (distance * SPLIT) % count
    if step == 0:
        return block
    return lax.ppermute(block, "expert", [(i, (i + step) % count) for i in range(count)])


def quad_from(block, distance):
    if distance % QUADS == 0:
        return block
    count = lax.axis_size("expert")
    route = []
    for i in range(count):
        base, place, side = i // SPLIT * SPLIT, i % SPLIT // 2, i % 2
        source = base + (place + distance) % QUADS * 2 + side
        route.append((source, i))
    return lax.ppermute(block, "expert", route)


def cross_pair(block, flip_side, flip_pipe):
    pipes, count = lax.axis_size("pipe"), lax.axis_size("expert")
    route = []
    for p in range(pipes):
        for i in range(count):
            other = (p + pipes // 2) % pipes if flip_pipe else p
            route.append((p * count + i, other * count + (i ^ 1 if flip_side else i)))
    return lax.ppermute(block, ("pipe", "expert"), route)


def routing(routed, gate_vals, experts):
    hits = routed[:, :, None] == experts[None, None, :]
    weights = jnp.sum(jnp.where(hits, gate_vals[:, :, None], jnp.float32(0.0)), axis=1)
    member = jnp.any(hits, axis=1)
    ranking = jnp.cumsum(member.astype(jnp.int32), axis=0) - 1
    ranking = jnp.where(member, ranking, CAP)
    return weights, ranking


def matching(ranking):
    slots = jnp.arange(CAP, dtype=jnp.int32)
    return ranking[..., None] == slots


def pick(array, index):
    return lax.dynamic_index_in_dim(array, index, 0, keepdims=False)


def per_device(tokens, expert_ids, gates, loss_weight, w_gate, w_up, w_down):
    tok_rows = tokens[0]
    tok_count, width = tok_rows.shape
    units = w_down.shape[1]
    experts = lax.axis_size("expert") // SPLIT
    eighth = width // 8
    place = lax.axis_index("expert")
    segment = place // SPLIT
    quad = place % SPLIT // 2
    half = lax.axis_index("pipe") // (lax.axis_size("pipe") // 2)

    gate_up = jnp.concatenate([w_gate[0], w_up[0]], axis=1)
    gate_up_other = cross_pair(gate_up, True, False)

    near = (segment + jnp.arange(experts, dtype=jnp.int32)) % experts
    weights, ranking = routing(expert_ids[0], gates[0], near)
    selector = matching(ranking).reshape(tok_count, experts * CAP)
    picked = jnp.dot(selector.astype(BF16).T, tok_rows, preferred_element_type=F32).astype(BF16)
    picked = picked.reshape(experts, CAP, width)
    rows = jnp.stack([segment_shift(picked[j], j) for j in range(experts)])
    rows = jnp.stack([quad_from(rows, r) for r in range(QUADS)]).reshape(-1, width)

    meta = jnp.concatenate(
        [weights.T, ranking.astype(F32).T, loss_weight, jnp.zeros((16 - 2 * experts - 1, tok_count), F32)]
    )
    metas = jnp.stack([quad_from(meta, r) for r in range(QUADS)])

    def act(both):
        acts = jnp.dot(rows, both, preferred_element_type=F32)
        return (jax.nn.silu(acts[:, :units]) * acts[:, units:]).astype(BF16)

    hidden = jnp.concatenate([act(gate_up), act(gate_up_other)], axis=1)
    hidden = hidden.reshape(QUADS, -1, 2 * units)
    hidden = jnp.concatenate(
        [jnp.roll(quad_from(hidden, r), r, axis=0) for r in range(QUADS)], axis=2
    ).reshape(-1, QUADS * 2 * units)

    quarters = w_down[0].T.reshape(2, QUADS, eighth, units).transpose(1, 0, 2, 3)
    quarters = quarters.reshape(QUADS, 2 * eighth, units)
    down_own = jnp.stack([quad_from(pick(quarters, (quad - r) % QUADS), r) for r in range(QUADS)])
    down_other = cross_pair(down_own, True, False)
    down = jnp.stack([down_own, down_other], axis=1)
    down = down.transpose(2, 0, 1, 3).reshape(2 * eighth, QUADS * 2 * units)
    out = lax.dot_general(
        hidden, down, (((1,), (1,)), ((), ())), preferred_element_type=F32
    ).astype(BF16)
    out = out.reshape(QUADS, experts, CAP, 2 * eighth)
    back = jnp.stack([segment_shift(out[:, j], -j) for j in range(experts)], axis=1)
    back = back.reshape(QUADS, experts * CAP, 2 * eighth)

    weight_r = metas[:, :experts]
    rank_r = metas[:, experts : 2 * experts].astype(jnp.int32)
    loss_r = metas[:, 2 * experts]
    spread = jnp.where(matching(rank_r), weight_r[..., None], jnp.float32(0.0))
    spread = spread.transpose(0, 2, 1, 3).reshape(QUADS, tok_count, experts * CAP)
    mixed = jnp.einsum(
        "rts,rsd->rtd", spread, back.astype(F32), precision=lax.Precision.HIGHEST,
        preferred_element_type=F32,
    ).astype(BF16)
    slope = loss_r[:, :, None] * mixed.astype(F32)
    cotan = jnp.einsum(
        "rts,rtd->rsd", spread, slope, precision=lax.Precision.HIGHEST, preferred_element_type=F32
    ).astype(BF16)
    cotan = cotan.reshape(QUADS, experts, CAP, 2 * eighth)
    cotan = jnp.stack([segment_shift(cotan[:, j], j) for j in range(experts)], axis=1)
    cotan = cotan.reshape(-1, 2 * eighth)

    pieces = jnp.stack([quad_from(mixed[-r % QUADS], r) for r in range(QUADS)])
    pieces = jnp.roll(pieces, quad, axis=0).reshape(QUADS, tok_count, 2, eighth)
    output = pieces.transpose(1, 2, 0, 3).reshape(tok_count, width)

    grads = lax.dot_general(cotan, hidden, (((0,), (0,)), ((), ())), preferred_element_type=F32)
    grads = grads.reshape(2, eighth, QUADS, 2, units).transpose(0, 3, 1, 2, 4)
    keep, give = pick(grads, half), pick(grads, 1 - half)
    total = (
        keep[0]
        + cross_pair(keep[1].astype(BF16), True, False).astype(F32)
        + cross_pair(give[0].astype(BF16), False, True).astype(F32)
        + cross_pair(give[1].astype(BF16), True, True).astype(F32)
    )
    share = total.astype(BF16)
    share = jnp.stack([quad_from(share[:, -r % QUADS], r) for r in range(QUADS)])
    share = jnp.roll(share, quad, axis=0).reshape(QUADS * eighth, units).T
    return output[None], share[None]


def solution(mesh):
    in_specs = (
        P("pipe", "expert", None),
        P("pipe", "expert", None),
        P("pipe", "expert", None),
        P("pipe", "expert"),
        P("pipe", None, "expert"),
        P("pipe", None, "expert"),
        P("pipe", "expert", None),
    )
    out_specs = (P("pipe", "expert", None), P("pipe", "expert", None))
    return jax.shard_map(
        per_device, mesh=mesh, in_specs=in_specs, out_specs=out_specs, check_vma=False
    )
```

time: 589 us -> 269 us (0.46)
  the two profiles are of different devices: /device:TPU:2 before, /device:TPU:4 now
where the time goes in v1:
time: 269 us; the launch traced here: 267 us
  starting transfers between devices  167 us (62%)
  waiting for transfers between devices  54 us (20%)
  local copies, waits for them, and re-layouts  22.9 us (9%)
  other arithmetic  14.8 us (6%)
  matrix products  7.11 us (3%)
    ppermute x18, starting transfers between devices, quad_from(): return lax.ppermute(block, 'expert', route)  83.5 us
    ppermute x9, starting transfers between devices, segment_shift(): lax.ppermute(block, 'expert', [(i, (i + step) % count) for i in range(cou...  66.4 us
    ppermute x18, waiting for transfers between devices, quad_from(): return lax.ppermute(block, 'expert', route)  22.7 us
    ppermute x5, starting transfers between devices, cross_pair(): return lax.ppermute(block, ('pipe', 'expert'), route)  16.7 us
    ppermute x9, waiting for transfers between devices, segment_shift(): lax.ppermute(block, 'expert', [(i, (i + step) % count) for i in range(cou...  15.8 us
    ppermute x5, waiting for transfers between devices, cross_pair(): return lax.ppermute(block, ('pipe', 'expert'), route)  15.6 us
    unnamed x55, local copies, waits for them, and re-layouts  9.46 us
  transfers between devices with their start and end apart: 32, of which 11 were waited for; matrix products, arithmetic and copies ran while one was open for 14% of the time, Pallas kernels for 0%

profile of v1, /device:TPU:4, one launch (start us, length us, event | category | flops | bytes accessed | tf_op | source)
XLA Modules:
  0.0 267.3 jit_solution(13115962875108462676)
XLA Ops:
  3.0 12.7 %collective-permute-start.5 = (bf16[16,3584]{1,0:T(8,128)(2,1)S(1)}, bf16[16,3584]{1,0:T(8,128)(2,1)S(1)}, u32[]{:S(2)}, u32[]{:S(2)}) collective-permute-start(bf16[16,3584]{1,0:T(8,128)(2,1)S(1)} %get-tuple-element.36), channel_id=1, source_target_pairs={{0,24},{1,25},{2,26},{3,27},{4,28},{5,29},{6,30},{7,31},{8,0},{9,1... | collective-permute-start | bytes 344072 | tf_op jit(solution)/shard_map/ppermute | solution.py:18
  15.7 4.9 %collective-permute-start.4 = (bf16[16,3584]{1,0:T(8,128)(2,1)S(1)}, bf16[16,3584]{1,0:T(8,128)(2,1)S(1)}, u32[]{:S(2)}, u32[]{:S(2)}) collective-permute-start(bf16[16,3584]{1,0:T(8,128)(2,1)S(1)} %get-tuple-element.37), channel_id=1, source_target_pairs={{0,16},{1,17},{2,18},{3,19},{4,20},{5,21},{6,22},{7,23},{8,24},{9,... | collective-permute-start | bytes 344072 | tf_op jit(solution)/shard_map/ppermute | solution.py:18
  20.6 7.8 %collective-permute-start.3 = (bf16[16,3584]{1,0:T(8,128)(2,1)S(1)}, bf16[16,3584]{1,0:T(8,128)(2,1)S(1)}, u32[]{:S(2)}, u32[]{:S(2)}) collective-permute-start(bf16[16,3584]{1,0:T(8,128)(2,1)S(1)} %get-tuple-element.38), channel_id=1, source_target_pairs={{0,8},{1,9},{2,10},{3,11},{4,12},{5,13},{6,14},{7,15},{8,16},{9,17... | collective-permute-start | bytes 344072 | tf_op jit(solution)/shard_map/ppermute | solution.py:18
  29.9 3.1 %collective-permute-start.9 = (bf16[3584,256]{1,0:T(8,128)(2,1)}, bf16[3584,256]{1,0:T(8,128)(2,1)}, u32[]{:S(2)}, u32[]{:S(2)}) collective-permute-start(bf16[3584,256]{1,0:T(8,128)(2,1)} %pad_maximum_fusion.1), channel_id=1, source_target_pairs={{0,1},{1,0},{2,3},{3,2},{4,5},{5,4},{6,7},{7,6},{8,9},{9,8},{10,11... | collective-permute-start | bytes 5505032 | tf_op jit(solution)/shard_map/ppermute | solution.py:40
  35.6 2.9 %collective-permute-start.15 = (bf16[896,128]{1,0:T(8,128)(2,1)S(1)}, bf16[896,128]{1,0:T(8,128)(2,1)}, u32[]{:S(2)}, u32[]{:S(2)}) collective-permute-start(bf16[896,128]{1,0:T(8,128)(2,1)S(1)} %get-tuple-element.19), channel_id=1, source_target_pairs={{6,0},{7,1},{0,2},{1,3},{2,4},{3,5},{4,6},{5,7},{14,8},{15,9},{8,1... | collective-permute-start | bytes 688136 | tf_op jit(solution)/shard_map/ppermute | solution.py:30
  38.5 3.4 %collective-permute-start.14 = (bf16[896,128]{1,0:T(8,128)(2,1)S(1)}, bf16[896,128]{1,0:T(8,128)(2,1)}, u32[]{:S(2)}, u32[]{:S(2)}) collective-permute-start(bf16[896,128]{1,0:T(8,128)(2,1)S(1)} %get-tuple-element.20), channel_id=1, source_target_pairs={{4,0},{5,1},{6,2},{7,3},{0,4},{1,5},{2,6},{3,7},{12,8},{13,9},{14,... | collective-permute-start | bytes 688136 | tf_op jit(solution)/shard_map/ppermute | solution.py:30
  41.9 3.8 %collective-permute-start.13 = (bf16[896,128]{1,0:T(8,128)(2,1)}, bf16[896,128]{1,0:T(8,128)(2,1)}, u32[]{:S(2)}, u32[]{:S(2)}) collective-permute-start(bf16[896,128]{1,0:T(8,128)(2,1)} %get-tuple-element.21), channel_id=1, source_target_pairs={{2,0},{3,1},{4,2},{5,3},{6,4},{7,5},{0,6},{1,7},{10,8},{11,9},{12,... | collective-permute-start | bytes 688136 | tf_op jit(solution)/shard_map/ppermute | solution.py:30
  49.5 12.2 %collective-permute-start.7 = (bf16[4,16,3584]{2,1,0:T(8,128)(2,1)S(1)}, bf16[4,16,3584]{2,1,0:T(8,128)(2,1)S(1)}, u32[]{:S(2)}, u32[]{:S(2)}) collective-permute-start(bf16[4,16,3584]{2,1,0:T(8,128)(2,1)S(1)} %get-tuple-element.34), channel_id=1, source_target_pairs={{4,0},{5,1},{6,2},{7,3},{0,4},{1,5},{2,6},{3,7},{12,8},{13,9},{14,... | collective-permute-start | bytes 1376264 | tf_op jit(solution)/shard_map/ppermute | solution.py:30
  61.6 11.3 %collective-permute-done.14 = bf16[896,128]{1,0:T(8,128)(2,1)} collective-permute-done((bf16[896,128]{1,0:T(8,128)(2,1)S(1)}, bf16[896,128]{1,0:T(8,128)(2,1)}, u32[]{:S(2)}, u32[]{:S(2)}) %collective-permute-start.14) | collective-permute-done | bytes 229408 | tf_op jit(solution)/shard_map/ppermute | solution.py:30
  77.1 5.5 %collective-permute-start.2 = (f32[16,128]{1,0:T(8,128)S(1)}, f32[16,128]{1,0:T(8,128)S(1)}, u32[]{:S(2)}, u32[]{:S(2)}) collective-permute-start(f32[16,128]{1,0:T(8,128)S(1)} %maximum_maximum_fusion), channel_id=1, source_target_pairs={{6,0},{7,1},{0,2},{1,3},{2,4},{3,5},{4,6},{5,7},{14,8},{15,9},{8,1... | collective-permute-start | bytes 24584 | tf_op jit(solution)/shard_map/ppermute | solution.py:30
  85.1 10.8 %collective-permute-start.1 = (f32[16,128]{1,0:T(8,128)S(1)}, f32[16,128]{1,0:T(8,128)}, u32[]{:S(2)}, u32[]{:S(2)}) collective-permute-start(f32[16,128]{1,0:T(8,128)S(1)} %maximum_maximum_fusion), channel_id=1, source_target_pairs={{4,0},{5,1},{6,2},{7,3},{0,4},{1,5},{2,6},{3,7},{12,8},{13,9},{14,... | collective-permute-start | bytes 24584 | tf_op jit(solution)/shard_map/ppermute | solution.py:30
  96.0 10.0 %collective-permute-start = (f32[16,128]{1,0:T(8,128)S(1)}, f32[16,128]{1,0:T(8,128)}, u32[]{:S(2)}, u32[]{:S(2)}) collective-permute-start(f32[16,128]{1,0:T(8,128)S(1)} %maximum_maximum_fusion), channel_id=1, source_target_pairs={{2,0},{3,1},{4,2},{5,3},{6,4},{7,5},{0,6},{1,7},{10,8},{11,9},{12,... | collective-permute-start | bytes 24584 | tf_op jit(solution)/shard_map/ppermute | solution.py:30
  106.0 2.7 %collective-permute-start.16 = (bf16[4,896,128]{2,1,0:T(8,128)(2,1)}, bf16[4,896,128]{2,1,0:T(8,128)(2,1)}, u32[]{:S(2)}, u32[]{:S(2)}) collective-permute-start(bf16[4,896,128]{2,1,0:T(8,128)(2,1)} %get-tuple-element.17), channel_id=1, source_target_pairs={{0,1},{1,0},{2,3},{3,2},{4,5},{5,4},{6,7},{7,6},{8,9},{9,8},{10,11... | collective-permute-start | bytes 2752520 | tf_op jit(solution)/shard_map/ppermute | solution.py:40
  117.4 11.7 %collective-permute-done.16 = bf16[4,896,128]{2,1,0:T(8,128)(2,1)} collective-permute-done((bf16[4,896,128]{2,1,0:T(8,128)(2,1)}, bf16[4,896,128]{2,1,0:T(8,128)(2,1)}, u32[]{:S(2)}, u32[]{:S(2)}) %collective-permute-start.16) | collective-permute-done | bytes 917536 | tf_op jit(solution)/shard_map/ppermute | solution.py:40
  135.6 2.8 %collective-permute-start.12 = (bf16[4,64,256]{2,1,0:T(8,128)(2,1)}, bf16[4,64,256]{2,1,0:T(8,128)(2,1)S(1)}, u32[]{:S(2)}, u32[]{:S(2)}) collective-permute-start(bf16[4,64,256]{2,1,0:T(8,128)(2,1)} %bitcast.28), channel_id=1, source_target_pairs={{6,0},{7,1},{0,2},{1,3},{2,4},{3,5},{4,6},{5,7},{14,8},{15,9},{8,1... | collective-permute-start | bytes 393224 | tf_op jit(solution)/shard_map/ppermute | solution.py:30
  138.4 4.2 %collective-permute-done.11 = bf16[4,64,256]{2,1,0:T(8,128)(2,1)S(1)} collective-permute-done((bf16[4,64,256]{2,1,0:T(8,128)(2,1)}, bf16[4,64,256]{2,1,0:T(8,128)(2,1)S(1)}, u32[]{:S(2)}, u32[]{:S(2)}) %collective-permute-start.11) | collective-permute-done | bytes 131104 | tf_op jit(solution)/shard_map/ppermute | solution.py:30
  145.3 7.5 %collective-permute-start.19 = (bf16[4,16,896]{2,1,0:T(8,128)(2,1)S(1)}, bf16[4,16,896]{2,1,0:T(8,128)(2,1)S(1)}, u32[]{:S(2)}, u32[]{:S(2)}) collective-permute-start(bf16[4,16,896]{2,1,0:T(8,128)(2,1)S(1)} %get-tuple-element.31), channel_id=1, source_target_pairs={{0,8},{1,9},{2,10},{3,11},{4,12},{5,13},{6,14},{7,15},{8,16},{9,17... | collective-permute-start | bytes 344072 | tf_op jit(solution)/shard_map/ppermute | solution.py:18
  152.8 6.6 %collective-permute-start.18 = (bf16[4,16,896]{2,1,0:T(8,128)(2,1)S(1)}, bf16[4,16,896]{2,1,0:T(8,128)(2,1)S(1)}, u32[]{:S(2)}, u32[]{:S(2)}) collective-permute-start(bf16[4,16,896]{2,1,0:T(8,128)(2,1)S(1)} %get-tuple-element.32), channel_id=1, source_target_pairs={{0,16},{1,17},{2,18},{3,19},{4,20},{5,21},{6,22},{7,23},{8,24},{9,... | collective-permute-start | bytes 344072 | tf_op jit(solution)/shard_map/ppermute | solution.py:18
  159.4 6.2 %collective-permute-start.17 = (bf16[4,16,896]{2,1,0:T(8,128)(2,1)S(1)}, bf16[4,16,896]{2,1,0:T(8,128)(2,1)S(1)}, u32[]{:S(2)}, u32[]{:S(2)}) collective-permute-start(bf16[4,16,896]{2,1,0:T(8,128)(2,1)S(1)} %get-tuple-element.30), channel_id=1, source_target_pairs={{0,24},{1,25},{2,26},{3,27},{4,28},{5,29},{6,30},{7,31},{8,0},{9,1... | collective-permute-start | bytes 344072 | tf_op jit(solution)/shard_map/ppermute | solution.py:18
  167.3 4.0 %collective-permute-done.18 = bf16[4,16,896]{2,1,0:T(8,128)(2,1)S(1)} collective-permute-done((bf16[4,16,896]{2,1,0:T(8,128)(2,1)S(1)}, bf16[4,16,896]{2,1,0:T(8,128)(2,1)S(1)}, u32[]{:S(2)}, u32[]{:S(2)}) %collective-permute-start.18) | collective-permute-done | bytes 114720 | tf_op jit(solution)/shard_map/ppermute | solution.py:18
  171.3 7.1 %collective-permute-done.17 = bf16[4,16,896]{2,1,0:T(8,128)(2,1)S(1)} collective-permute-done((bf16[4,16,896]{2,1,0:T(8,128)(2,1)S(1)}, bf16[4,16,896]{2,1,0:T(8,128)(2,1)S(1)}, u32[]{:S(2)}, u32[]{:S(2)}) %collective-permute-start.17) | collective-permute-done | bytes 114720 | tf_op jit(solution)/shard_map/ppermute | solution.py:18
  180.8 6.3 %collective-permute-start.25 = (bf16[4,16,896]{2,1,0:T(8,128)(2,1)S(1)}, bf16[4,16,896]{2,1,0:T(8,128)(2,1)S(1)}, u32[]{:S(2)}, u32[]{:S(2)}) collective-permute-start(bf16[4,16,896]{2,1,0:T(8,128)(2,1)S(1)} %get-tuple-element.28), channel_id=1, source_target_pairs={{0,24},{1,25},{2,26},{3,27},{4,28},{5,29},{6,30},{7,31},{8,0},{9,1... | collective-permute-start | bytes 344072 | tf_op jit(solution)/shard_map/ppermute | solution.py:18
  187.2 8.4 %collective-permute-start.24 = (bf16[4,16,896]{2,1,0:T(8,128)(2,1)S(1)}, bf16[4,16,896]{2,1,0:T(8,128)(2,1)S(1)}, u32[]{:S(2)}, u32[]{:S(2)}) collective-permute-start(bf16[4,16,896]{2,1,0:T(8,128)(2,1)S(1)} %get-tuple-element.26), channel_id=1, source_target_pairs={{0,16},{1,17},{2,18},{3,19},{4,20},{5,21},{6,22},{7,23},{8,24},{9,... | collective-permute-start | bytes 344072 | tf_op jit(solution)/shard_map/ppermute | solution.py:18
  195.6 6.0 %collective-permute-start.23 = (bf16[4,16,896]{2,1,0:T(8,128)(2,1)S(1)}, bf16[4,16,896]{2,1,0:T(8,128)(2,1)S(1)}, u32[]{:S(2)}, u32[]{:S(2)}) collective-permute-start(bf16[4,16,896]{2,1,0:T(8,128)(2,1)S(1)} %get-tuple-element.27), channel_id=1, source_target_pairs={{0,8},{1,9},{2,10},{3,11},{4,12},{5,13},{6,14},{7,15},{8,16},{9,17... | collective-permute-start | bytes 344072 | tf_op jit(solution)/shard_map/ppermute | solution.py:18
  207.1 3.2 %collective-permute-start.22 = (bf16[128,896]{1,0:T(8,128)(2,1)}, bf16[128,896]{1,0:T(8,128)(2,1)}, u32[]{:S(2)}, u32[]{:S(2)}) collective-permute-start(bf16[128,896]{1,0:T(8,128)(2,1)} %get-tuple-element.12), channel_id=1, source_target_pairs={{6,0},{7,1},{0,2},{1,3},{2,4},{3,5},{4,6},{5,7},{14,8},{15,9},{8,1... | collective-permute-start | bytes 688136 | tf_op jit(solution)/shard_map/ppermute | solution.py:30
  210.4 2.9 %collective-permute-done.24 = bf16[4,16,896]{2,1,0:T(8,128)(2,1)S(1)} collective-permute-done((bf16[4,16,896]{2,1,0:T(8,128)(2,1)S(1)}, bf16[4,16,896]{2,1,0:T(8,128)(2,1)S(1)}, u32[]{:S(2)}, u32[]{:S(2)}) %collective-permute-start.24) | collective-permute-done | bytes 114720 | tf_op jit(solution)/shard_map/ppermute | solution.py:18
  219.7 4.5 %collective-permute-start.27 = (bf16[448,4,128]{2,0,1:T(8,128)(2,1)S(1)}, bf16[448,4,128]{2,0,1:T(8,128)(2,1)}, u32[]{:S(2)}, u32[]{:S(2)}) collective-permute-start(bf16[448,4,128]{2,0,1:T(8,128)(2,1)S(1)} %get-tuple-element.10), channel_id=1, source_target_pairs={{0,256},{1,257},{2,258},{3,259},{4,260},{5,261},{6,262},{7,263},{8... | collective-permute-start | bytes 1376264 | tf_op jit(solution)/shard_map/ppermute | solution.py:40
  225.1 3.8 %collective-permute-start.26 = (bf16[448,4,128]{2,0,1:T(8,128)(2,1)}, bf16[448,4,128]{2,0,1:T(8,128)(2,1)}, u32[]{:S(2)}, u32[]{:S(2)}) collective-permute-start(bf16[448,4,128]{2,0,1:T(8,128)(2,1)} %fusion.13), channel_id=1, source_target_pairs={{0,1},{1,0},{2,3},{3,2},{4,5},{5,4},{6,7},{7,6},{8,9},{9,8},{10,11... | collective-permute-start | bytes 1376264 | tf_op jit(solution)/shard_map/ppermute | solution.py:40
  238.8 3.9 %collective-permute-done.27 = bf16[448,4,128]{2,0,1:T(8,128)(2,1)} collective-permute-done((bf16[448,4,128]{2,0,1:T(8,128)(2,1)S(1)}, bf16[448,4,128]{2,0,1:T(8,128)(2,1)}, u32[]{:S(2)}, u32[]{:S(2)}) %collective-permute-start.27) | collective-permute-done | bytes 458784 | tf_op jit(solution)/shard_map/ppermute | solution.py:40
  246.1 11.5 %collective-permute-start.30 = (bf16[448,128]{1,0:T(8,128)(2,1)S(1)}, bf16[448,128]{1,0:T(8,128)(2,1)S(1)}, u32[]{:S(2)}, u32[]{:S(2)}) collective-permute-start(bf16[448,128]{1,0:T(8,128)(2,1)S(1)} %get-tuple-element.23), channel_id=1, source_target_pairs={{4,0},{5,1},{6,2},{7,3},{0,4},{1,5},{2,6},{3,7},{12,8},{13,9},{14,... | collective-permute-start | bytes 344072 | tf_op jit(solution)/shard_map/ppermute | solution.py:30
  257.7 3.1 %collective-permute-start.31 = (bf16[448,128]{1,0:T(8,128)(2,1)S(1)}, bf16[448,128]{1,0:T(8,128)(2,1)S(1)}, u32[]{:S(2)}, u32[]{:S(2)}) collective-permute-start(bf16[448,128]{1,0:T(8,128)(2,1)S(1)} %get-tuple-element.22), channel_id=1, source_target_pairs={{6,0},{7,1},{0,2},{1,3},{2,4},{3,5},{4,6},{5,7},{14,8},{15,9},{8,1... | collective-permute-start | bytes 344072 | tf_op jit(solution)/shard_map/ppermute | solution.py:30
  260.8 3.8 %collective-permute-done.30 = bf16[448,128]{1,0:T(8,128)(2,1)S(1)} collective-permute-done((bf16[448,128]{1,0:T(8,128)(2,1)S(1)}, bf16[448,128]{1,0:T(8,128)(2,1)S(1)}, u32[]{:S(2)}, u32[]{:S(2)}) %collective-permute-start.30) | collective-permute-done | bytes 114720 | tf_op jit(solution)/shard_map/ppermute | solution.py:30
  (156 shorter events, 67.0 us)
Async XLA Ops:
  3.0 35.5 %collective-permute-start.5 = (bf16[16,3584]{1,0:T(8,128)(2,1)S(1)}, bf16[16,3584]{1,0:T(8,128)(2,1)S(1)}, u32[]{:S(2)}, u32[]{:S(2)}) collective-permute-start(bf16[16,3584]{1,0:T(8,128)(2,1)S(1)} %get-tuple-element.36), channel_id=1, source_target_pairs={{0,24},{1,25},{2,26},{3,27},{4,28},{5,29},{6,30},{7,31},{8,0},{9,1... | collective-permute-start | bytes 344072 | tf_op jit(solution)/shard_map/ppermute | solution.py:18
  15.7 26.2 %collective-permute-start.4 = (bf16[16,3584]{1,0:T(8,128)(2,1)S(1)}, bf16[16,3584]{1,0:T(8,128)(2,1)S(1)}, u32[]{:S(2)}, u32[]{:S(2)}) collective-permute-start(bf16[16,3584]{1,0:T(8,128)(2,1)S(1)} %get-tuple-element.37), channel_id=1, source_target_pairs={{0,16},{1,17},{2,18},{3,19},{4,20},{5,21},{6,22},{7,23},{8,24},{9,... | collective-permute-start | bytes 344072 | tf_op jit(solution)/shard_map/ppermute | solution.py:18
  20.6 25.1 %collective-permute-start.3 = (bf16[16,3584]{1,0:T(8,128)(2,1)S(1)}, bf16[16,3584]{1,0:T(8,128)(2,1)S(1)}, u32[]{:S(2)}, u32[]{:S(2)}) collective-permute-start(bf16[16,3584]{1,0:T(8,128)(2,1)S(1)} %get-tuple-element.38), channel_id=1, source_target_pairs={{0,8},{1,9},{2,10},{3,11},{4,12},{5,13},{6,14},{7,15},{8,16},{9,17... | collective-permute-start | bytes 344072 | tf_op jit(solution)/shard_map/ppermute | solution.py:18
  29.9 82.4 %collective-permute-start.9 = (bf16[3584,256]{1,0:T(8,128)(2,1)}, bf16[3584,256]{1,0:T(8,128)(2,1)}, u32[]{:S(2)}, u32[]{:S(2)}) collective-permute-start(bf16[3584,256]{1,0:T(8,128)(2,1)} %pad_maximum_fusion.1), channel_id=1, source_target_pairs={{0,1},{1,0},{2,3},{3,2},{4,5},{5,4},{6,7},{7,6},{8,9},{9,8},{10,11... | collective-permute-start | bytes 5505032 | tf_op jit(solution)/shard_map/ppermute | solution.py:40
  35.6 13.9 %collective-permute-start.15 = (bf16[896,128]{1,0:T(8,128)(2,1)S(1)}, bf16[896,128]{1,0:T(8,128)(2,1)}, u32[]{:S(2)}, u32[]{:S(2)}) collective-permute-start(bf16[896,128]{1,0:T(8,128)(2,1)S(1)} %get-tuple-element.19), channel_id=1, source_target_pairs={{6,0},{7,1},{0,2},{1,3},{2,4},{3,5},{4,6},{5,7},{14,8},{15,9},{8,1... | collective-permute-start | bytes 688136 | tf_op jit(solution)/shard_map/ppermute | solution.py:30
  38.5 34.5 %collective-permute-start.14 = (bf16[896,128]{1,0:T(8,128)(2,1)S(1)}, bf16[896,128]{1,0:T(8,128)(2,1)}, u32[]{:S(2)}, u32[]{:S(2)}) collective-permute-start(bf16[896,128]{1,0:T(8,128)(2,1)S(1)} %get-tuple-element.20), channel_id=1, source_target_pairs={{4,0},{5,1},{6,2},{7,3},{0,4},{1,5},{2,6},{3,7},{12,8},{13,9},{14,... | collective-permute-start | bytes 688136 | tf_op jit(solution)/shard_map/ppermute | solution.py:30
  41.9 35.2 %collective-permute-start.13 = (bf16[896,128]{1,0:T(8,128)(2,1)}, bf16[896,128]{1,0:T(8,128)(2,1)}, u32[]{:S(2)}, u32[]{:S(2)}) collective-permute-start(bf16[896,128]{1,0:T(8,128)(2,1)} %get-tuple-element.21), channel_id=1, source_target_pairs={{2,0},{3,1},{4,2},{5,3},{6,4},{7,5},{0,6},{1,7},{10,8},{11,9},{12,... | collective-permute-start | bytes 688136 | tf_op jit(solution)/shard_map/ppermute | solution.py:30
  47.4 37.7 %collective-permute-start.8 = (bf16[4,16,3584]{2,1,0:T(8,128)(2,1)S(1)}, bf16[4,16,3584]{2,1,0:T(8,128)(2,1)S(1)}, u32[]{:S(2)}, u32[]{:S(2)}) collective-permute-start(bf16[4,16,3584]{2,1,0:T(8,128)(2,1)S(1)} %get-tuple-element.34), channel_id=1, source_target_pairs={{6,0},{7,1},{0,2},{1,3},{2,4},{3,5},{4,6},{5,7},{14,8},{15,9},{8,1... | collective-permute-start | bytes 1376264 | tf_op jit(solution)/shard_map/ppermute | solution.py:30
  49.5 46.5 %collective-permute-start.7 = (bf16[4,16,3584]{2,1,0:T(8,128)(2,1)S(1)}, bf16[4,16,3584]{2,1,0:T(8,128)(2,1)S(1)}, u32[]{:S(2)}, u32[]{:S(2)}) collective-permute-start(bf16[4,16,3584]{2,1,0:T(8,128)(2,1)S(1)} %get-tuple-element.34), channel_id=1, source_target_pairs={{4,0},{5,1},{6,2},{7,3},{0,4},{1,5},{2,6},{3,7},{12,8},{13,9},{14,... | collective-permute-start | bytes 1376264 | tf_op jit(solution)/shard_map/ppermute | solution.py:30
  73.0 33.0 %collective-permute-start.6 = (bf16[4,16,3584]{2,1,0:T(8,128)(2,1)S(1)}, bf16[4,16,3584]{2,1,0:T(8,128)(2,1)S(1)}, u32[]{:S(2)}, u32[]{:S(2)}) collective-permute-start(bf16[4,16,3584]{2,1,0:T(8,128)(2,1)S(1)} %get-tuple-element.34), channel_id=1, source_target_pairs={{2,0},{3,1},{4,2},{5,3},{6,4},{7,5},{0,6},{1,7},{10,8},{11,9},{12,... | collective-permute-start | bytes 1376264 | tf_op jit(solution)/shard_map/ppermute | solution.py:30
  77.1 82.3 %collective-permute-start.2 = (f32[16,128]{1,0:T(8,128)S(1)}, f32[16,128]{1,0:T(8,128)S(1)}, u32[]{:S(2)}, u32[]{:S(2)}) collective-permute-start(f32[16,128]{1,0:T(8,128)S(1)} %maximum_maximum_fusion), channel_id=1, source_target_pairs={{6,0},{7,1},{0,2},{1,3},{2,4},{3,5},{4,6},{5,7},{14,8},{15,9},{8,1... | collective-permute-start | bytes 24584 | tf_op jit(solution)/shard_map/ppermute | solution.py:30
  85.1 80.4 %collective-permute-start.1 = (f32[16,128]{1,0:T(8,128)S(1)}, f32[16,128]{1,0:T(8,128)}, u32[]{:S(2)}, u32[]{:S(2)}) collective-permute-start(f32[16,128]{1,0:T(8,128)S(1)} %maximum_maximum_fusion), channel_id=1, source_target_pairs={{4,0},{5,1},{6,2},{7,3},{0,4},{1,5},{2,6},{3,7},{12,8},{13,9},{14,... | collective-permute-start | bytes 24584 | tf_op jit(solution)/shard_map/ppermute | solution.py:30
  96.0 69.6 %collective-permute-start = (f32[16,128]{1,0:T(8,128)S(1)}, f32[16,128]{1,0:T(8,128)}, u32[]{:S(2)}, u32[]{:S(2)}) collective-permute-start(f32[16,128]{1,0:T(8,128)S(1)} %maximum_maximum_fusion), channel_id=1, source_target_pairs={{2,0},{3,1},{4,2},{5,3},{6,4},{7,5},{0,6},{1,7},{10,8},{11,9},{12,... | collective-permute-start | bytes 24584 | tf_op jit(solution)/shard_map/ppermute | solution.py:30
  106.0 23.1 %collective-permute-start.16 = (bf16[4,896,128]{2,1,0:T(8,128)(2,1)}, bf16[4,896,128]{2,1,0:T(8,128)(2,1)}, u32[]{:S(2)}, u32[]{:S(2)}) collective-permute-start(bf16[4,896,128]{2,1,0:T(8,128)(2,1)} %get-tuple-element.17), channel_id=1, source_target_pairs={{0,1},{1,0},{2,3},{3,2},{4,5},{5,4},{6,7},{7,6},{8,9},{9,8},{10,11... | collective-permute-start | bytes 2752520 | tf_op jit(solution)/shard_map/ppermute | solution.py:40
  115.5 20.1 %collective-permute-start.10 = (bf16[4,64,256]{2,1,0:T(8,128)(2,1)}, bf16[4,64,256]{2,1,0:T(8,128)(2,1)S(1)}, u32[]{:S(2)}, u32[]{:S(2)}) collective-permute-start(bf16[4,64,256]{2,1,0:T(8,128)(2,1)} %bitcast.28), channel_id=1, source_target_pairs={{2,0},{3,1},{4,2},{5,3},{6,4},{7,5},{0,6},{1,7},{10,8},{11,9},{12,... | collective-permute-start | bytes 393224 | tf_op jit(solution)/shard_map/ppermute | solution.py:30
  133.5 9.1 %collective-permute-start.11 = (bf16[4,64,256]{2,1,0:T(8,128)(2,1)}, bf16[4,64,256]{2,1,0:T(8,128)(2,1)S(1)}, u32[]{:S(2)}, u32[]{:S(2)}) collective-permute-start(bf16[4,64,256]{2,1,0:T(8,128)(2,1)} %bitcast.28), channel_id=1, source_target_pairs={{4,0},{5,1},{6,2},{7,3},{0,4},{1,5},{2,6},{3,7},{12,8},{13,9},{14,... | collective-permute-start | bytes 393224 | tf_op jit(solution)/shard_map/ppermute | solution.py:30
  135.6 8.9 %collective-permute-start.12 = (bf16[4,64,256]{2,1,0:T(8,128)(2,1)}, bf16[4,64,256]{2,1,0:T(8,128)(2,1)S(1)}, u32[]{:S(2)}, u32[]{:S(2)}) collective-permute-start(bf16[4,64,256]{2,1,0:T(8,128)(2,1)} %bitcast.28), channel_id=1, source_target_pairs={{6,0},{7,1},{0,2},{1,3},{2,4},{3,5},{4,6},{5,7},{14,8},{15,9},{8,1... | collective-permute-start | bytes 393224 | tf_op jit(solution)/shard_map/ppermute | solution.py:30
  145.3 22.0 %collective-permute-start.19 = (bf16[4,16,896]{2,1,0:T(8,128)(2,1)S(1)}, bf16[4,16,896]{2,1,0:T(8,128)(2,1)S(1)}, u32[]{:S(2)}, u32[]{:S(2)}) collective-permute-start(bf16[4,16,896]{2,1,0:T(8,128)(2,1)S(1)} %get-tuple-element.31), channel_id=1, source_target_pairs={{0,8},{1,9},{2,10},{3,11},{4,12},{5,13},{6,14},{7,15},{8,16},{9,17... | collective-permute-start | bytes 344072 | tf_op jit(solution)/shard_map/ppermute | solution.py:18
  152.8 18.5 %collective-permute-start.18 = (bf16[4,16,896]{2,1,0:T(8,128)(2,1)S(1)}, bf16[4,16,896]{2,1,0:T(8,128)(2,1)S(1)}, u32[]{:S(2)}, u32[]{:S(2)}) collective-permute-start(bf16[4,16,896]{2,1,0:T(8,128)(2,1)S(1)} %get-tuple-element.32), channel_id=1, source_target_pairs={{0,16},{1,17},{2,18},{3,19},{4,20},{5,21},{6,22},{7,23},{8,24},{9,... | collective-permute-start | bytes 344072 | tf_op jit(solution)/shard_map/ppermute | solution.py:18
  159.4 19.0 %collective-permute-start.17 = (bf16[4,16,896]{2,1,0:T(8,128)(2,1)S(1)}, bf16[4,16,896]{2,1,0:T(8,128)(2,1)S(1)}, u32[]{:S(2)}, u32[]{:S(2)}) collective-permute-start(bf16[4,16,896]{2,1,0:T(8,128)(2,1)S(1)} %get-tuple-element.30), channel_id=1, source_target_pairs={{0,24},{1,25},{2,26},{3,27},{4,28},{5,29},{6,30},{7,31},{8,0},{9,1... | collective-permute-start | bytes 344072 | tf_op jit(solution)/shard_map/ppermute | solution.py:18
  180.8 26.3 %collective-permute-start.25 = (bf16[4,16,896]{2,1,0:T(8,128)(2,1)S(1)}, bf16[4,16,896]{2,1,0:T(8,128)(2,1)S(1)}, u32[]{:S(2)}, u32[]{:S(2)}) collective-permute-start(bf16[4,16,896]{2,1,0:T(8,128)(2,1)S(1)} %get-tuple-element.28), channel_id=1, source_target_pairs={{0,24},{1,25},{2,26},{3,27},{4,28},{5,29},{6,30},{7,31},{8,0},{9,1... | collective-permute-start | bytes 344072 | tf_op jit(solution)/shard_map/ppermute | solution.py:18
  187.2 26.1 %collective-permute-start.24 = (bf16[4,16,896]{2,1,0:T(8,128)(2,1)S(1)}, bf16[4,16,896]{2,1,0:T(8,128)(2,1)S(1)}, u32[]{:S(2)}, u32[]{:S(2)}) collective-permute-start(bf16[4,16,896]{2,1,0:T(8,128)(2,1)S(1)} %get-tuple-element.26), channel_id=1, source_target_pairs={{0,16},{1,17},{2,18},{3,19},{4,20},{5,21},{6,22},{7,23},{8,24},{9,... | collective-permute-start | bytes 344072 | tf_op jit(solution)/shard_map/ppermute | solution.py:18
  195.6 19.4 %collective-permute-start.23 = (bf16[4,16,896]{2,1,0:T(8,128)(2,1)S(1)}, bf16[4,16,896]{2,1,0:T(8,128)(2,1)S(1)}, u32[]{:S(2)}, u32[]{:S(2)}) collective-permute-start(bf16[4,16,896]{2,1,0:T(8,128)(2,1)S(1)} %get-tuple-element.27), channel_id=1, source_target_pairs={{0,8},{1,9},{2,10},{3,11},{4,12},{5,13},{6,14},{7,15},{8,16},{9,17... | collective-permute-start | bytes 344072 | tf_op jit(solution)/shard_map/ppermute | solution.py:18
  202.6 22.5 %collective-permute-start.20 = (bf16[128,896]{1,0:T(8,128)(2,1)}, bf16[128,896]{1,0:T(8,128)(2,1)S(1)}, u32[]{:S(2)}, u32[]{:S(2)}) collective-permute-start(bf16[128,896]{1,0:T(8,128)(2,1)} %get-tuple-element.15), channel_id=1, source_target_pairs={{2,0},{3,1},{4,2},{5,3},{6,4},{7,5},{0,6},{1,7},{10,8},{11,9},{12,... | collective-permute-start | bytes 688136 | tf_op jit(solution)/shard_map/ppermute | solution.py:30
  205.2 23.7 %collective-permute-start.21 = (bf16[128,896]{1,0:T(8,128)(2,1)}, bf16[128,896]{1,0:T(8,128)(2,1)}, u32[]{:S(2)}, u32[]{:S(2)}) collective-permute-start(bf16[128,896]{1,0:T(8,128)(2,1)} %get-tuple-element.14), channel_id=1, source_target_pairs={{4,0},{5,1},{6,2},{7,3},{0,4},{1,5},{2,6},{3,7},{12,8},{13,9},{14,... | collective-permute-start | bytes 688136 | tf_op jit(solution)/shard_map/ppermute | solution.py:30
  207.1 22.7 %collective-permute-start.22 = (bf16[128,896]{1,0:T(8,128)(2,1)}, bf16[128,896]{1,0:T(8,128)(2,1)}, u32[]{:S(2)}, u32[]{:S(2)}) collective-permute-start(bf16[128,896]{1,0:T(8,128)(2,1)} %get-tuple-element.12), channel_id=1, source_target_pairs={{6,0},{7,1},{0,2},{1,3},{2,4},{3,5},{4,6},{5,7},{14,8},{15,9},{8,1... | collective-permute-start | bytes 688136 | tf_op jit(solution)/shard_map/ppermute | solution.py:30
  217.2 21.6 %collective-permute-start.28 = (bf16[448,4,128]{2,0,1:T(8,128)(2,1)}, bf16[448,4,128]{2,0,1:T(8,128)(2,1)}, u32[]{:S(2)}, u32[]{:S(2)}) collective-permute-start(bf16[448,4,128]{2,0,1:T(8,128)(2,1)} %get-tuple-element.11), channel_id=1, source_target_pairs={{0,257},{1,256},{2,259},{3,258},{4,261},{5,260},{6,263},{7,262},{8... | collective-permute-start | bytes 1376264 | tf_op jit(solution)/shard_map/ppermute | solution.py:40
  219.7 22.9 %collective-permute-start.27 = (bf16[448,4,128]{2,0,1:T(8,128)(2,1)S(1)}, bf16[448,4,128]{2,0,1:T(8,128)(2,1)}, u32[]{:S(2)}, u32[]{:S(2)}) collective-permute-start(bf16[448,4,128]{2,0,1:T(8,128)(2,1)S(1)} %get-tuple-element.10), channel_id=1, source_target_pairs={{0,256},{1,257},{2,258},{3,259},{4,260},{5,261},{6,262},{7,263},{8... | collective-permute-start | bytes 1376264 | tf_op jit(solution)/shard_map/ppermute | solution.py:40
  225.1 17.6 %collective-permute-start.26 = (bf16[448,4,128]{2,0,1:T(8,128)(2,1)}, bf16[448,4,128]{2,0,1:T(8,128)(2,1)}, u32[]{:S(2)}, u32[]{:S(2)}) collective-permute-start(bf16[448,4,128]{2,0,1:T(8,128)(2,1)} %fusion.13), channel_id=1, source_target_pairs={{0,1},{1,0},{2,3},{3,2},{4,5},{5,4},{6,7},{7,6},{8,9},{9,8},{10,11... | collective-permute-start | bytes 1376264 | tf_op jit(solution)/shard_map/ppermute | solution.py:40
  244.2 16.6 %collective-permute-start.29 = (bf16[448,128]{1,0:T(8,128)(2,1)S(1)}, bf16[448,128]{1,0:T(8,128)(2,1)S(1)}, u32[]{:S(2)}, u32[]{:S(2)}) collective-permute-start(bf16[448,128]{1,0:T(8,128)(2,1)S(1)} %get-tuple-element.24), channel_id=1, source_target_pairs={{2,0},{3,1},{4,2},{5,3},{6,4},{7,5},{0,6},{1,7},{10,8},{11,9},{12,... | collective-permute-start | bytes 344072 | tf_op jit(solution)/shard_map/ppermute | solution.py:30
  246.1 18.5 %collective-permute-start.30 = (bf16[448,128]{1,0:T(8,128)(2,1)S(1)}, bf16[448,128]{1,0:T(8,128)(2,1)S(1)}, u32[]{:S(2)}, u32[]{:S(2)}) collective-permute-start(bf16[448,128]{1,0:T(8,128)(2,1)S(1)} %get-tuple-element.23), channel_id=1, source_target_pairs={{4,0},{5,1},{6,2},{7,3},{0,4},{1,5},{2,6},{3,7},{12,8},{13,9},{14,... | collective-permute-start | bytes 344072 | tf_op jit(solution)/shard_map/ppermute | solution.py:30
  257.7 8.5 %collective-permute-start.31 = (bf16[448,128]{1,0:T(8,128)(2,1)S(1)}, bf16[448,128]{1,0:T(8,128)(2,1)S(1)}, u32[]{:S(2)}, u32[]{:S(2)}) collective-permute-start(bf16[448,128]{1,0:T(8,128)(2,1)S(1)} %get-tuple-element.22), channel_id=1, source_target_pairs={{6,0},{7,1},{0,2},{1,3},{2,4},{3,5},{4,6},{5,7},{14,8},{15,9},{8,1... | collective-permute-start | bytes 344072 | tf_op jit(solution)/shard_map/ppermute | solution.py:30
  (17 other events, 172.6 us)

commit v2 on v0

v2 whole, which is shorter than its diff:
```python
import functools

import jax
import jax.numpy as jnp
from jax import lax
from jax.experimental import pallas as pl
from jax.experimental.pallas import tpu as pltpu
from jax.sharding import PartitionSpec as P

SPLIT = 8
CAP = 16
QUADS = 4
BF16 = jnp.bfloat16
F32 = jnp.float32
VMEM_LIMIT = 48 * 1024 * 1024


def columns(count):
    return [[i for i in range(count) if i % 2 == side] for side in range(2)]


def quads(count):
    return [
        [base + 2 * place + side for place in range(QUADS)]
        for base in range(0, count, SPLIT)
        for side in range(2)
    ]


def exchange(blocks, axis, groups):
    return lax.all_to_all(blocks, axis, 0, 0, axis_index_groups=groups, tiled=True)


def pass_on(block, step, turn):
    count = lax.axis_size("expert")
    route = []
    for i in range(count):
        place = i % SPLIT // 2
        came = place - step * (turn - 1)
        if 0 <= came < QUADS and 0 <= place + step < QUADS:
            route.append((i, i + 2 * step))
    return lax.ppermute(block, "expert", route)


def neighbour(block):
    count = lax.axis_size("expert")
    return lax.ppermute(block, "expert", [(i, i ^ 1) for i in range(count)])


def swap(block, distance):
    count = lax.axis_size("expert")
    return lax.ppermute(block, "expert", [(i, i ^ 2 * distance) for i in range(count)])


def reduce_groups(pipes, count):
    half = pipes // 2
    return [
        [(p + half * h) * count + i + side for h in range(2) for side in range(2)]
        for p in range(half)
        for i in range(0, count, 2)
    ]


def dot(a, b, dims=((1,), (0,))):
    return lax.dot_general(a, b, (dims, ((), ())), preferred_element_type=F32)


def kernel_call(body, out_shape, flops, moved, scalars=0, **kwargs):
    def call(*operands):
        specs = [pl.BlockSpec(memory_space=pltpu.SMEM)] * scalars
        specs += [pl.BlockSpec(memory_space=pltpu.VMEM)] * (len(operands) - scalars)
        return pl.pallas_call(
            body,
            out_shape=out_shape,
            in_specs=specs,
            out_specs=jax.tree.map(lambda _: pl.BlockSpec(memory_space=pltpu.VMEM), out_shape),
            compiler_params=pltpu.CompilerParams(vmem_limit_bytes=VMEM_LIMIT),
            cost_estimate=pl.CostEstimate(flops=flops, bytes_accessed=moved, transcendentals=0),
            **kwargs,
        )(*operands)

    return call


def relay_kernel(quad_ref, w_ref, *rest):
    outs, turned = rest[:-1], rest[-1]
    quad = quad_ref[0]
    turned[...] = w_ref[...].T
    eighth = outs[0].shape[0] // 2
    for d, out in enumerate(outs):
        for h in range(2):
            start = pl.multiple_of((h * QUADS + (quad ^ d)) * eighth, 16)
            out[h * eighth : (h + 1) * eighth, :] = turned[pl.ds(start, eighth), :]


def gather_kernel(window, ids_ref, gates_ref, tok_ref, picked_ref, spread_ref):
    slots, toks = window * CAP, tok_ref.shape[0]
    slot = lax.broadcasted_iota(jnp.int32, (slots, toks), 0)
    expert, nth = slot // CAP, slot % CAP
    weight = jnp.zeros((slots, toks), F32)
    member = jnp.zeros((slots, toks), F32)
    for j in range(ids_ref.shape[0]):
        hit = ids_ref[j : j + 1, :] == expert
        weight = weight + jnp.where(hit, gates_ref[j : j + 1, :], 0.0)
        member = jnp.where(hit, 1.0, member)
    before = lax.broadcasted_iota(jnp.int32, (toks, toks), 0)
    after = lax.broadcasted_iota(jnp.int32, (toks, toks), 1)
    upto = jnp.where(before <= after, 1.0, 0.0).astype(BF16)
    ranking = dot(member.astype(BF16), upto)
    matched = (member > 0.5) & (ranking == (nth + 1).astype(F32))
    spread_ref[...] = jnp.where(matched, weight, 0.0)
    selector = jnp.where(matched, 1.0, 0.0).astype(BF16)
    quarter = picked_ref.shape[2]
    for q in range(QUADS):
        rows = dot(selector, tok_ref[:, q * quarter : (q + 1) * quarter]).astype(BF16)
        for k in range(window):
            picked_ref[k * QUADS + q] = rows[k * CAP : (k + 1) * CAP]


def acts_kernel(quad_ref, here, up1, up2, down1, down2, wg, wu, wg2, wu2, acts_ref):
    quad = quad_ref[0]
    quarter, units = here.shape[1], wg.shape[1]
    parts = ((here, None, 0), (up1, None, 1), (down1, None, 3), (up2, down2, 2))
    totals = [None] * 4
    for first, second, distance in parts:
        start = pl.multiple_of((quad + distance) % QUADS * quarter, quarter)
        rows = first[...] if second is None else first[...] + second[...]
        for n, weight in enumerate((wg, wu, wg2, wu2)):
            part = dot(rows, weight[pl.ds(start, quarter), :])
            totals[n] = part if totals[n] is None else totals[n] + part
    for n in range(4):
        acts_ref[:, n * units : (n + 1) * units] = totals[n]


def hidden_kernel(quad_ref, acts, up3, down3, wg, wu, wg2, wu2, hidden_ref):
    quad = quad_ref[0]
    quarter, units = up3.shape[1], wg.shape[1]
    last = jnp.where(quad * 2 < QUADS, QUADS - 1, 0)
    start = pl.multiple_of(last * quarter, quarter)
    rows = up3[...] + down3[...]
    both = []
    for n, weight in enumerate((wg, wu, wg2, wu2)):
        both.append(acts[:, n * units : (n + 1) * units] + dot(rows, weight[pl.ds(start, quarter), :]))
    for side in range(2):
        gate, up = both[2 * side], both[2 * side + 1]
        value = (gate / (1.0 + jnp.exp(-gate)) * up).astype(BF16)
        for s in range(QUADS):
            hidden_ref[s, :, side * units : (side + 1) * units] = value


def down_kernel(quad_ref, hidden, down, down_other, out_ref):
    quad = quad_ref[0]
    total = None
    for d in range(QUADS):
        slab = jnp.concatenate([down[d], down_other[d]], axis=1)
        part = dot(hidden[quad ^ d], slab, ((1,), (1,)))
        total = part if total is None else total + part
    blocks, cap, quarter = out_ref.shape
    out_ref[...] = total.astype(BF16).reshape(blocks, cap, quarter)


def mix_kernel(window, spread_ref, loss_ref, back, mixed_ref, cotan_ref):
    spread = spread_ref[...]
    high = spread.astype(BF16)
    rest = spread - high.astype(F32)
    middle = rest.astype(BF16)
    low = (rest - middle.astype(F32)).astype(BF16)
    weights = jnp.concatenate([high, middle, low], axis=0)
    chosen = jnp.where(spread > 0.0, 1.0, 0.0).astype(BF16)
    scale = jnp.sum(spread * loss_ref[...], axis=1, keepdims=True)
    eighth = back.shape[2] // 2
    halves = [[], []]
    for q in range(QUADS):
        rows = jnp.concatenate([back[k * QUADS + q] for k in range(window)], axis=0)
        rows = jnp.concatenate([rows, rows, rows], axis=0)
        mixed = dot(weights, rows, ((0,), (0,))).astype(BF16)
        cotan = (scale * dot(chosen, mixed)).astype(BF16)
        for k in range(window):
            cotan_ref[k * QUADS + q] = cotan[k * CAP : (k + 1) * CAP]
        for h in range(2):
            halves[h].append(mixed[:, h * eighth : (h + 1) * eighth])
    mixed_ref[...] = jnp.concatenate(halves[0] + halves[1], axis=1)


def grads_kernel(side_ref, cotan, hidden, grads_ref):
    side = side_ref[0]
    eighth, units = grads_ref.shape[2:]
    for s in range(QUADS):
        part = dot(cotan[...], hidden[s], ((0,), (0,))).astype(BF16)
        for h in range(2):
            for other in range(2):
                grads_ref[2 * h + (side + other) % 2, s] = part[
                    h * eighth : (h + 1) * eighth, other * units : (other + 1) * units
                ]


def per_device(tokens, expert_ids, gates, loss_weight, w_gate, w_up, w_down):
    tok_count, width = tokens.shape[1:]
    units = w_down.shape[1]
    count = lax.axis_size("expert")
    window = count // SPLIT
    quarter, eighth = width // QUADS, width // (2 * QUADS)
    place = lax.axis_index("expert")
    quad = (place % SPLIT // 2).reshape(1)
    side = (place % 2).reshape(1)
    by_column, by_quad = columns(count), quads(count)
    blocks = count // 2
    held = blocks * CAP

    gate_other = neighbour(w_gate[0])
    up_other = neighbour(w_up[0])

    down = kernel_call(
        relay_kernel, (jax.ShapeDtypeStruct((quarter, units), BF16),) * QUADS,
        0, 4 * width * units, 1, scratch_shapes=[pltpu.VMEM((width, units), BF16)],
    )(quad, w_down[0])
    down = jnp.stack([down[0]] + [swap(down[d], d) for d in range(1, QUADS)])

    picked, spread = kernel_call(
        functools.partial(gather_kernel, window),
        (
            jax.ShapeDtypeStruct((window * QUADS, CAP, quarter), BF16),
            jax.ShapeDtypeStruct((window * CAP, tok_count), F32),
        ),
        2 * window * CAP * tok_count * width, 3 * tok_count * width,
    )(expert_ids[0].T, gates[0].T, tokens[0])
    rows = exchange(picked, "expert", by_column).reshape(held, quarter)
    rows, gate_other, up_other, down = lax.optimization_barrier((rows, gate_other, up_other, down))
    down_other = neighbour(down)
    ups, downs = [rows], [rows]
    for turn in range(1, QUADS):
        ups.append(pass_on(ups[-1], 1, turn))
        downs.append(pass_on(downs[-1], -1, turn))
    weights = (w_gate[0], w_up[0], gate_other, up_other)
    acts = kernel_call(
        acts_kernel, jax.ShapeDtypeStruct((held, 4 * units), F32),
        8 * held * width * units, 8 * width * units, 1,
    )(quad, rows, downs[1], downs[2], ups[1], ups[2], *weights)
    hidden = kernel_call(
        hidden_kernel, jax.ShapeDtypeStruct((QUADS, held, 2 * units), BF16),
        2 * held * width * units, 2 * width * units, 1,
    )(quad, acts, downs[3], ups[3], *weights)
    hidden, down_other = lax.optimization_barrier((hidden, down_other))
    hidden = exchange(hidden, "expert", by_quad)
    out = kernel_call(
        down_kernel, jax.ShapeDtypeStruct((blocks, CAP, quarter), BF16),
        4 * held * width * units, 4 * width * units, 1,
    )(quad, hidden, down, down_other)
    back = exchange(out, "expert", by_column)

    output, cotan = kernel_call(
        functools.partial(mix_kernel, window),
        (
            jax.ShapeDtypeStruct((tok_count, width), BF16),
            jax.ShapeDtypeStruct((window * QUADS, CAP, quarter), BF16),
        ),
        8 * window * CAP * tok_count * width, 4 * tok_count * width,
    )(spread, loss_weight, back)
    cotan = exchange(cotan, "expert", by_column).reshape(held, quarter)

    grads = kernel_call(
        grads_kernel, jax.ShapeDtypeStruct((2 * 2, QUADS, eighth, units), BF16),
        4 * held * width * units, 4 * width * units, 1,
    )(side, cotan, hidden)
    groups = reduce_groups(lax.axis_size("pipe"), count)
    parts = exchange(grads, ("pipe", "expert"), groups)
    share = jnp.sum(parts.astype(F32), axis=0).astype(BF16)
    share = exchange(share, "expert", by_quad).reshape(QUADS * eighth, units).T
    return output[None], share[None]


def solution(mesh):
    in_specs = (
        P("pipe", "expert", None),
        P("pipe", "expert", None),
        P("pipe", "expert", None),
        P("pipe", "expert"),
        P("pipe", None, "expert"),
        P("pipe", None, "expert"),
        P("pipe", "expert", None),
    )
    out_specs = (P("pipe", "expert", None), P("pipe", "expert", None))
    return jax.shard_map(
        per_device, mesh=mesh, in_specs=in_specs, out_specs=out_specs, check_vma=False
    )
```

time: 589 us -> 220 us (0.37)
  blocking collectives: 355 us -> 82.3 us
  waiting for transfers between devices: 206 us -> 68.8 us
  starting transfers between devices: 10.2 us -> 50.9 us
  Pallas kernels: 0 us -> 10.8 us
  matrix products: 10.2 us -> 0 us
    all_to_all x2 -> x4, blocking collectives: 355 us -> 82.3 us  [exchange(): lax.all_to_all(blocks, axis, 0, 0, axis_index_groups=groups, tiled=True)]
    all_to_all x1 -> x2, waiting for transfers between devices: 166 us -> 22.8 us  [exchange(): lax.all_to_all(blocks, axis, 0, 0, axis_index_groups=groups, tiled=True)]
    ppermute x1 -> x12, starting transfers between devices: 5.1 us -> 28.2 us  [the longest x3 10.1 us: swap(): lax.ppermute(block, 'expert', [(i, i ^ 2 * distance) for i in range(count)])]
    all_to_all x1 -> x2, starting transfers between devices: 5.06 us -> 22.7 us  [exchange(): lax.all_to_all(blocks, axis, 0, 0, axis_index_groups=groups, tiled=True)]
    pallas_call x0 -> x7, Pallas kernels: none -> 10.8 us  [call(): pl.pallas_call(body, out_shape=out_shape, in_specs=specs, out_specs=jax.t...]
    dot_general x7 -> x0, matrix products: 10.2 us -> none  [the longest x1 2.94 us: per_device(): jnp.einsum('rch,hd->rcd', hidden, down_rows, preferred_element_type=jnp.f...]
    ppermute x1 -> x12, waiting for transfers between devices: 39.3 us -> 46 us  [the longest x3 25 us: swap(): lax.ppermute(block, 'expert', [(i, i ^ 2 * distance) for i in range(count)])]
  transfers between devices with their start and end apart: 2 -> 14, of which waited for: 2 -> 7; matrix products, arithmetic and copies ran while one was open for 0% -> 0% of each run, Pallas kernels for 0% -> 3%
where the time goes in v2:
time: 220 us; the launch traced here: 219 us
  blocking collectives  82.3 us (37%)
  waiting for transfers between devices  68.8 us (31%)
  starting transfers between devices  50.9 us (23%)
  Pallas kernels  10.8 us (5%)
  local copies, waits for them, and re-layouts  4.85 us (2%)
    all_to_all x4, blocking collectives, exchange(): lax.all_to_all(blocks, axis, 0, 0, axis_index_groups=groups, tiled=True)  82.3 us
    ppermute x3, waiting for transfers between devices, swap(): lax.ppermute(block, 'expert', [(i, i ^ 2 * distance) for i in range(count)])  25 us
    all_to_all x2, waiting for transfers between devices, exchange(): lax.all_to_all(blocks, axis, 0, 0, axis_index_groups=groups, tiled=True)  22.8 us
    all_to_all x2, starting transfers between devices, exchange(): lax.all_to_all(blocks, axis, 0, 0, axis_index_groups=groups, tiled=True)  22.7 us
    ppermute x6, waiting for transfers between devices, pass_on(): return lax.ppermute(block, 'expert', route)  20.2 us
    pallas_call x7, Pallas kernels, call(): pl.pallas_call(body, out_shape=out_shape, in_specs=specs, out_specs=jax.t...  10.8 us
    ppermute x3, starting transfers between devices, swap(): lax.ppermute(block, 'expert', [(i, i ^ 2 * distance) for i in range(count)])  10.1 us
    ppermute x6, starting transfers between devices, pass_on(): return lax.ppermute(block, 'expert', route)  9.8 us
  transfers between devices with their start and end apart: 14, of which 7 were waited for; matrix products, arithmetic and copies ran while one was open for 0% of the time, Pallas kernels for 3%

profile of v2, /device:TPU:2, one launch (start us, length us, event | category | flops | bytes accessed | tf_op | source)
XLA Modules:
  0.0 219.1 jit_solution(8133447295592842536)
XLA Ops:
  0.7 1.3 copy-done.2
  3.3 1.2 shard_map.86
  4.5 15.2 %all-to-all-start = ((bf16[16,16,896]{2,1,0:T(8,128)(2,1)}), bf16[16,16,896]{2,1,0:T(8,128)(2,1)S(1)}, u32[]{:S(2)}, u32[]{:S(2)}) async-start(bf16[16,16,896]{2,1,0:T(8,128)(2,1)} %get-tuple-element.17), calls=%async_computation | async-start | bytes 917504 | tf_op jit(solution)/shard_map/all_to_all | solution.py:31
  19.7 2.4 %collective-permute-start = (bf16[3584,128]{1,0:T(8,128)(2,1)S(1)}, bf16[3584,128]{1,0:T(8,128)(2,1)}, u32[]{:S(2)}, u32[]{:S(2)}) collective-permute-start(bf16[3584,128]{1,0:T(8,128)(2,1)S(1)} %bitcast.24), channel_id=1, source_target_pairs={{0,1},{1,0},{2,3},{3,2},{4,5},{5,4},{6,7},{7,6},{8,9},{9,8},{10,11... | collective-permute-start | bytes 2752520 | tf_op jit(solution)/shard_map/ppermute | solution.py:47
  22.2 3.4 %collective-permute-start.1 = (bf16[3584,128]{1,0:T(8,128)(2,1)S(1)}, bf16[3584,128]{1,0:T(8,128)(2,1)}, u32[]{:S(2)}, u32[]{:S(2)}) collective-permute-start(bf16[3584,128]{1,0:T(8,128)(2,1)S(1)} %bitcast.27), channel_id=1, source_target_pairs={{0,1},{1,0},{2,3},{3,2},{4,5},{5,4},{6,7},{7,6},{8,9},{9,8},{10,11... | collective-permute-start | bytes 2752520 | tf_op jit(solution)/shard_map/ppermute | solution.py:47
  25.7 1.2 copy-done.3
  27.2 5.6 %collective-permute-start.4 = (bf16[896,128]{1,0:T(8,128)(2,1)S(1)}, bf16[896,128]{1,0:T(8,128)(2,1)S(1)}, u32[]{:S(2)}, u32[]{:S(2)}) collective-permute-start(bf16[896,128]{1,0:T(8,128)(2,1)S(1)} %get-tuple-element.21), channel_id=1, source_target_pairs={{0,6},{1,7},{2,4},{3,5},{4,2},{5,3},{6,0},{7,1},{8,14},{9,15},{10,... | collective-permute-start | bytes 688136 | tf_op jit(solution)/shard_map/ppermute | solution.py:52
  32.8 1.9 collective-permute-start.3
  34.7 2.6 %collective-permute-start.2 = (bf16[896,128]{1,0:T(8,128)(2,1)S(1)}, bf16[896,128]{1,0:T(8,128)(2,1)S(1)}, u32[]{:S(2)}, u32[]{:S(2)}) collective-permute-start(bf16[896,128]{1,0:T(8,128)(2,1)S(1)} %get-tuple-element.19), channel_id=1, source_target_pairs={{0,2},{1,3},{2,0},{3,1},{4,6},{5,7},{6,4},{7,5},{8,10},{9,11},{10,... | collective-permute-start | bytes 688136 | tf_op jit(solution)/shard_map/ppermute | solution.py:52
  37.3 12.6 %collective-permute-done.4 = bf16[896,128]{1,0:T(8,128)(2,1)S(1)} collective-permute-done((bf16[896,128]{1,0:T(8,128)(2,1)S(1)}, bf16[896,128]{1,0:T(8,128)(2,1)S(1)}, u32[]{:S(2)}, u32[]{:S(2)}) %collective-permute-start.4) | collective-permute-done | bytes 229408 | tf_op jit(solution)/shard_map/ppermute | solution.py:52
  49.9 12.4 %collective-permute-done.3 = bf16[896,128]{1,0:T(8,128)(2,1)S(1)} collective-permute-done((bf16[896,128]{1,0:T(8,128)(2,1)S(1)}, bf16[896,128]{1,0:T(8,128)(2,1)S(1)}, u32[]{:S(2)}, u32[]{:S(2)}) %collective-permute-start.3) | collective-permute-done | bytes 229408 | tf_op jit(solution)/shard_map/ppermute | solution.py:52
  62.4 0.8 collective-permute-done.1.wu2
  63.2 1.3 collective-permute-start.5
  64.5 4.6 %collective-permute-start.7 = (bf16[256,896]{1,0:T(8,128)(2,1)S(1)}, bf16[256,896]{1,0:T(8,128)(2,1)S(1)}, u32[]{:S(2)}, u32[]{:S(2)}) collective-permute-start(bf16[256,896]{1,0:T(8,128)(2,1)S(1)} %bitcast.31), channel_id=1, source_target_pairs={{0,2},{1,3},{2,4},{3,5},{4,6},{5,7},{8,10},{9,11},{10,12},{11,13},... | collective-permute-start | bytes 1376264 | tf_op jit(solution)/shard_map/ppermute | solution.py:42
  69.1 7.1 %collective-permute-done.5.up1 = bf16[256,896]{1,0:T(8,128)(2,1)S(1)} collective-permute-done((bf16[256,896]{1,0:T(8,128)(2,1)S(1)}, bf16[256,896]{1,0:T(8,128)(2,1)S(1)}, u32[]{:S(2)}, u32[]{:S(2)}) %collective-permute-start.5) | collective-permute-done | bytes 458784 | tf_op jit(solution)/shard_map/ppermute | solution.py:42
  76.2 1.3 collective-permute-start.6
  78.2 2.4 %collective-permute-start.11 = (bf16[4,896,128]{2,1,0:T(8,128)(2,1)S(1)}, bf16[4,896,128]{2,1,0:T(8,128)(2,1)S(1)}, u32[]{:S(2)}, u32[]{:S(2)}) collective-permute-start(bf16[4,896,128]{2,1,0:T(8,128)(2,1)S(1)} %pad_maximum_fusion.down), channel_id=1, source_target_pairs={{0,1},{1,0},{2,3},{3,2},{4,5},{5,4},{6,7},{7,6},{8,9},{9,8},{10,11... | collective-permute-start | bytes 2752520 | tf_op jit(solution)/shard_map/ppermute | solution.py:47
  80.6 7.6 %collective-permute-done.6.up2 = bf16[256,896]{1,0:T(8,128)(2,1)S(1)} collective-permute-done((bf16[256,896]{1,0:T(8,128)(2,1)S(1)}, bf16[256,896]{1,0:T(8,128)(2,1)S(1)}, u32[]{:S(2)}, u32[]{:S(2)}) %collective-permute-start.6) | collective-permute-done | bytes 458784 | tf_op jit(solution)/shard_map/ppermute | solution.py:42
  88.2 1.3 collective-permute-start.9
  90.2 3.6 %shard_map.88.acts = f32[256,512]{1,0:T(8,128)S(1)} custom-call(s32[1]{0:T(128)} %bitcast.5.quad_ref, bf16[256,896]{1,0:T(8,128)(2,1)S(1)} %bitcast.32, bf16[256,896]{1,0:T(8,128)(2,1)S(1)} %collective-permute-done.5.up1, bf16[256,896]{1,0:T(8,128)(2,1)S(1)} %collective-permute-done.6.up2, bf16[256,896]{1,0:T(8,128)(2,1)S(1)} %collective-permute-done.7.down1, ...), custom_call_target="tpu_custom_call" | custom-call | flops 939524096 | bytes 3670016 | tf_op jit(solution)/shard_map/pallas_call | solution.py:72
  93.8 5.5 %collective-permute-done.9.up3 = bf16[256,896]{1,0:T(8,128)(2,1)S(1)} collective-permute-done((bf16[256,896]{1,0:T(8,128)(2,1)S(1)}, bf16[256,896]{1,0:T(8,128)(2,1)S(1)}, u32[]{:S(2)}, u32[]{:S(2)}) %collective-permute-start.9) | collective-permute-done | bytes 458784 | tf_op jit(solution)/shard_map/ppermute | solution.py:42
  99.3 2.1 shard_map.89
  101.5 15.6 %all_to_all.30.hidden = bf16[4,256,256]{2,1,0:T(8,128)(2,1)S(1)} all-to-all(bf16[4,256,256]{2,1,0:T(8,128)(2,1)S(1)} %shard_map.89), channel_id=1, replica_groups={{0,2,4,6},{1,3,5,7},{8,10,12,14},{9,11,13,15},{16,18,20,22},{17,19,21,2..., dimensions={0} | all-to-all | bytes 1048576 | tf_op jit(solution)/shard_map/all_to_all | solution.py:31
  117.0 0.7 shard_map.90
  117.8 29.1 %all_to_all.31.back = bf16[16,16,896]{2,1,0:T(8,128)(2,1)S(1)} all-to-all(bf16[16,16,896]{2,1,0:T(8,128)(2,1)S(1)} %shard_map.90), channel_id=1, replica_groups={{0,2,4,6,8,10,12,14,16,18,20,22,24,26,28,30},{1,3,5,7,9,11,13,15,17,19,..., dimensions={0} | all-to-all | bytes 917504 | tf_op jit(solution)/shard_map/all_to_all | solution.py:31
  146.9 2.1 shard_map.91
  149.0 7.5 %all-to-all-start.3 = ((bf16[16,16,896]{2,1,0:T(8,128)(2,1)}), bf16[16,16,896]{2,1,0:T(8,128)(2,1)S(1)}, u32[]{:S(2)}, u32[]{:S(2)}) async-start(bf16[16,16,896]{2,1,0:T(8,128)(2,1)} %get-tuple-element.29), calls=%async_computation.3 | async-start | bytes 917504 | tf_op jit(solution)/shard_map/all_to_all | solution.py:31
  156.5 22.8 %all-to-all-done.3 = bf16[16,16,896]{2,1,0:T(8,128)(2,1)S(1)} async-done(((bf16[16,16,896]{2,1,0:T(8,128)(2,1)}), bf16[16,16,896]{2,1,0:T(8,128)(2,1)S(1)}, u32[]{:S(2)}, u32[]{:S(2)}) %all-to-all-start.3) | async-done | bytes 458784 | tf_op jit(solution)/shard_map/all_to_all | solution.py:31
  179.3 0.7 shard_map.92
  180.0 20.3 %all_to_all.32 = bf16[4,4,448,128]{3,2,1,0:T(8,128)(2,1)S(1)} all-to-all(bf16[4,4,448,128]{3,2,1,0:T(8,128)(2,1)S(1)} %shard_map.92), channel_id=1, replica_groups={{0,1,256,257},{2,3,258,259},{4,5,260,261},{6,7,262,263},{8,9,264,265},{..., dimensions={0} | all-to-all | bytes 3670016 | tf_op jit(solution)/shard_map/all_to_all | solution.py:31
  200.8 17.3 %all_to_all.33 = bf16[4,448,128]{2,1,0:T(8,128)(2,1)S(1)} all-to-all(bf16[4,448,128]{2,1,0:T(8,128)(2,1)S(1)} %reduce_sum.12), channel_id=1, replica_groups={{0,2,4,6},{1,3,5,7},{8,10,12,14},{9,11,13,15},{16,18,20,22},{17,19,21,2..., dimensions={0} | all-to-all | bytes 917504 | tf_op jit(solution)/shard_map/all_to_all | solution.py:31
  218.1 1.0 copy.9
  (24 shorter events, 3.8 us)
Async XLA Ops:
  0.6 19.1 %copy-start = (bf16[1,3584,128]{2,1,0:T(8,128)(2,1)S(1)}, bf16[1,3584,128]{2,1,0:T(8,128)(2,1)}, u32[]{:S(2)}) copy-start(bf16[1,3584,128]{2,1,0:T(8,128)(2,1)} %param.11) | copy-start | bytes 2752516
  0.6 21.6 %copy-start.1 = (bf16[1,3584,128]{2,1,0:T(8,128)(2,1)S(1)}, bf16[1,3584,128]{2,1,0:T(8,128)(2,1)}, u32[]{:S(2)}) copy-start(bf16[1,3584,128]{2,1,0:T(8,128)(2,1)} %param.12) | copy-start | bytes 2752516
  0.7 1.3 copy-start.2
  2.0 0.7 copy-start.4
  2.6 0.7 copy-start.5
  4.5 58.7 %all-to-all-start = ((bf16[16,16,896]{2,1,0:T(8,128)(2,1)}), bf16[16,16,896]{2,1,0:T(8,128)(2,1)S(1)}, u32[]{:S(2)}, u32[]{:S(2)}) async-start(bf16[16,16,896]{2,1,0:T(8,128)(2,1)} %get-tuple-element.17), calls=%async_computation | async-start | bytes 917504 | tf_op jit(solution)/shard_map/all_to_all | solution.py:31
  19.7 42.7 %collective-permute-start = (bf16[3584,128]{1,0:T(8,128)(2,1)S(1)}, bf16[3584,128]{1,0:T(8,128)(2,1)}, u32[]{:S(2)}, u32[]{:S(2)}) collective-permute-start(bf16[3584,128]{1,0:T(8,128)(2,1)S(1)} %bitcast.24), channel_id=1, source_target_pairs={{0,1},{1,0},{2,3},{3,2},{4,5},{5,4},{6,7},{7,6},{8,9},{9,8},{10,11... | collective-permute-start | bytes 2752520 | tf_op jit(solution)/shard_map/ppermute | solution.py:47
  22.2 41.0 %collective-permute-start.1 = (bf16[3584,128]{1,0:T(8,128)(2,1)S(1)}, bf16[3584,128]{1,0:T(8,128)(2,1)}, u32[]{:S(2)}, u32[]{:S(2)}) collective-permute-start(bf16[3584,128]{1,0:T(8,128)(2,1)S(1)} %bitcast.27), channel_id=1, source_target_pairs={{0,1},{1,0},{2,3},{3,2},{4,5},{5,4},{6,7},{7,6},{8,9},{9,8},{10,11... | collective-permute-start | bytes 2752520 | tf_op jit(solution)/shard_map/ppermute | solution.py:47
  25.6 1.2 copy-start.3
  27.2 22.7 %collective-permute-start.4 = (bf16[896,128]{1,0:T(8,128)(2,1)S(1)}, bf16[896,128]{1,0:T(8,128)(2,1)S(1)}, u32[]{:S(2)}, u32[]{:S(2)}) collective-permute-start(bf16[896,128]{1,0:T(8,128)(2,1)S(1)} %get-tuple-element.21), channel_id=1, source_target_pairs={{0,6},{1,7},{2,4},{3,5},{4,2},{5,3},{6,0},{7,1},{8,14},{9,15},{10,... | collective-permute-start | bytes 688136 | tf_op jit(solution)/shard_map/ppermute | solution.py:52
  32.8 29.5 %collective-permute-start.3 = (bf16[896,128]{1,0:T(8,128)(2,1)S(1)}, bf16[896,128]{1,0:T(8,128)(2,1)S(1)}, u32[]{:S(2)}, u32[]{:S(2)}) collective-permute-start(bf16[896,128]{1,0:T(8,128)(2,1)S(1)} %get-tuple-element.20), channel_id=1, source_target_pairs={{0,4},{1,5},{2,6},{3,7},{4,0},{5,1},{6,2},{7,3},{8,12},{9,13},{10,... | collective-permute-start | bytes 688136 | tf_op jit(solution)/shard_map/ppermute | solution.py:52
  34.7 27.6 %collective-permute-start.2 = (bf16[896,128]{1,0:T(8,128)(2,1)S(1)}, bf16[896,128]{1,0:T(8,128)(2,1)S(1)}, u32[]{:S(2)}, u32[]{:S(2)}) collective-permute-start(bf16[896,128]{1,0:T(8,128)(2,1)S(1)} %get-tuple-element.19), channel_id=1, source_target_pairs={{0,2},{1,3},{2,0},{3,1},{4,6},{5,7},{6,4},{7,5},{8,10},{9,11},{10,... | collective-permute-start | bytes 688136 | tf_op jit(solution)/shard_map/ppermute | solution.py:52
  63.2 13.0 %collective-permute-start.5 = (bf16[256,896]{1,0:T(8,128)(2,1)S(1)}, bf16[256,896]{1,0:T(8,128)(2,1)S(1)}, u32[]{:S(2)}, u32[]{:S(2)}) collective-permute-start(bf16[256,896]{1,0:T(8,128)(2,1)S(1)} %bitcast.30), channel_id=1, source_target_pairs={{2,0},{3,1},{4,2},{5,3},{6,4},{7,5},{10,8},{11,9},{12,10},{13,11},... | collective-permute-start | bytes 1376264 | tf_op jit(solution)/shard_map/ppermute | solution.py:42
  64.5 13.0 %collective-permute-start.7 = (bf16[256,896]{1,0:T(8,128)(2,1)S(1)}, bf16[256,896]{1,0:T(8,128)(2,1)S(1)}, u32[]{:S(2)}, u32[]{:S(2)}) collective-permute-start(bf16[256,896]{1,0:T(8,128)(2,1)S(1)} %bitcast.31), channel_id=1, source_target_pairs={{0,2},{1,3},{2,4},{3,5},{4,6},{5,7},{8,10},{9,11},{10,12},{11,13},... | collective-permute-start | bytes 1376264 | tf_op jit(solution)/shard_map/ppermute | solution.py:42
  76.2 12.0 %collective-permute-start.6 = (bf16[256,896]{1,0:T(8,128)(2,1)S(1)}, bf16[256,896]{1,0:T(8,128)(2,1)S(1)}, u32[]{:S(2)}, u32[]{:S(2)}) collective-permute-start(bf16[256,896]{1,0:T(8,128)(2,1)S(1)} %collective-permute-done.5.up1), channel_id=1, source_target_pairs={{2,0},{3,1},{4,2},{5,3},{10,8},{11,9},{12,10},{13,11},{18,16},{19,... | collective-permute-start | bytes 1376264 | tf_op jit(solution)/shard_map/ppermute | solution.py:42
  77.5 12.0 %collective-permute-start.8 = (bf16[256,896]{1,0:T(8,128)(2,1)S(1)}, bf16[256,896]{1,0:T(8,128)(2,1)S(1)}, u32[]{:S(2)}, u32[]{:S(2)}) collective-permute-start(bf16[256,896]{1,0:T(8,128)(2,1)S(1)} %collective-permute-done.7.down1), channel_id=1, source_target_pairs={{2,4},{3,5},{4,6},{5,7},{10,12},{11,13},{12,14},{13,15},{18,20},{1... | collective-permute-start | bytes 1376264 | tf_op jit(solution)/shard_map/ppermute | solution.py:42
  78.2 23.3 %collective-permute-start.11 = (bf16[4,896,128]{2,1,0:T(8,128)(2,1)S(1)}, bf16[4,896,128]{2,1,0:T(8,128)(2,1)S(1)}, u32[]{:S(2)}, u32[]{:S(2)}) collective-permute-start(bf16[4,896,128]{2,1,0:T(8,128)(2,1)S(1)} %pad_maximum_fusion.down), channel_id=1, source_target_pairs={{0,1},{1,0},{2,3},{3,2},{4,5},{5,4},{6,7},{7,6},{8,9},{9,8},{10,11... | collective-permute-start | bytes 2752520 | tf_op jit(solution)/shard_map/ppermute | solution.py:47
  88.2 11.1 %collective-permute-start.9 = (bf16[256,896]{1,0:T(8,128)(2,1)S(1)}, bf16[256,896]{1,0:T(8,128)(2,1)S(1)}, u32[]{:S(2)}, u32[]{:S(2)}) collective-permute-start(bf16[256,896]{1,0:T(8,128)(2,1)S(1)} %collective-permute-done.6.up2), channel_id=1, source_target_pairs={{2,0},{3,1},{10,8},{11,9},{18,16},{19,17},{26,24},{27,25},{34,32},... | collective-permute-start | bytes 1376264 | tf_op jit(solution)/shard_map/ppermute | solution.py:42
  89.5 9.8 %collective-permute-start.10 = (bf16[256,896]{1,0:T(8,128)(2,1)S(1)}, bf16[256,896]{1,0:T(8,128)(2,1)S(1)}, u32[]{:S(2)}, u32[]{:S(2)}) collective-permute-start(bf16[256,896]{1,0:T(8,128)(2,1)S(1)} %collective-permute-done.8.down2), channel_id=1, source_target_pairs={{4,6},{5,7},{12,14},{13,15},{20,22},{21,23},{28,30},{29,31},{36,38... | collective-permute-start | bytes 1376264 | tf_op jit(solution)/shard_map/ppermute | solution.py:42
  117.0 29.9 %copy-start.6 = (f32[1,128]{1,0:T(1,128)S(1)}, f32[1,128]{1,0:T(1,128)}, u32[]{:S(2)}) copy-start(f32[1,128]{1,0:T(1,128)} %loss_ref.1) | copy-start | bytes 1540
  149.0 30.3 %all-to-all-start.3 = ((bf16[16,16,896]{2,1,0:T(8,128)(2,1)}), bf16[16,16,896]{2,1,0:T(8,128)(2,1)S(1)}, u32[]{:S(2)}, u32[]{:S(2)}) async-start(bf16[16,16,896]{2,1,0:T(8,128)(2,1)} %get-tuple-element.29), calls=%async_computation.3 | async-start | bytes 917504 | tf_op jit(solution)/shard_map/all_to_all | solution.py:31

commit v3 on v2

--- a/solution.py
+++ b/solution.py
@@ -52,6 +52,16 @@
     return lax.ppermute(block, "expert", [(i, i ^ 2 * distance) for i in range(count)])
 
 
+def cross(block, flip_side, flip_pipe):
+    pipes, count = lax.axis_size("pipe"), lax.axis_size("expert")
+    route = []
+    for p in range(pipes):
+        for i in range(count):
+            other = (p + pipes // 2) % pipes if flip_pipe else p
+            route.append((p * count + i, other * count + (i ^ 1 if flip_side else i)))
+    return lax.ppermute(block, ("pipe", "expert"), route)
+
+
 def reduce_groups(pipes, count):
     half = pipes // 2
     return [
@@ -65,10 +75,10 @@
     return lax.dot_general(a, b, (dims, ((), ())), preferred_element_type=F32)
 
 
-def kernel_call(body, out_shape, flops, moved, scalars=0, **kwargs):
+def kernel_call(body, out_shape, flops, moved, scalars=0, space=pltpu.VMEM, **kwargs):
     def call(*operands):
         specs = [pl.BlockSpec(memory_space=pltpu.SMEM)] * scalars
-        specs += [pl.BlockSpec(memory_space=pltpu.VMEM)] * (len(operands) - scalars)
+        specs += [pl.BlockSpec(memory_space=space)] * (len(operands) - scalars)
         return pl.pallas_call(
             body,
             out_shape=out_shape,
@@ -82,9 +92,13 @@
     return call
 
 
-def relay_kernel(quad_ref, w_ref, *rest):
+def quad_of(place_ref):
+    return (place_ref[0] & (SPLIT - 1)) >> 1
+
+
+def relay_kernel(place_ref, w_ref, *rest):
     outs, turned = rest[:-1], rest[-1]
-    quad = quad_ref[0]
+    quad = quad_of(place_ref)
     turned[...] = w_ref[...].T
     eighth = outs[0].shape[0] // 2
     for d, out in enumerate(outs):
@@ -93,7 +107,13 @@
             out[h * eighth : (h + 1) * eighth, :] = turned[pl.ds(start, eighth), :]
 
 
-def gather_kernel(window, ids_ref, gates_ref, tok_ref, picked_ref, spread_ref):
+def gather_kernel(window, ids, gates, tokens, picked_ref, spread_ref, ids_ref, gates_ref, tok_ref, sems):
+    pairs = ((ids, ids_ref), (gates, gates_ref), (tokens, tok_ref))
+    copies = [pltpu.make_async_copy(a, b, sems.at[n]) for n, (a, b) in enumerate(pairs)]
+    for copy in copies:
+        copy.start()
+    for copy in copies:
+        copy.wait()
     slots, toks = window * CAP, tok_ref.shape[0]
     slot = lax.broadcasted_iota(jnp.int32, (slots, toks), 0)
     expert, nth = slot // CAP, slot % CAP
@@ -117,13 +137,13 @@
             picked_ref[k * QUADS + q] = rows[k * CAP : (k + 1) * CAP]
 
 
-def acts_kernel(quad_ref, here, up1, up2, down1, down2, wg, wu, wg2, wu2, acts_ref):
-    quad = quad_ref[0]
+def acts_kernel(place_ref, here, up1, up2, down1, down2, wg, wu, wg2, wu2, acts_ref):
+    quad = quad_of(place_ref)
     quarter, units = here.shape[1], wg.shape[1]
     parts = ((here, None, 0), (up1, None, 1), (down1, None, 3), (up2, down2, 2))
     totals = [None] * 4
     for first, second, distance in parts:
-        start = pl.multiple_of((quad + distance) % QUADS * quarter, quarter)
+        start = pl.multiple_of(((quad + distance) & (QUADS - 1)) * quarter, quarter)
         rows = first[...] if second is None else first[...] + second[...]
         for n, weight in enumerate((wg, wu, wg2, wu2)):
             part = dot(rows, weight[pl.ds(start, quarter), :])
@@ -132,8 +152,8 @@
         acts_ref[:, n * units : (n + 1) * units] = totals[n]
 
 
-def hidden_kernel(quad_ref, acts, up3, down3, wg, wu, wg2, wu2, hidden_ref):
-    quad = quad_ref[0]
+def hidden_kernel(place_ref, acts, up3, down3, wg, wu, wg2, wu2, hidden_ref):
+    quad = quad_of(place_ref)
     quarter, units = up3.shape[1], wg.shape[1]
     last = jnp.where(quad * 2 < QUADS, QUADS - 1, 0)
     start = pl.multiple_of(last * quarter, quarter)
@@ -148,8 +168,8 @@
             hidden_ref[s, :, side * units : (side + 1) * units] = value
 
 
-def down_kernel(quad_ref, hidden, down, down_other, out_ref):
-    quad = quad_ref[0]
+def down_kernel(place_ref, hidden, down, down_other, out_ref):
+    quad = quad_of(place_ref)
     total = None
     for d in range(QUADS):
         slab = jnp.concatenate([down[d], down_other[d]], axis=1)
@@ -182,27 +202,36 @@
     mixed_ref[...] = jnp.concatenate(halves[0] + halves[1], axis=1)
 
 
-def grads_kernel(side_ref, cotan, hidden, grads_ref):
-    side = side_ref[0]
-    eighth, units = grads_ref.shape[2:]
+def turn_kernel(cotan, out_ref):
+    turned = cotan[...].T
+    eighth = out_ref.shape[1]
+    for h in range(2):
+        for side in range(2):
+            out_ref[2 * h + side] = turned[h * eighth : (h + 1) * eighth, :]
+
+
+def grads_kernel(place_ref, cotans, own, across, mirrored, opposite, grads_ref):
+    mine = 2 * place_ref[1] + (place_ref[0] & 1)
+    units = own.shape[2]
+    total = None
+    for flip, hidden in enumerate((own, across, mirrored, opposite)):
+        slab = jnp.concatenate([hidden[s] for s in range(QUADS)], axis=1)
+        part = dot(cotans[mine ^ flip], slab)
+        total = part if total is None else total + part
     for s in range(QUADS):
-        part = dot(cotan[...], hidden[s], ((0,), (0,))).astype(BF16)
-        for h in range(2):
-            for other in range(2):
-                grads_ref[2 * h + (side + other) % 2, s] = part[
-                    h * eighth : (h + 1) * eighth, other * units : (other + 1) * units
-                ]
+        grads_ref[s] = total[:, s * units : (s + 1) * units].astype(BF16)
 
 
 def per_device(tokens, expert_ids, gates, loss_weight, w_gate, w_up, w_down):
     tok_count, width = tokens.shape[1:]
+    choices = gates.shape[2]
     units = w_down.shape[1]
     count = lax.axis_size("expert")
     window = count // SPLIT
     quarter, eighth = width // QUADS, width // (2 * QUADS)
     place = lax.axis_index("expert")
-    quad = (place % SPLIT // 2).reshape(1)
-    side = (place % 2).reshape(1)
+    mirror = lax.axis_index("pipe") // (lax.axis_size("pipe") // 2)
+    place = jnp.stack([place, mirror])
     by_column, by_quad = columns(count), quads(count)
     blocks = count // 2
     held = blocks * CAP
@@ -213,8 +242,8 @@
     down = kernel_call(
         relay_kernel, (jax.ShapeDtypeStruct((quarter, units), BF16),) * QUADS,
         0, 4 * width * units, 1, scratch_shapes=[pltpu.VMEM((width, units), BF16)],
-    )(quad, w_down[0])
-    down = jnp.stack([down[0]] + [swap(down[d], d) for d in range(1, QUADS)])
+    )(place, w_down[0])
+    down = [down[0]] + [swap(down[d], d) for d in range(1, QUADS)]
 
     picked, spread = kernel_call(
         functools.partial(gather_kernel, window),
@@ -222,10 +251,19 @@
             jax.ShapeDtypeStruct((window * QUADS, CAP, quarter), BF16),
             jax.ShapeDtypeStruct((window * CAP, tok_count), F32),
         ),
-        2 * window * CAP * tok_count * width, 3 * tok_count * width,
+        2 * window * CAP * tok_count * width, 3 * tok_count * width, space=pl.ANY,
+        scratch_shapes=[
+            pltpu.VMEM((choices, tok_count), jnp.int32),
+            pltpu.VMEM((choices, tok_count), F32),
+            pltpu.VMEM((tok_count, width), BF16),
+            pltpu.SemaphoreType.DMA((3,)),
+        ],
     )(expert_ids[0].T, gates[0].T, tokens[0])
-    rows = exchange(picked, "expert", by_column).reshape(held, quarter)
-    rows, gate_other, up_other, down = lax.optimization_barrier((rows, gate_other, up_other, down))
+    once = lax.optimization_barrier(jnp.int32(1))
+    rows = lax.fori_loop(0, once, lambda _, blocks: exchange(blocks, "expert", by_column), picked)
+    rows = rows.reshape(held, quarter)
+    rows, gate_other, up_other, *down = lax.optimization_barrier((rows, gate_other, up_other, *down))
+    down = jnp.stack(down)
     down_other = neighbour(down)
     ups, downs = [rows], [rows]
     for turn in range(1, QUADS):
@@ -235,18 +273,21 @@
     acts = kernel_call(
         acts_kernel, jax.ShapeDtypeStruct((held, 4 * units), F32),
         8 * held * width * units, 8 * width * units, 1,
-    )(quad, rows, downs[1], downs[2], ups[1], ups[2], *weights)
+    )(place, rows, downs[1], downs[2], ups[1], ups[2], *weights)
     hidden = kernel_call(
         hidden_kernel, jax.ShapeDtypeStruct((QUADS, held, 2 * units), BF16),
         2 * held * width * units, 2 * width * units, 1,
-    )(quad, acts, downs[3], ups[3], *weights)
+    )(place, acts, downs[3], ups[3], *weights)
     hidden, down_other = lax.optimization_barrier((hidden, down_other))
     hidden = exchange(hidden, "expert", by_quad)
     out = kernel_call(
         down_kernel, jax.ShapeDtypeStruct((blocks, CAP, quarter), BF16),
         4 * held * width * units, 4 * width * units, 1,
-    )(quad, hidden, down, down_other)
+    )(place, hidden, down, down_other)
     back = exchange(out, "expert", by_column)
+    own, other = hidden[:, :, :units], hidden[:, :, units:]
+    across, mirrored, opposite = cross(other, 1, 0), cross(own, 0, 1), cross(other, 1, 1)
+    back, across, mirrored, opposite = lax.optimization_barrier((back, across, mirrored, opposite))
 
     output, cotan = kernel_call(
         functools.partial(mix_kernel, window),
@@ -258,13 +299,15 @@
     )(spread, loss_weight, back)
     cotan = exchange(cotan, "expert", by_column).reshape(held, quarter)
 
-    grads = kernel_call(
-        grads_kernel, jax.ShapeDtypeStruct((2 * 2, QUADS, eighth, units), BF16),
+    groups = reduce_groups(lax.axis_size("pipe"), count)
+    cotan = kernel_call(
+        turn_kernel, jax.ShapeDtypeStruct((2 * 2, eighth, held), BF16), 0, 6 * held * quarter
+    )(cotan)
+    cotan = exchange(cotan, ("pipe", "expert"), groups)
+    share = kernel_call(
+        grads_kernel, jax.ShapeDtypeStruct((QUADS, eighth, units), BF16),
         4 * held * width * units, 4 * width * units, 1,
-    )(side, cotan, hidden)
-    groups = reduce_groups(lax.axis_size("pipe"), count)
-    parts = exchange(grads, ("pipe", "expert"), groups)
-    share = jnp.sum(parts.astype(F32), axis=0).astype(BF16)
+    )(place, cotan, own, across, mirrored, opposite)
     share = exchange(share, "expert", by_quad).reshape(QUADS * eighth, units).T
     return output[None], share[None]
 

time: 220 us -> 212 us (0.964)
  waiting for transfers between devices: 68.8 us -> 56.3 us
  starting transfers between devices: 50.9 us -> 61.7 us
  blocking collectives: 82.3 us -> 74.3 us
    ppermute x3, waiting for transfers between devices: 25 us -> 0.01 us  [swap(): lax.ppermute(block, 'expert', [(i, i ^ 2 * distance) for i in range(count)])]
    ppermute x0 -> x3, starting transfers between devices: none -> 10.7 us  [cross(): return lax.ppermute(block, ('pipe', 'expert'), route)]
    all_to_all x2, waiting for transfers between devices: 22.8 us -> 31.8 us  [exchange(): lax.all_to_all(blocks, axis, 0, 0, axis_index_groups=groups, tiled=True)]
    all_to_all x4, blocking collectives: 82.3 us -> 74.3 us  [exchange(): lax.all_to_all(blocks, axis, 0, 0, axis_index_groups=groups, tiled=True)]
    ppermute x0 -> x3, waiting for transfers between devices: none -> 7.48 us  [cross(): return lax.ppermute(block, ('pipe', 'expert'), route)]
    ppermute x6, waiting for transfers between devices: 20.2 us -> 15.9 us  [pass_on(): return lax.ppermute(block, 'expert', route)]
    ppermute x3, starting transfers between devices: 8.29 us -> 12.3 us  [neighbour(): return lax.ppermute(block, 'expert', [(i, i ^ 1) for i in range(count)])]
    all_to_all x2, starting transfers between devices: 22.7 us -> 18.7 us  [exchange(): lax.all_to_all(blocks, axis, 0, 0, axis_index_groups=groups, tiled=True)]
  transfers between devices with their start and end apart: 14 -> 17, of which waited for: 7 -> 8; matrix products, arithmetic and copies ran while one was open for 0% -> 1% of each run, Pallas kernels for 3% -> 4%
where the time goes in v3:
time: 212 us; the launch traced here: 211 us
  blocking collectives  74.3 us (35%)
  starting transfers between devices  61.7 us (29%)
  waiting for transfers between devices  56.3 us (27%)
  Pallas kernels  12.8 us (6%)
  local copies, waits for them, and re-layouts  3.06 us (1%)
    all_to_all x4, blocking collectives, exchange(): lax.all_to_all(blocks, axis, 0, 0, axis_index_groups=groups, tiled=True)  74.3 us
    all_to_all x2, waiting for transfers between devices, exchange(): lax.all_to_all(blocks, axis, 0, 0, axis_index_groups=groups, tiled=True)  31.8 us
    all_to_all x2, starting transfers between devices, exchange(): lax.all_to_all(blocks, axis, 0, 0, axis_index_groups=groups, tiled=True)  18.7 us
    ppermute x6, waiting for transfers between devices, pass_on(): return lax.ppermute(block, 'expert', route)  15.9 us
    pallas_call x8, Pallas kernels, call(): pl.pallas_call(body, out_shape=out_shape, in_specs=specs, out_specs=jax.t...  12.8 us
    ppermute x3, starting transfers between devices, neighbour(): return lax.ppermute(block, 'expert', [(i, i ^ 1) for i in range(count)])  12.3 us
    ppermute x3, starting transfers between devices, cross(): return lax.ppermute(block, ('pipe', 'expert'), route)  10.7 us
    ppermute x3, starting transfers between devices, swap(): lax.ppermute(block, 'expert', [(i, i ^ 2 * distance) for i in range(count)])  10.1 us
  transfers between devices with their start and end apart: 17, of which 8 were waited for; matrix products, arithmetic and copies ran while one was open for 1% of the time, Pallas kernels for 4%

profile of v3, /device:TPU:2, one launch (start us, length us, event | category | flops | bytes accessed | tf_op | source)
XLA Modules:
  0.0 210.6 jit_solution(18263652066332453917)
XLA Ops:
  0.6 8.0 %collective-permute-start = (bf16[3584,128]{1,0:T(8,128)(2,1)}, bf16[3584,128]{1,0:T(8,128)(2,1)S(1)}, u32[]{:S(2)}, u32[]{:S(2)}) collective-permute-start(bf16[3584,128]{1,0:T(8,128)(2,1)} %bitcast.23), channel_id=1, source_target_pairs={{0,1},{1,0},{2,3},{3,2},{4,5},{5,4},{6,7},{7,6},{8,9},{9,8},{10,11... | collective-permute-start | bytes 2752520 | tf_op jit(solution)/shard_map/ppermute | solution.py:47
  8.6 1.9 collective-permute-start.1
  11.8 1.6 shard_map.87
  13.4 1.9 collective-permute-start.2
  15.4 3.2 %collective-permute-start.3 = (bf16[896,128]{1,0:T(8,128)(2,1)S(1)}, bf16[896,128]{1,0:T(8,128)(2,1)}, u32[]{:S(2)}, u32[]{:S(2)}) collective-permute-start(bf16[896,128]{1,0:T(8,128)(2,1)S(1)} %get-tuple-element.46), channel_id=1, source_target_pairs={{0,4},{1,5},{2,6},{3,7},{4,0},{5,1},{6,2},{7,3},{8,12},{9,13},{10,... | collective-permute-start | bytes 688136 | tf_op jit(solution)/shard_map/ppermute | solution.py:52
  18.6 5.0 %collective-permute-start.4 = (bf16[896,128]{1,0:T(8,128)(2,1)S(1)}, bf16[896,128]{1,0:T(8,128)(2,1)}, u32[]{:S(2)}, u32[]{:S(2)}) collective-permute-start(bf16[896,128]{1,0:T(8,128)(2,1)S(1)} %get-tuple-element.47), channel_id=1, source_target_pairs={{0,6},{1,7},{2,4},{3,5},{4,2},{5,3},{6,0},{7,1},{8,14},{9,15},{10,... | collective-permute-start | bytes 688136 | tf_op jit(solution)/shard_map/ppermute | solution.py:52
  23.6 1.5 shard_map.86
  25.1 42.9 %while.10 = (s32[]{:T(128)}, bf16[16,16,896]{2,1,0:T(8,128)(2,1)}, s32[]{:T(128)}, s32[]{:T(128)}) while((s32[]{:T(128)}, bf16[16,16,896]{2,1,0:T(8,128)(2,1)}, s32[]{:T(128)}, s32[]{:T(128)}) %tuple.29), condition=%wide.region_1.2_spmd, body=%wide.region_0.1_spmd.sunk | while | flops 2 | bytes 2293845 | solution.py:263
  25.1 11.3 %all-to-all-start = ((bf16[16,16,896]{2,1,0:T(8,128)(2,1)}), bf16[16,16,896]{2,1,0:T(8,128)(2,1)S(1)}, u32[]{:S(2)}, u32[]{:S(2)}) async-start(bf16[16,16,896]{2,1,0:T(8,128)(2,1)} %get-tuple-element.96), calls=%async_computation | async-start | bytes 917504 | tf_op jit(solution)/shard_map/while/body/all_to_all | solution.py:31
  36.4 30.8 %all-to-all-done = bf16[16,16,896]{2,1,0:T(8,128)(2,1)S(1)} async-done(((bf16[16,16,896]{2,1,0:T(8,128)(2,1)}), bf16[16,16,896]{2,1,0:T(8,128)(2,1)S(1)}, u32[]{:S(2)}, u32[]{:S(2)}) %all-to-all-start) | async-done | bytes 458784 | tf_op jit(solution)/shard_map/while/body/all_to_all | solution.py:31
  68.0 1.3 collective-permute-start.5
  69.3 4.6 %collective-permute-start.7 = (bf16[256,896]{1,0:T(8,128)(2,1)}, bf16[256,896]{1,0:T(8,128)(2,1)S(1)}, u32[]{:S(2)}, u32[]{:S(2)}) collective-permute-start(bf16[256,896]{1,0:T(8,128)(2,1)} %bitcast.36), channel_id=1, source_target_pairs={{0,2},{1,3},{2,4},{3,5},{4,6},{5,7},{8,10},{9,11},{10,12},{11,13},... | collective-permute-start | bytes 1376264 | tf_op jit(solution)/shard_map/ppermute | solution.py:42
  73.9 5.6 %collective-permute-done.5.up1 = bf16[256,896]{1,0:T(8,128)(2,1)S(1)} collective-permute-done((bf16[256,896]{1,0:T(8,128)(2,1)}, bf16[256,896]{1,0:T(8,128)(2,1)S(1)}, u32[]{:S(2)}, u32[]{:S(2)}) %collective-permute-start.5) | collective-permute-done | bytes 458784 | tf_op jit(solution)/shard_map/ppermute | solution.py:42
  79.5 1.3 collective-permute-start.6
  81.5 1.4 pad_maximum_fusion.down
  82.9 2.4 %collective-permute-start.11 = (bf16[4,896,128]{2,1,0:T(8,128)(2,1)S(1)}, bf16[4,896,128]{2,1,0:T(8,128)(2,1)S(1)}, u32[]{:S(2)}, u32[]{:S(2)}) collective-permute-start(bf16[4,896,128]{2,1,0:T(8,128)(2,1)S(1)} %pad_maximum_fusion.down), channel_id=1, source_target_pairs={{0,1},{1,0},{2,3},{3,2},{4,5},{5,4},{6,7},{7,6},{8,9},{9,8},{10,11... | collective-permute-start | bytes 2752520 | tf_op jit(solution)/shard_map/ppermute | solution.py:47
  85.4 5.0 %collective-permute-done.6.up2 = bf16[256,896]{1,0:T(8,128)(2,1)S(1)} collective-permute-done((bf16[256,896]{1,0:T(8,128)(2,1)S(1)}, bf16[256,896]{1,0:T(8,128)(2,1)S(1)}, u32[]{:S(2)}, u32[]{:S(2)}) %collective-permute-start.6) | collective-permute-done | bytes 458784 | tf_op jit(solution)/shard_map/ppermute | solution.py:42
  90.4 1.3 collective-permute-start.9
  92.4 3.1 %shard_map.88.acts = f32[256,512]{1,0:T(8,128)S(1)} custom-call(s32[2]{0:T(128)S(1)} %pad_add_fusion.place_ref, bf16[256,896]{1,0:T(8,128)(2,1)} %bitcast.37, bf16[256,896]{1,0:T(8,128)(2,1)S(1)} %collective-permute-done.5.up1, bf16[256,896]{1,0:T(8,128)(2,1)S(1)} %collective-permute-done.6.up2, bf16[256,896]{1,0:T(8,128)(2,1)S(1)} %collective-permute-done.7.down1, ...), custom_call_target="tpu_custom_call" | custom-call | flops 939524096 | bytes 3670016 | tf_op jit(solution)/shard_map/pallas_call | solution.py:82
  95.5 5.2 %collective-permute-done.9.up3 = bf16[256,896]{1,0:T(8,128)(2,1)S(1)} collective-permute-done((bf16[256,896]{1,0:T(8,128)(2,1)S(1)}, bf16[256,896]{1,0:T(8,128)(2,1)S(1)}, u32[]{:S(2)}, u32[]{:S(2)}) %collective-permute-start.9) | collective-permute-done | bytes 458784 | tf_op jit(solution)/shard_map/ppermute | solution.py:42
  103.1 15.0 %all_to_all.31.hidden = bf16[4,256,256]{2,1,0:T(8,128)(2,1)S(1)} all-to-all(bf16[4,256,256]{2,1,0:T(8,128)(2,1)S(1)} %shard_map.89), channel_id=1, replica_groups={{0,2,4,6},{1,3,5,7},{8,10,12,14},{9,11,13,15},{16,18,20,22},{17,19,21,2..., dimensions={0} | all-to-all | bytes 1048576 | tf_op jit(solution)/shard_map/all_to_all | solution.py:31
  118.0 2.0 shard_map.90
  120.1 7.4 %all-to-all-start.2 = ((bf16[16,16,896]{2,1,0:T(8,128)(2,1)}), bf16[16,16,896]{2,1,0:T(8,128)(2,1)S(1)}, u32[]{:S(2)}, u32[]{:S(2)}) async-start(bf16[16,16,896]{2,1,0:T(8,128)(2,1)} %shard_map.90), calls=%async_computation.2 | async-start | bytes 917504 | tf_op jit(solution)/shard_map/all_to_all | solution.py:31
  127.6 2.4 %collective-permute-start.12 = (bf16[4,256,128]{2,1,0:T(8,128)(2,1)S(1)}, bf16[4,256,128]{2,1,0:T(8,128)(2,1)S(1)}, u32[]{:S(2)}, u32[]{:S(2)}) collective-permute-start(bf16[4,256,128]{2,1,0:T(8,128)(2,1)S(1)} %get-tuple-element.70), channel_id=1, source_target_pairs={{0,1},{1,0},{2,3},{3,2},{4,5},{5,4},{6,7},{7,6},{8,9},{9,8},{10,11... | collective-permute-start | bytes 786440 | tf_op jit(solution)/shard_map/ppermute | solution.py:62
  130.1 5.1 %collective-permute-start.13 = (bf16[4,256,128]{2,1,0:T(8,128)(2,1)S(1)}, bf16[4,256,128]{2,1,0:T(8,128)(2,1)S(1)}, u32[]{:S(2)}, u32[]{:S(2)}) collective-permute-start(bf16[4,256,128]{2,1,0:T(8,128)(2,1)S(1)} %get-tuple-element.69.own), channel_id=1, source_target_pairs={{0,256},{1,257},{2,258},{3,259},{4,260},{5,261},{6,262},{7,263},{8... | collective-permute-start | bytes 786440 | tf_op jit(solution)/shard_map/ppermute | solution.py:62
  135.2 3.2 %collective-permute-start.14 = (bf16[4,256,128]{2,1,0:T(8,128)(2,1)S(1)}, bf16[4,256,128]{2,1,0:T(8,128)(2,1)S(1)}, u32[]{:S(2)}, u32[]{:S(2)}) collective-permute-start(bf16[4,256,128]{2,1,0:T(8,128)(2,1)S(1)} %get-tuple-element.70), channel_id=1, source_target_pairs={{0,257},{1,256},{2,259},{3,258},{4,261},{5,260},{6,263},{7,262},{8... | collective-permute-start | bytes 786440 | tf_op jit(solution)/shard_map/ppermute | solution.py:62
  138.4 3.3 %collective-permute-done.13.mirrored = bf16[4,256,128]{2,1,0:T(8,128)(2,1)S(1)} collective-permute-done((bf16[4,256,128]{2,1,0:T(8,128)(2,1)S(1)}, bf16[4,256,128]{2,1,0:T(8,128)(2,1)S(1)}, u32[]{:S(2)}, u32[]{:S(2)}) %collective-permute-start.13) | collective-permute-done | bytes 262176 | tf_op jit(solution)/shard_map/ppermute | solution.py:62
  141.7 4.2 %collective-permute-done.14.opposite = bf16[4,256,128]{2,1,0:T(8,128)(2,1)S(1)} collective-permute-done((bf16[4,256,128]{2,1,0:T(8,128)(2,1)S(1)}, bf16[4,256,128]{2,1,0:T(8,128)(2,1)S(1)}, u32[]{:S(2)}, u32[]{:S(2)}) %collective-permute-start.14) | collective-permute-done | bytes 262176 | tf_op jit(solution)/shard_map/ppermute | solution.py:62
  147.0 1.9 shard_map.91
  148.9 30.3 %all_to_all.32 = bf16[16,16,896]{2,1,0:T(8,128)(2,1)S(1)} all-to-all(bf16[16,16,896]{2,1,0:T(8,128)(2,1)S(1)} %get-tuple-element.59), channel_id=1, replica_groups={{0,2,4,6,8,10,12,14,16,18,20,22,24,26,28,30},{1,3,5,7,9,11,13,15,17,19,..., dimensions={0} | all-to-all | bytes 917504 | tf_op jit(solution)/shard_map/all_to_all | solution.py:31
  179.4 14.9 %all_to_all.33.cotans = bf16[4,448,256]{2,1,0:T(8,128)(2,1)S(1)} all-to-all(bf16[4,448,256]{2,1,0:T(8,128)(2,1)S(1)} %shard_map.92), channel_id=1, replica_groups={{0,1,256,257},{2,3,258,259},{4,5,260,261},{6,7,262,263},{8,9,264,265},{..., dimensions={0} | all-to-all | bytes 1835008 | tf_op jit(solution)/shard_map/all_to_all | solution.py:31
  195.5 14.1 %all_to_all.34 = bf16[4,448,128]{2,1,0:T(8,128)(2,1)S(1)} all-to-all(bf16[4,448,128]{2,1,0:T(8,128)(2,1)S(1)} %shard_map.93), channel_id=1, replica_groups={{0,2,4,6},{1,3,5,7},{8,10,12,14},{9,11,13,15},{16,18,20,22},{17,19,21,2..., dimensions={0} | all-to-all | bytes 917504 | tf_op jit(solution)/shard_map/all_to_all | solution.py:31
  (34 shorter events, 9.3 us)
Async XLA Ops:
  0.6 23.0 %copy-start.2 = (bf16[1,128,3584]{2,1,0:T(8,128)(2,1)S(1)}, bf16[1,128,3584]{2,1,0:T(8,128)(2,1)}, u32[]{:S(2)}) copy-start(bf16[1,128,3584]{2,1,0:T(8,128)(2,1)} %param.9) | copy-start | bytes 2752516
  0.6 67.3 %collective-permute-start = (bf16[3584,128]{1,0:T(8,128)(2,1)}, bf16[3584,128]{1,0:T(8,128)(2,1)S(1)}, u32[]{:S(2)}, u32[]{:S(2)}) collective-permute-start(bf16[3584,128]{1,0:T(8,128)(2,1)} %bitcast.23), channel_id=1, source_target_pairs={{0,1},{1,0},{2,3},{3,2},{4,5},{5,4},{6,7},{7,6},{8,9},{9,8},{10,11... | collective-permute-start | bytes 2752520 | tf_op jit(solution)/shard_map/ppermute | solution.py:47
  8.6 59.4 %collective-permute-start.1 = (bf16[3584,128]{1,0:T(8,128)(2,1)}, bf16[3584,128]{1,0:T(8,128)(2,1)S(1)}, u32[]{:S(2)}, u32[]{:S(2)}) collective-permute-start(bf16[3584,128]{1,0:T(8,128)(2,1)} %bitcast.26), channel_id=1, source_target_pairs={{0,1},{1,0},{2,3},{3,2},{4,5},{5,4},{6,7},{7,6},{8,9},{9,8},{10,11... | collective-permute-start | bytes 2752520 | tf_op jit(solution)/shard_map/ppermute | solution.py:47
  10.6 1.2 copy-start.3
  13.4 54.5 %collective-permute-start.2 = (bf16[896,128]{1,0:T(8,128)(2,1)}, bf16[896,128]{1,0:T(8,128)(2,1)}, u32[]{:S(2)}, u32[]{:S(2)}) collective-permute-start(bf16[896,128]{1,0:T(8,128)(2,1)} %get-tuple-element.45), channel_id=1, source_target_pairs={{0,2},{1,3},{2,0},{3,1},{4,6},{5,7},{6,4},{7,5},{8,10},{9,11},{10,... | collective-permute-start | bytes 688136 | tf_op jit(solution)/shard_map/ppermute | solution.py:52
  15.3 8.2 %copy-start.5 = (f32[1,128,8]{1,2,0:T(8,128)S(1)}, f32[1,128,8]{1,2,0:T(8,128)}, u32[]{:S(2)}) copy-start(f32[1,128,8]{1,2,0:T(8,128)} %param.11) | copy-start | bytes 12292
  15.4 8.2 %copy-start.4 = (s32[1,128,8]{1,2,0:T(8,128)S(1)}, s32[1,128,8]{1,2,0:T(8,128)}, u32[]{:S(2)}) copy-start(s32[1,128,8]{1,2,0:T(8,128)} %param.10) | copy-start | bytes 12292
  15.4 52.6 %collective-permute-start.3 = (bf16[896,128]{1,0:T(8,128)(2,1)S(1)}, bf16[896,128]{1,0:T(8,128)(2,1)}, u32[]{:S(2)}, u32[]{:S(2)}) collective-permute-start(bf16[896,128]{1,0:T(8,128)(2,1)S(1)} %get-tuple-element.46), channel_id=1, source_target_pairs={{0,4},{1,5},{2,6},{3,7},{4,0},{5,1},{6,2},{7,3},{8,12},{9,13},{10,... | collective-permute-start | bytes 688136 | tf_op jit(solution)/shard_map/ppermute | solution.py:52
  18.6 49.4 %collective-permute-start.4 = (bf16[896,128]{1,0:T(8,128)(2,1)S(1)}, bf16[896,128]{1,0:T(8,128)(2,1)}, u32[]{:S(2)}, u32[]{:S(2)}) collective-permute-start(bf16[896,128]{1,0:T(8,128)(2,1)S(1)} %get-tuple-element.47), channel_id=1, source_target_pairs={{0,6},{1,7},{2,4},{3,5},{4,2},{5,3},{6,0},{7,1},{8,14},{9,15},{10,... | collective-permute-start | bytes 688136 | tf_op jit(solution)/shard_map/ppermute | solution.py:52
  25.1 42.1 %all-to-all-start = ((bf16[16,16,896]{2,1,0:T(8,128)(2,1)}), bf16[16,16,896]{2,1,0:T(8,128)(2,1)S(1)}, u32[]{:S(2)}, u32[]{:S(2)}) async-start(bf16[16,16,896]{2,1,0:T(8,128)(2,1)} %get-tuple-element.96), calls=%async_computation | async-start | bytes 917504 | tf_op jit(solution)/shard_map/while/body/all_to_all | solution.py:31
  68.0 11.5 %collective-permute-start.5 = (bf16[256,896]{1,0:T(8,128)(2,1)}, bf16[256,896]{1,0:T(8,128)(2,1)S(1)}, u32[]{:S(2)}, u32[]{:S(2)}) collective-permute-start(bf16[256,896]{1,0:T(8,128)(2,1)} %bitcast.35), channel_id=1, source_target_pairs={{2,0},{3,1},{4,2},{5,3},{6,4},{7,5},{10,8},{11,9},{12,10},{13,11},... | collective-permute-start | bytes 1376264 | tf_op jit(solution)/shard_map/ppermute | solution.py:42
  69.3 11.5 %collective-permute-start.7 = (bf16[256,896]{1,0:T(8,128)(2,1)}, bf16[256,896]{1,0:T(8,128)(2,1)S(1)}, u32[]{:S(2)}, u32[]{:S(2)}) collective-permute-start(bf16[256,896]{1,0:T(8,128)(2,1)} %bitcast.36), channel_id=1, source_target_pairs={{0,2},{1,3},{2,4},{3,5},{4,6},{5,7},{8,10},{9,11},{10,12},{11,13},... | collective-permute-start | bytes 1376264 | tf_op jit(solution)/shard_map/ppermute | solution.py:42
  79.5 10.9 %collective-permute-start.6 = (bf16[256,896]{1,0:T(8,128)(2,1)S(1)}, bf16[256,896]{1,0:T(8,128)(2,1)S(1)}, u32[]{:S(2)}, u32[]{:S(2)}) collective-permute-start(bf16[256,896]{1,0:T(8,128)(2,1)S(1)} %collective-permute-done.5.up1), channel_id=1, source_target_pairs={{2,0},{3,1},{4,2},{5,3},{10,8},{11,9},{12,10},{13,11},{18,16},{19,... | collective-permute-start | bytes 1376264 | tf_op jit(solution)/shard_map/ppermute | solution.py:42
  80.8 10.9 %collective-permute-start.8 = (bf16[256,896]{1,0:T(8,128)(2,1)S(1)}, bf16[256,896]{1,0:T(8,128)(2,1)S(1)}, u32[]{:S(2)}, u32[]{:S(2)}) collective-permute-start(bf16[256,896]{1,0:T(8,128)(2,1)S(1)} %collective-permute-done.7.down1), channel_id=1, source_target_pairs={{2,4},{3,5},{4,6},{5,7},{10,12},{11,13},{12,14},{13,15},{18,20},{1... | collective-permute-start | bytes 1376264 | tf_op jit(solution)/shard_map/ppermute | solution.py:42
  81.5 10.9 %copy-start = (bf16[1,3584,128]{2,1,0:T(8,128)(2,1)S(1)}, bf16[1,3584,128]{2,1,0:T(8,128)(2,1)}, u32[]{:S(2)}) copy-start(bf16[1,3584,128]{2,1,0:T(8,128)(2,1)} %param.13) | copy-start | bytes 2752516
  81.5 10.9 %copy-start.1 = (bf16[1,3584,128]{2,1,0:T(8,128)(2,1)S(1)}, bf16[1,3584,128]{2,1,0:T(8,128)(2,1)}, u32[]{:S(2)}) copy-start(bf16[1,3584,128]{2,1,0:T(8,128)(2,1)} %param.14) | copy-start | bytes 2752516
  82.9 20.2 %collective-permute-start.11 = (bf16[4,896,128]{2,1,0:T(8,128)(2,1)S(1)}, bf16[4,896,128]{2,1,0:T(8,128)(2,1)S(1)}, u32[]{:S(2)}, u32[]{:S(2)}) collective-permute-start(bf16[4,896,128]{2,1,0:T(8,128)(2,1)S(1)} %pad_maximum_fusion.down), channel_id=1, source_target_pairs={{0,1},{1,0},{2,3},{3,2},{4,5},{5,4},{6,7},{7,6},{8,9},{9,8},{10,11... | collective-permute-start | bytes 2752520 | tf_op jit(solution)/shard_map/ppermute | solution.py:47
  90.4 10.4 %collective-permute-start.9 = (bf16[256,896]{1,0:T(8,128)(2,1)S(1)}, bf16[256,896]{1,0:T(8,128)(2,1)S(1)}, u32[]{:S(2)}, u32[]{:S(2)}) collective-permute-start(bf16[256,896]{1,0:T(8,128)(2,1)S(1)} %collective-permute-done.6.up2), channel_id=1, source_target_pairs={{2,0},{3,1},{10,8},{11,9},{18,16},{19,17},{26,24},{27,25},{34,32},... | collective-permute-start | bytes 1376264 | tf_op jit(solution)/shard_map/ppermute | solution.py:42
  91.7 9.1 %collective-permute-start.10 = (bf16[256,896]{1,0:T(8,128)(2,1)S(1)}, bf16[256,896]{1,0:T(8,128)(2,1)S(1)}, u32[]{:S(2)}, u32[]{:S(2)}) collective-permute-start(bf16[256,896]{1,0:T(8,128)(2,1)S(1)} %collective-permute-done.8.down2), channel_id=1, source_target_pairs={{4,6},{5,7},{12,14},{13,15},{20,22},{21,23},{28,30},{29,31},{36,38... | collective-permute-start | bytes 1376264 | tf_op jit(solution)/shard_map/ppermute | solution.py:42
  120.1 26.9 %all-to-all-start.2 = ((bf16[16,16,896]{2,1,0:T(8,128)(2,1)}), bf16[16,16,896]{2,1,0:T(8,128)(2,1)S(1)}, u32[]{:S(2)}, u32[]{:S(2)}) async-start(bf16[16,16,896]{2,1,0:T(8,128)(2,1)} %shard_map.90), calls=%async_computation.2 | async-start | bytes 917504 | tf_op jit(solution)/shard_map/all_to_all | solution.py:31
  127.6 10.8 %collective-permute-start.12 = (bf16[4,256,128]{2,1,0:T(8,128)(2,1)S(1)}, bf16[4,256,128]{2,1,0:T(8,128)(2,1)S(1)}, u32[]{:S(2)}, u32[]{:S(2)}) collective-permute-start(bf16[4,256,128]{2,1,0:T(8,128)(2,1)S(1)} %get-tuple-element.70), channel_id=1, source_target_pairs={{0,1},{1,0},{2,3},{3,2},{4,5},{5,4},{6,7},{7,6},{8,9},{9,8},{10,11... | collective-permute-start | bytes 786440 | tf_op jit(solution)/shard_map/ppermute | solution.py:62
  130.1 16.9 %copy-start.6 = (f32[1,128]{1,0:T(1,128)S(1)}, f32[1,128]{1,0:T(1,128)}, u32[]{:S(2)}) copy-start(f32[1,128]{1,0:T(1,128)} %loss_ref.1) | copy-start | bytes 1540
  130.1 11.6 %collective-permute-start.13 = (bf16[4,256,128]{2,1,0:T(8,128)(2,1)S(1)}, bf16[4,256,128]{2,1,0:T(8,128)(2,1)S(1)}, u32[]{:S(2)}, u32[]{:S(2)}) collective-permute-start(bf16[4,256,128]{2,1,0:T(8,128)(2,1)S(1)} %get-tuple-element.69.own), channel_id=1, source_target_pairs={{0,256},{1,257},{2,258},{3,259},{4,260},{5,261},{6,262},{7,263},{8... | collective-permute-start | bytes 786440 | tf_op jit(solution)/shard_map/ppermute | solution.py:62
  135.2 10.7 %collective-permute-start.14 = (bf16[4,256,128]{2,1,0:T(8,128)(2,1)S(1)}, bf16[4,256,128]{2,1,0:T(8,128)(2,1)S(1)}, u32[]{:S(2)}, u32[]{:S(2)}) collective-permute-start(bf16[4,256,128]{2,1,0:T(8,128)(2,1)S(1)} %get-tuple-element.70), channel_id=1, source_target_pairs={{0,257},{1,256},{2,259},{3,258},{4,261},{5,260},{6,263},{7,262},{8... | collective-permute-start | bytes 786440 | tf_op jit(solution)/shard_map/ppermute | solution.py:62

commit v4 on v3

--- a/solution.py
+++ b/solution.py
@@ -12,7 +12,7 @@
 QUADS = 4
 BF16 = jnp.bfloat16
 F32 = jnp.float32
-VMEM_LIMIT = 48 * 1024 * 1024
+VMEM_LIMIT = 20 * 1024 * 1024
 
 
 def columns(count):
@@ -260,7 +260,7 @@
         ],
     )(expert_ids[0].T, gates[0].T, tokens[0])
     once = lax.optimization_barrier(jnp.int32(1))
-    rows = lax.fori_loop(0, once, lambda _, blocks: exchange(blocks, "expert", by_column), picked)
+    rows = lax.cond(once > 0, lambda b: exchange(b, "expert", by_column), lambda b: b, picked)
     rows = rows.reshape(held, quarter)
     rows, gate_other, up_other, *down = lax.optimization_barrier((rows, gate_other, up_other, *down))
     down = jnp.stack(down)

time: 212 us -> 210 us (level)
  blocking collectives: 74.3 us -> 116 us
  waiting for transfers between devices: 56.3 us -> 26.2 us
  starting transfers between devices: 61.7 us -> 49.9 us
    all_to_all x4 -> x5, blocking collectives: 74.3 us -> 116 us  [exchange(): lax.all_to_all(blocks, axis, 0, 0, axis_index_groups=groups, tiled=True)]
    all_to_all x2 -> x1, waiting for transfers between devices: 31.8 us -> 1.06 us  [exchange(): lax.all_to_all(blocks, axis, 0, 0, axis_index_groups=groups, tiled=True)]
    all_to_all x2 -> x1, starting transfers between devices: 18.7 us -> 6.99 us  [exchange(): lax.all_to_all(blocks, axis, 0, 0, axis_index_groups=groups, tiled=True)]
  transfers between devices with their start and end apart: 17 -> 16, of which waited for: 8 -> 7; matrix products, arithmetic and copies ran while one was open for 1% -> 1% of each run, Pallas kernels for 4% -> 3%
where the time goes in v4:
time: 210 us
  blocking collectives  116 us (55%)
  starting transfers between devices  49.9 us (24%)
  waiting for transfers between devices  26.2 us (12%)
  Pallas kernels  11.5 us (5%)
  local copies, waits for them, and re-layouts  2.96 us (1%)
    all_to_all x5, blocking collectives, exchange(): lax.all_to_all(blocks, axis, 0, 0, axis_index_groups=groups, tiled=True)  116 us
    ppermute x6, waiting for transfers between devices, pass_on(): return lax.ppermute(block, 'expert', route)  16.1 us
    ppermute x3, starting transfers between devices, neighbour(): return lax.ppermute(block, 'expert', [(i, i ^ 1) for i in range(count)])  12.3 us
    pallas_call x8, Pallas kernels, call(): pl.pallas_call(body, out_shape=out_shape, in_specs=specs, out_specs=jax.t...  11.5 us
    ppermute x3, starting transfers between devices, cross(): return lax.ppermute(block, ('pipe', 'expert'), route)  10.7 us
    ppermute x3, starting transfers between devices, swap(): lax.ppermute(block, 'expert', [(i, i ^ 2 * distance) for i in range(count)])  10.1 us
    ppermute x6, starting transfers between devices, pass_on(): return lax.ppermute(block, 'expert', route)  9.81 us
    ppermute x3, waiting for transfers between devices, cross(): return lax.ppermute(block, ('pipe', 'expert'), route)  7.48 us
  transfers between devices with their start and end apart: 16, of which 7 were waited for; matrix products, arithmetic and copies ran while one was open for 1% of the time, Pallas kernels for 3%

profile of v4, /device:TPU:2, one launch (start us, length us, event | category | flops | bytes accessed | tf_op | source)
XLA Modules:
  0.0 209.6 jit_solution(14416355253833627613)
XLA Ops:
  0.6 8.0 %collective-permute-start = (bf16[3584,128]{1,0:T(8,128)(2,1)}, bf16[3584,128]{1,0:T(8,128)(2,1)S(1)}, u32[]{:S(2)}, u32[]{:S(2)}) collective-permute-start(bf16[3584,128]{1,0:T(8,128)(2,1)} %bitcast.23), channel_id=1, source_target_pairs={{0,1},{1,0},{2,3},{3,2},{4,5},{5,4},{6,7},{7,6},{8,9},{9,8},{10,11... | collective-permute-start | bytes 2752520 | tf_op jit(solution)/shard_map/ppermute | solution.py:47
  8.6 1.9 collective-permute-start.1
  11.8 1.6 shard_map.87
  13.4 1.9 collective-permute-start.2
  15.3 3.2 %collective-permute-start.3 = (bf16[896,128]{1,0:T(8,128)(2,1)S(1)}, bf16[896,128]{1,0:T(8,128)(2,1)}, u32[]{:S(2)}, u32[]{:S(2)}) collective-permute-start(bf16[896,128]{1,0:T(8,128)(2,1)S(1)} %get-tuple-element.38), channel_id=1, source_target_pairs={{0,4},{1,5},{2,6},{3,7},{4,0},{5,1},{6,2},{7,3},{8,12},{9,13},{10,... | collective-permute-start | bytes 688136 | tf_op jit(solution)/shard_map/ppermute | solution.py:52
  18.6 5.0 %collective-permute-start.4 = (bf16[896,128]{1,0:T(8,128)(2,1)S(1)}, bf16[896,128]{1,0:T(8,128)(2,1)}, u32[]{:S(2)}, u32[]{:S(2)}) collective-permute-start(bf16[896,128]{1,0:T(8,128)(2,1)S(1)} %get-tuple-element.39), channel_id=1, source_target_pairs={{0,6},{1,7},{2,4},{3,5},{4,2},{5,3},{6,0},{7,1},{8,14},{9,15},{10,... | collective-permute-start | bytes 688136 | tf_op jit(solution)/shard_map/ppermute | solution.py:52
  25.0 42.2 %conditional.1 = (bf16[16,16,896]{2,1,0:T(8,128)(2,1)S(1)}) conditional(s32[]{:T(128)} %convert_element_type.3, bf16[16,16,896]{2,1,0:T(8,128)(2,1)S(1)} %get-tuple-element.35, bf16[16,16,896]{2,1,0:T(8,128)(2,1)S(1)} %get-tuple-element.35), branch_computations={%region_0.1_spmd, %region_1.2_spmd} | conditional | bytes 917512 | solution.py:263
  25.0 42.2 %all_to_all.29 = bf16[16,16,896]{2,1,0:T(8,128)(2,1)S(1)} all-to-all(bf16[16,16,896]{2,1,0:T(8,128)(2,1)S(1)} %param.1), channel_id=1, replica_groups={{0,2,4,6,8,10,12,14,16,18,20,22,24,26,28,30},{1,3,5,7,9,11,13,15,17,19,..., dimensions={0} | all-to-all | bytes 917504 | tf_op jit(solution)/shard_map/cond/branch_1_fun/all_to_all | solution.py:31
  67.2 1.3 collective-permute-start.5
  68.5 4.6 %collective-permute-start.7 = (bf16[256,896]{1,0:T(8,128)(2,1)S(1)}, bf16[256,896]{1,0:T(8,128)(2,1)S(1)}, u32[]{:S(2)}, u32[]{:S(2)}) collective-permute-start(bf16[256,896]{1,0:T(8,128)(2,1)S(1)} %bitcast.36), channel_id=1, source_target_pairs={{0,2},{1,3},{2,4},{3,5},{4,6},{5,7},{8,10},{9,11},{10,12},{11,13},... | collective-permute-start | bytes 1376264 | tf_op jit(solution)/shard_map/ppermute | solution.py:42
  73.1 5.6 %collective-permute-done.5.up1 = bf16[256,896]{1,0:T(8,128)(2,1)S(1)} collective-permute-done((bf16[256,896]{1,0:T(8,128)(2,1)S(1)}, bf16[256,896]{1,0:T(8,128)(2,1)S(1)}, u32[]{:S(2)}, u32[]{:S(2)}) %collective-permute-start.5) | collective-permute-done | bytes 458784 | tf_op jit(solution)/shard_map/ppermute | solution.py:42
  78.7 1.3 collective-permute-start.6
  80.7 1.4 pad_maximum_fusion.down
  82.1 2.4 %collective-permute-start.11 = (bf16[4,896,128]{2,1,0:T(8,128)(2,1)S(1)}, bf16[4,896,128]{2,1,0:T(8,128)(2,1)S(1)}, u32[]{:S(2)}, u32[]{:S(2)}) collective-permute-start(bf16[4,896,128]{2,1,0:T(8,128)(2,1)S(1)} %pad_maximum_fusion.down), channel_id=1, source_target_pairs={{0,1},{1,0},{2,3},{3,2},{4,5},{5,4},{6,7},{7,6},{8,9},{9,8},{10,11... | collective-permute-start | bytes 2752520 | tf_op jit(solution)/shard_map/ppermute | solution.py:47
  84.6 4.8 %collective-permute-done.6.up2 = bf16[256,896]{1,0:T(8,128)(2,1)S(1)} collective-permute-done((bf16[256,896]{1,0:T(8,128)(2,1)S(1)}, bf16[256,896]{1,0:T(8,128)(2,1)S(1)}, u32[]{:S(2)}, u32[]{:S(2)}) %collective-permute-start.6) | collective-permute-done | bytes 458784 | tf_op jit(solution)/shard_map/ppermute | solution.py:42
  89.4 1.3 collective-permute-start.9
  91.4 2.6 %shard_map.88.acts = f32[256,512]{1,0:T(8,128)S(1)} custom-call(s32[2]{0:T(128)S(1)} %pad_add_fusion.place_ref, bf16[256,896]{1,0:T(8,128)(2,1)S(1)} %bitcast.37, bf16[256,896]{1,0:T(8,128)(2,1)S(1)} %collective-permute-done.5.up1, bf16[256,896]{1,0:T(8,128)(2,1)S(1)} %collective-permute-done.6.up2, bf16[256,896]{1,0:T(8,128)(2,1)S(1)} %collective-permute-done.7.down1, ...), custom_call_target="tpu_custom_call" | custom-call | flops 939524096 | bytes 3670016 | tf_op jit(solution)/shard_map/pallas_call | solution.py:82
  94.0 5.7 %collective-permute-done.9.up3 = bf16[256,896]{1,0:T(8,128)(2,1)S(1)} collective-permute-done((bf16[256,896]{1,0:T(8,128)(2,1)S(1)}, bf16[256,896]{1,0:T(8,128)(2,1)S(1)}, u32[]{:S(2)}, u32[]{:S(2)}) %collective-permute-start.9) | collective-permute-done | bytes 458784 | tf_op jit(solution)/shard_map/ppermute | solution.py:42
  99.7 1.2 shard_map.89
  100.9 1.6 collective-permute-done.11.down_other
  102.5 15.0 %all_to_all.30.hidden = bf16[4,256,256]{2,1,0:T(8,128)(2,1)S(1)} all-to-all(bf16[4,256,256]{2,1,0:T(8,128)(2,1)S(1)} %shard_map.89), channel_id=1, replica_groups={{0,2,4,6},{1,3,5,7},{8,10,12,14},{9,11,13,15},{16,18,20,22},{17,19,21,2..., dimensions={0} | all-to-all | bytes 1048576 | tf_op jit(solution)/shard_map/all_to_all | solution.py:31
  117.5 2.0 shard_map.90
  119.5 7.0 %all-to-all-start.2 = ((bf16[16,16,896]{2,1,0:T(8,128)(2,1)}), bf16[16,16,896]{2,1,0:T(8,128)(2,1)S(1)}, u32[]{:S(2)}, u32[]{:S(2)}) async-start(bf16[16,16,896]{2,1,0:T(8,128)(2,1)} %shard_map.90), calls=%async_computation.2 | async-start | bytes 917504 | tf_op jit(solution)/shard_map/all_to_all | solution.py:31
  126.6 2.4 %collective-permute-start.12 = (bf16[4,256,128]{2,1,0:T(8,128)(2,1)S(1)}, bf16[4,256,128]{2,1,0:T(8,128)(2,1)S(1)}, u32[]{:S(2)}, u32[]{:S(2)}) collective-permute-start(bf16[4,256,128]{2,1,0:T(8,128)(2,1)S(1)} %get-tuple-element.58), channel_id=1, source_target_pairs={{0,1},{1,0},{2,3},{3,2},{4,5},{5,4},{6,7},{7,6},{8,9},{9,8},{10,11... | collective-permute-start | bytes 786440 | tf_op jit(solution)/shard_map/ppermute | solution.py:62
  129.1 5.1 %collective-permute-start.13 = (bf16[4,256,128]{2,1,0:T(8,128)(2,1)S(1)}, bf16[4,256,128]{2,1,0:T(8,128)(2,1)S(1)}, u32[]{:S(2)}, u32[]{:S(2)}) collective-permute-start(bf16[4,256,128]{2,1,0:T(8,128)(2,1)S(1)} %get-tuple-element.57.own), channel_id=1, source_target_pairs={{0,256},{1,257},{2,258},{3,259},{4,260},{5,261},{6,262},{7,263},{8... | collective-permute-start | bytes 786440 | tf_op jit(solution)/shard_map/ppermute | solution.py:62
  134.2 3.2 %collective-permute-start.14 = (bf16[4,256,128]{2,1,0:T(8,128)(2,1)S(1)}, bf16[4,256,128]{2,1,0:T(8,128)(2,1)S(1)}, u32[]{:S(2)}, u32[]{:S(2)}) collective-permute-start(bf16[4,256,128]{2,1,0:T(8,128)(2,1)S(1)} %get-tuple-element.58), channel_id=1, source_target_pairs={{0,257},{1,256},{2,259},{3,258},{4,261},{5,260},{6,263},{7,262},{8... | collective-permute-start | bytes 786440 | tf_op jit(solution)/shard_map/ppermute | solution.py:62
  137.4 3.3 %collective-permute-done.13.mirrored = bf16[4,256,128]{2,1,0:T(8,128)(2,1)S(1)} collective-permute-done((bf16[4,256,128]{2,1,0:T(8,128)(2,1)S(1)}, bf16[4,256,128]{2,1,0:T(8,128)(2,1)S(1)}, u32[]{:S(2)}, u32[]{:S(2)}) %collective-permute-start.13) | collective-permute-done | bytes 262176 | tf_op jit(solution)/shard_map/ppermute | solution.py:62
  140.7 4.2 %collective-permute-done.14.opposite = bf16[4,256,128]{2,1,0:T(8,128)(2,1)S(1)} collective-permute-done((bf16[4,256,128]{2,1,0:T(8,128)(2,1)S(1)}, bf16[4,256,128]{2,1,0:T(8,128)(2,1)S(1)}, u32[]{:S(2)}, u32[]{:S(2)}) %collective-permute-start.14) | collective-permute-done | bytes 262176 | tf_op jit(solution)/shard_map/ppermute | solution.py:62
  145.9 1.9 shard_map.91
  147.9 30.3 %all_to_all.31 = bf16[16,16,896]{2,1,0:T(8,128)(2,1)S(1)} all-to-all(bf16[16,16,896]{2,1,0:T(8,128)(2,1)S(1)} %get-tuple-element.51), channel_id=1, replica_groups={{0,2,4,6,8,10,12,14,16,18,20,22,24,26,28,30},{1,3,5,7,9,11,13,15,17,19,..., dimensions={0} | all-to-all | bytes 917504 | tf_op jit(solution)/shard_map/all_to_all | solution.py:31
  178.4 14.9 %all_to_all.32.cotans = bf16[4,448,256]{2,1,0:T(8,128)(2,1)S(1)} all-to-all(bf16[4,448,256]{2,1,0:T(8,128)(2,1)S(1)} %shard_map.92), channel_id=1, replica_groups={{0,1,256,257},{2,3,258,259},{4,5,260,261},{6,7,262,263},{8,9,264,265},{..., dimensions={0} | all-to-all | bytes 1835008 | tf_op jit(solution)/shard_map/all_to_all | solution.py:31
  194.5 14.1 %all_to_all.33 = bf16[4,448,128]{2,1,0:T(8,128)(2,1)S(1)} all-to-all(bf16[4,448,128]{2,1,0:T(8,128)(2,1)S(1)} %shard_map.93), channel_id=1, replica_groups={{0,2,4,6},{1,3,5,7},{8,10,12,14},{9,11,13,15},{16,18,20,22},{17,19,21,2..., dimensions={0} | all-to-all | bytes 917504 | tf_op jit(solution)/shard_map/all_to_all | solution.py:31
  (32 shorter events, 7.5 us)
Async XLA Ops:
  0.6 23.0 %copy-start.2 = (bf16[1,128,3584]{2,1,0:T(8,128)(2,1)S(1)}, bf16[1,128,3584]{2,1,0:T(8,128)(2,1)}, u32[]{:S(2)}) copy-start(bf16[1,128,3584]{2,1,0:T(8,128)(2,1)} %param.9) | copy-start | bytes 2752516
  0.6 66.5 %collective-permute-start = (bf16[3584,128]{1,0:T(8,128)(2,1)}, bf16[3584,128]{1,0:T(8,128)(2,1)S(1)}, u32[]{:S(2)}, u32[]{:S(2)}) collective-permute-start(bf16[3584,128]{1,0:T(8,128)(2,1)} %bitcast.23), channel_id=1, source_target_pairs={{0,1},{1,0},{2,3},{3,2},{4,5},{5,4},{6,7},{7,6},{8,9},{9,8},{10,11... | collective-permute-start | bytes 2752520 | tf_op jit(solution)/shard_map/ppermute | solution.py:47
  8.6 58.6 %collective-permute-start.1 = (bf16[3584,128]{1,0:T(8,128)(2,1)}, bf16[3584,128]{1,0:T(8,128)(2,1)S(1)}, u32[]{:S(2)}, u32[]{:S(2)}) collective-permute-start(bf16[3584,128]{1,0:T(8,128)(2,1)} %bitcast.26), channel_id=1, source_target_pairs={{0,1},{1,0},{2,3},{3,2},{4,5},{5,4},{6,7},{7,6},{8,9},{9,8},{10,11... | collective-permute-start | bytes 2752520 | tf_op jit(solution)/shard_map/ppermute | solution.py:47
  10.6 1.2 copy-start.3
  13.4 53.7 %collective-permute-start.2 = (bf16[896,128]{1,0:T(8,128)(2,1)}, bf16[896,128]{1,0:T(8,128)(2,1)}, u32[]{:S(2)}, u32[]{:S(2)}) collective-permute-start(bf16[896,128]{1,0:T(8,128)(2,1)} %get-tuple-element.37), channel_id=1, source_target_pairs={{0,2},{1,3},{2,0},{3,1},{4,6},{5,7},{6,4},{7,5},{8,10},{9,11},{10,... | collective-permute-start | bytes 688136 | tf_op jit(solution)/shard_map/ppermute | solution.py:52
  15.3 51.8 %collective-permute-start.3 = (bf16[896,128]{1,0:T(8,128)(2,1)S(1)}, bf16[896,128]{1,0:T(8,128)(2,1)}, u32[]{:S(2)}, u32[]{:S(2)}) collective-permute-start(bf16[896,128]{1,0:T(8,128)(2,1)S(1)} %get-tuple-element.38), channel_id=1, source_target_pairs={{0,4},{1,5},{2,6},{3,7},{4,0},{5,1},{6,2},{7,3},{8,12},{9,13},{10,... | collective-permute-start | bytes 688136 | tf_op jit(solution)/shard_map/ppermute | solution.py:52
  18.6 48.6 %collective-permute-start.4 = (bf16[896,128]{1,0:T(8,128)(2,1)S(1)}, bf16[896,128]{1,0:T(8,128)(2,1)}, u32[]{:S(2)}, u32[]{:S(2)}) collective-permute-start(bf16[896,128]{1,0:T(8,128)(2,1)S(1)} %get-tuple-element.39), channel_id=1, source_target_pairs={{0,6},{1,7},{2,4},{3,5},{4,2},{5,3},{6,0},{7,1},{8,14},{9,15},{10,... | collective-permute-start | bytes 688136 | tf_op jit(solution)/shard_map/ppermute | solution.py:52
  23.6 0.7 copy-start.5
  23.6 0.7 copy-start.4
  67.2 11.5 %collective-permute-start.5 = (bf16[256,896]{1,0:T(8,128)(2,1)S(1)}, bf16[256,896]{1,0:T(8,128)(2,1)S(1)}, u32[]{:S(2)}, u32[]{:S(2)}) collective-permute-start(bf16[256,896]{1,0:T(8,128)(2,1)S(1)} %bitcast.35), channel_id=1, source_target_pairs={{2,0},{3,1},{4,2},{5,3},{6,4},{7,5},{10,8},{11,9},{12,10},{13,11},... | collective-permute-start | bytes 1376264 | tf_op jit(solution)/shard_map/ppermute | solution.py:42
  68.5 11.5 %collective-permute-start.7 = (bf16[256,896]{1,0:T(8,128)(2,1)S(1)}, bf16[256,896]{1,0:T(8,128)(2,1)S(1)}, u32[]{:S(2)}, u32[]{:S(2)}) collective-permute-start(bf16[256,896]{1,0:T(8,128)(2,1)S(1)} %bitcast.36), channel_id=1, source_target_pairs={{0,2},{1,3},{2,4},{3,5},{4,6},{5,7},{8,10},{9,11},{10,12},{11,13},... | collective-permute-start | bytes 1376264 | tf_op jit(solution)/shard_map/ppermute | solution.py:42
  78.7 10.7 %collective-permute-start.6 = (bf16[256,896]{1,0:T(8,128)(2,1)S(1)}, bf16[256,896]{1,0:T(8,128)(2,1)S(1)}, u32[]{:S(2)}, u32[]{:S(2)}) collective-permute-start(bf16[256,896]{1,0:T(8,128)(2,1)S(1)} %collective-permute-done.5.up1), channel_id=1, source_target_pairs={{2,0},{3,1},{4,2},{5,3},{10,8},{11,9},{12,10},{13,11},{18,16},{19,... | collective-permute-start | bytes 1376264 | tf_op jit(solution)/shard_map/ppermute | solution.py:42
  80.0 10.7 %collective-permute-start.8 = (bf16[256,896]{1,0:T(8,128)(2,1)S(1)}, bf16[256,896]{1,0:T(8,128)(2,1)S(1)}, u32[]{:S(2)}, u32[]{:S(2)}) collective-permute-start(bf16[256,896]{1,0:T(8,128)(2,1)S(1)} %collective-permute-done.7.down1), channel_id=1, source_target_pairs={{2,4},{3,5},{4,6},{5,7},{10,12},{11,13},{12,14},{13,15},{18,20},{1... | collective-permute-start | bytes 1376264 | tf_op jit(solution)/shard_map/ppermute | solution.py:42
  80.7 10.7 %copy-start = (bf16[1,3584,128]{2,1,0:T(8,128)(2,1)S(1)}, bf16[1,3584,128]{2,1,0:T(8,128)(2,1)}, u32[]{:S(2)}) copy-start(bf16[1,3584,128]{2,1,0:T(8,128)(2,1)} %param.13) | copy-start | bytes 2752516
  80.7 10.7 %copy-start.1 = (bf16[1,3584,128]{2,1,0:T(8,128)(2,1)S(1)}, bf16[1,3584,128]{2,1,0:T(8,128)(2,1)}, u32[]{:S(2)}) copy-start(bf16[1,3584,128]{2,1,0:T(8,128)(2,1)} %param.14) | copy-start | bytes 2752516
  82.1 20.4 %collective-permute-start.11 = (bf16[4,896,128]{2,1,0:T(8,128)(2,1)S(1)}, bf16[4,896,128]{2,1,0:T(8,128)(2,1)S(1)}, u32[]{:S(2)}, u32[]{:S(2)}) collective-permute-start(bf16[4,896,128]{2,1,0:T(8,128)(2,1)S(1)} %pad_maximum_fusion.down), channel_id=1, source_target_pairs={{0,1},{1,0},{2,3},{3,2},{4,5},{5,4},{6,7},{7,6},{8,9},{9,8},{10,11... | collective-permute-start | bytes 2752520 | tf_op jit(solution)/shard_map/ppermute | solution.py:47
  89.4 10.4 %collective-permute-start.9 = (bf16[256,896]{1,0:T(8,128)(2,1)S(1)}, bf16[256,896]{1,0:T(8,128)(2,1)S(1)}, u32[]{:S(2)}, u32[]{:S(2)}) collective-permute-start(bf16[256,896]{1,0:T(8,128)(2,1)S(1)} %collective-permute-done.6.up2), channel_id=1, source_target_pairs={{2,0},{3,1},{10,8},{11,9},{18,16},{19,17},{26,24},{27,25},{34,32},... | collective-permute-start | bytes 1376264 | tf_op jit(solution)/shard_map/ppermute | solution.py:42
  90.7 9.1 %collective-permute-start.10 = (bf16[256,896]{1,0:T(8,128)(2,1)S(1)}, bf16[256,896]{1,0:T(8,128)(2,1)S(1)}, u32[]{:S(2)}, u32[]{:S(2)}) collective-permute-start(bf16[256,896]{1,0:T(8,128)(2,1)S(1)} %collective-permute-done.8.down2), channel_id=1, source_target_pairs={{4,6},{5,7},{12,14},{13,15},{20,22},{21,23},{28,30},{29,31},{36,38... | collective-permute-start | bytes 1376264 | tf_op jit(solution)/shard_map/ppermute | solution.py:42
  119.5 26.4 %all-to-all-start.2 = ((bf16[16,16,896]{2,1,0:T(8,128)(2,1)}), bf16[16,16,896]{2,1,0:T(8,128)(2,1)S(1)}, u32[]{:S(2)}, u32[]{:S(2)}) async-start(bf16[16,16,896]{2,1,0:T(8,128)(2,1)} %shard_map.90), calls=%async_computation.2 | async-start | bytes 917504 | tf_op jit(solution)/shard_map/all_to_all | solution.py:31
  126.6 10.8 %collective-permute-start.12 = (bf16[4,256,128]{2,1,0:T(8,128)(2,1)S(1)}, bf16[4,256,128]{2,1,0:T(8,128)(2,1)S(1)}, u32[]{:S(2)}, u32[]{:S(2)}) collective-permute-start(bf16[4,256,128]{2,1,0:T(8,128)(2,1)S(1)} %get-tuple-element.58), channel_id=1, source_target_pairs={{0,1},{1,0},{2,3},{3,2},{4,5},{5,4},{6,7},{7,6},{8,9},{9,8},{10,11... | collective-permute-start | bytes 786440 | tf_op jit(solution)/shard_map/ppermute | solution.py:62
  129.1 16.9 %copy-start.6 = (f32[1,128]{1,0:T(1,128)S(1)}, f32[1,128]{1,0:T(1,128)}, u32[]{:S(2)}) copy-start(f32[1,128]{1,0:T(1,128)} %loss_ref.1) | copy-start | bytes 1540
  129.1 11.6 %collective-permute-start.13 = (bf16[4,256,128]{2,1,0:T(8,128)(2,1)S(1)}, bf16[4,256,128]{2,1,0:T(8,128)(2,1)S(1)}, u32[]{:S(2)}, u32[]{:S(2)}) collective-permute-start(bf16[4,256,128]{2,1,0:T(8,128)(2,1)S(1)} %get-tuple-element.57.own), channel_id=1, source_target_pairs={{0,256},{1,257},{2,258},{3,259},{4,260},{5,261},{6,262},{7,263},{8... | collective-permute-start | bytes 786440 | tf_op jit(solution)/shard_map/ppermute | solution.py:62
  134.2 10.7 %collective-permute-start.14 = (bf16[4,256,128]{2,1,0:T(8,128)(2,1)S(1)}, bf16[4,256,128]{2,1,0:T(8,128)(2,1)S(1)}, u32[]{:S(2)}, u32[]{:S(2)}) collective-permute-start(bf16[4,256,128]{2,1,0:T(8,128)(2,1)S(1)} %get-tuple-element.58), channel_id=1, source_target_pairs={{0,257},{1,256},{2,259},{3,258},{4,261},{5,260},{6,263},{7,262},{8... | collective-permute-start | bytes 786440 | tf_op jit(solution)/shard_map/ppermute | solution.py:62

commit v5 on v4

--- a/solution.py
+++ b/solution.py
@@ -75,16 +75,17 @@
     return lax.dot_general(a, b, (dims, ((), ())), preferred_element_type=F32)
 
 
-def kernel_call(body, out_shape, flops, moved, scalars=0, space=pltpu.VMEM, **kwargs):
+def kernel_call(body, out_shape, flops, moved, scalars=0, left=0, vmem=VMEM_LIMIT, **kwargs):
     def call(*operands):
         specs = [pl.BlockSpec(memory_space=pltpu.SMEM)] * scalars
-        specs += [pl.BlockSpec(memory_space=space)] * (len(operands) - scalars)
+        specs += [pl.BlockSpec(memory_space=pltpu.VMEM)] * (len(operands) - scalars - left)
+        specs += [pl.BlockSpec(memory_space=pl.ANY)] * left
         return pl.pallas_call(
             body,
             out_shape=out_shape,
             in_specs=specs,
             out_specs=jax.tree.map(lambda _: pl.BlockSpec(memory_space=pltpu.VMEM), out_shape),
-            compiler_params=pltpu.CompilerParams(vmem_limit_bytes=VMEM_LIMIT),
+            compiler_params=pltpu.CompilerParams(vmem_limit_bytes=vmem),
             cost_estimate=pl.CostEstimate(flops=flops, bytes_accessed=moved, transcendentals=0),
             **kwargs,
         )(*operands)
@@ -96,8 +97,13 @@
     return (place_ref[0] & (SPLIT - 1)) >> 1
 
 
-def relay_kernel(place_ref, w_ref, *rest):
-    outs, turned = rest[:-1], rest[-1]
+def relay_kernel(place_ref, w_ref, gate_ref, up_ref, *rest):
+    *outs, pair_ref, turned, sems = rest
+    copies = [
+        pltpu.make_async_copy(a, pair_ref.at[n], sems.at[n]) for n, a in enumerate((gate_ref, up_ref))
+    ]
+    for copy in copies:
+        copy.start()
     quad = quad_of(place_ref)
     turned[...] = w_ref[...].T
     eighth = outs[0].shape[0] // 2
@@ -105,6 +111,8 @@
         for h in range(2):
             start = pl.multiple_of((h * QUADS + (quad ^ d)) * eighth, 16)
             out[h * eighth : (h + 1) * eighth, :] = turned[pl.ds(start, eighth), :]
+    for copy in copies:
+        copy.wait()
 
 
 def gather_kernel(window, ids, gates, tokens, picked_ref, spread_ref, ids_ref, gates_ref, tok_ref, sems):
@@ -137,7 +145,7 @@
             picked_ref[k * QUADS + q] = rows[k * CAP : (k + 1) * CAP]
 
 
-def acts_kernel(place_ref, here, up1, up2, down1, down2, wg, wu, wg2, wu2, acts_ref):
+def acts_kernel(place_ref, here, up1, up2, down1, down2, wg, wu, others, acts_ref):
     quad = quad_of(place_ref)
     quarter, units = here.shape[1], wg.shape[1]
     parts = ((here, None, 0), (up1, None, 1), (down1, None, 3), (up2, down2, 2))
@@ -145,21 +153,21 @@
     for first, second, distance in parts:
         start = pl.multiple_of(((quad + distance) & (QUADS - 1)) * quarter, quarter)
         rows = first[...] if second is None else first[...] + second[...]
-        for n, weight in enumerate((wg, wu, wg2, wu2)):
+        for n, weight in enumerate((wg, wu, others.at[0], others.at[1])):
             part = dot(rows, weight[pl.ds(start, quarter), :])
             totals[n] = part if totals[n] is None else totals[n] + part
     for n in range(4):
         acts_ref[:, n * units : (n + 1) * units] = totals[n]
 
 
-def hidden_kernel(place_ref, acts, up3, down3, wg, wu, wg2, wu2, hidden_ref):
+def hidden_kernel(place_ref, acts, up3, down3, wg, wu, others, hidden_ref):
     quad = quad_of(place_ref)
     quarter, units = up3.shape[1], wg.shape[1]
     last = jnp.where(quad * 2 < QUADS, QUADS - 1, 0)
     start = pl.multiple_of(last * quarter, quarter)
     rows = up3[...] + down3[...]
     both = []
-    for n, weight in enumerate((wg, wu, wg2, wu2)):
+    for n, weight in enumerate((wg, wu, others.at[0], others.at[1])):
         both.append(acts[:, n * units : (n + 1) * units] + dot(rows, weight[pl.ds(start, quarter), :]))
     for side in range(2):
         gate, up = both[2 * side], both[2 * side + 1]
@@ -236,13 +244,14 @@
     blocks = count // 2
     held = blocks * CAP
 
-    gate_other = neighbour(w_gate[0])
-    up_other = neighbour(w_up[0])
-
-    down = kernel_call(
-        relay_kernel, (jax.ShapeDtypeStruct((quarter, units), BF16),) * QUADS,
-        0, 4 * width * units, 1, scratch_shapes=[pltpu.VMEM((width, units), BF16)],
-    )(place, w_down[0])
+    *down, gate_up = kernel_call(
+        relay_kernel,
+        (jax.ShapeDtypeStruct((quarter, units), BF16),) * QUADS
+        + (jax.ShapeDtypeStruct((2, width, units), BF16),),
+        0, 12 * width * units, 1, left=2, vmem=3 * VMEM_LIMIT,
+        scratch_shapes=[pltpu.VMEM((width, units), BF16), pltpu.SemaphoreType.DMA((2,))],
+    )(place, w_down[0], w_gate[0], w_up[0])
+    others = neighbour(gate_up)
     down = [down[0]] + [swap(down[d], d) for d in range(1, QUADS)]
 
     picked, spread = kernel_call(
@@ -251,7 +260,7 @@
             jax.ShapeDtypeStruct((window * QUADS, CAP, quarter), BF16),
             jax.ShapeDtypeStruct((window * CAP, tok_count), F32),
         ),
-        2 * window * CAP * tok_count * width, 3 * tok_count * width, space=pl.ANY,
+        2 * window * CAP * tok_count * width, 3 * tok_count * width, left=3,
         scratch_shapes=[
             pltpu.VMEM((choices, tok_count), jnp.int32),
             pltpu.VMEM((choices, tok_count), F32),
@@ -262,14 +271,14 @@
     once = lax.optimization_barrier(jnp.int32(1))
     rows = lax.cond(once > 0, lambda b: exchange(b, "expert", by_column), lambda b: b, picked)
     rows = rows.reshape(held, quarter)
-    rows, gate_other, up_other, *down = lax.optimization_barrier((rows, gate_other, up_other, *down))
+    rows, others, *down = lax.optimization_barrier((rows, others, *down))
     down = jnp.stack(down)
     down_other = neighbour(down)
     ups, downs = [rows], [rows]
     for turn in range(1, QUADS):
         ups.append(pass_on(ups[-1], 1, turn))
         downs.append(pass_on(downs[-1], -1, turn))
-    weights = (w_gate[0], w_up[0], gate_other, up_other)
+    weights = (w_gate[0], w_up[0], others)
     acts = kernel_call(
         acts_kernel, jax.ShapeDtypeStruct((held, 4 * units), F32),
         8 * held * width * units, 8 * width * units, 1,

time: 210 us -> 210 us (level)
  the two profiles are of different devices: /device:TPU:2 before, /device:TPU:4 now
where the time goes in v5:
time: 210 us; the launch traced here: 209 us
  blocking collectives  120 us (57%)
  starting transfers between devices  44.4 us (21%)
  waiting for transfers between devices  24.3 us (12%)
  Pallas kernels  16 us (8%)
    all_to_all x5, blocking collectives, exchange(): lax.all_to_all(blocks, axis, 0, 0, axis_index_groups=groups, tiled=True)  120 us
    pallas_call x8, Pallas kernels, call(): pl.pallas_call(body, out_shape=out_shape, in_specs=specs, out_specs=jax.t...  16 us
    ppermute x6, waiting for transfers between devices, pass_on(): return lax.ppermute(block, 'expert', route)  15.3 us
    ppermute x3, starting transfers between devices, swap(): lax.ppermute(block, 'expert', [(i, i ^ 2 * distance) for i in range(count)])  10.9 us
    ppermute x3, starting transfers between devices, cross(): return lax.ppermute(block, ('pipe', 'expert'), route)  10.7 us
    ppermute x6, starting transfers between devices, pass_on(): return lax.ppermute(block, 'expert', route)  9.81 us
    ppermute x3, waiting for transfers between devices, cross(): return lax.ppermute(block, ('pipe', 'expert'), route)  7.79 us
    all_to_all x1, starting transfers between devices, exchange(): lax.all_to_all(blocks, axis, 0, 0, axis_index_groups=groups, tiled=True)  6.96 us
  transfers between devices with their start and end apart: 15, of which 8 were waited for; matrix products, arithmetic and copies ran while one was open for 1% of the time, Pallas kernels for 3%

profile of v5, /device:TPU:4, one launch (start us, length us, event | category | flops | bytes accessed | tf_op | source)
XLA Modules:
  0.0 208.7 jit_solution(3341733289576947683)
XLA Ops:
  1.3 4.2 %shard_map.87 = (bf16[896,128]{1,0:T(8,128)(2,1)}, bf16[896,128]{1,0:T(8,128)(2,1)}, bf16[896,128]{1,0:T(8,128)(2,1)}, bf16[896,128]{1,0:T(8,128)(2,1)}, bf16[2,3584,128]{2,1,0:T(8,128)(2,1)}) custom-call(s32[2]{0:T(128)} %pad_add_fusion.place_ref, bf16[128,3584]{1,0:T(8,128)(2,1)} %bitcast.37, bf16[3584,128]{1,0:T(8,128)(2,1)} %bitcast.23, ...), custom_call_target="tpu_custom_call" | custom-call | bytes 5505024 | tf_op jit(solution)/shard_map/pallas_call | solution.py:83
  5.5 3.2 %collective-permute-start = (bf16[2,3584,128]{2,1,0:T(8,128)(2,1)}, bf16[2,3584,128]{2,1,0:T(8,128)(2,1)}, u32[]{:S(2)}, u32[]{:S(2)}) collective-permute-start(bf16[2,3584,128]{2,1,0:T(8,128)(2,1)} %get-tuple-element.36), channel_id=1, source_target_pairs={{0,1},{1,0},{2,3},{3,2},{4,5},{5,4},{6,7},{7,6},{8,9},{9,8},{10,11... | collective-permute-start | bytes 5505032 | tf_op jit(solution)/shard_map/ppermute | solution.py:47
  8.8 3.8 %collective-permute-start.1 = (bf16[896,128]{1,0:T(8,128)(2,1)}, bf16[896,128]{1,0:T(8,128)(2,1)S(1)}, u32[]{:S(2)}, u32[]{:S(2)}) collective-permute-start(bf16[896,128]{1,0:T(8,128)(2,1)} %get-tuple-element.38), channel_id=1, source_target_pairs={{0,2},{1,3},{2,0},{3,1},{4,6},{5,7},{6,4},{7,5},{8,10},{9,11},{10,... | collective-permute-start | bytes 688136 | tf_op jit(solution)/shard_map/ppermute | solution.py:52
  12.6 5.2 %collective-permute-start.2 = (bf16[896,128]{1,0:T(8,128)(2,1)}, bf16[896,128]{1,0:T(8,128)(2,1)S(1)}, u32[]{:S(2)}, u32[]{:S(2)}) collective-permute-start(bf16[896,128]{1,0:T(8,128)(2,1)} %get-tuple-element.39), channel_id=1, source_target_pairs={{0,4},{1,5},{2,6},{3,7},{4,0},{5,1},{6,2},{7,3},{8,12},{9,13},{10,... | collective-permute-start | bytes 688136 | tf_op jit(solution)/shard_map/ppermute | solution.py:52
  17.8 1.9 collective-permute-start.3
  20.5 46.4 %conditional.1 = (bf16[16,16,896]{2,1,0:T(8,128)(2,1)S(1)}) conditional(s32[]{:T(128)} %convert_element_type.3, bf16[16,16,896]{2,1,0:T(8,128)(2,1)S(1)} %get-tuple-element.35, bf16[16,16,896]{2,1,0:T(8,128)(2,1)S(1)} %get-tuple-element.35), branch_computations={%region_0.1_spmd, %region_1.2_spmd} | conditional | bytes 917512 | solution.py:272
  20.5 46.4 %all_to_all.29 = bf16[16,16,896]{2,1,0:T(8,128)(2,1)S(1)} all-to-all(bf16[16,16,896]{2,1,0:T(8,128)(2,1)S(1)} %param.1), channel_id=1, replica_groups={{0,2,4,6,8,10,12,14,16,18,20,22,24,26,28,30},{1,3,5,7,9,11,13,15,17,19,..., dimensions={0} | all-to-all | bytes 917504 | tf_op jit(solution)/shard_map/cond/branch_1_fun/all_to_all | solution.py:31
  66.9 1.3 collective-permute-start.4
  68.2 4.6 %collective-permute-start.6 = (bf16[256,896]{1,0:T(8,128)(2,1)S(1)}, bf16[256,896]{1,0:T(8,128)(2,1)S(1)}, u32[]{:S(2)}, u32[]{:S(2)}) collective-permute-start(bf16[256,896]{1,0:T(8,128)(2,1)S(1)} %bitcast.34), channel_id=1, source_target_pairs={{0,2},{1,3},{2,4},{3,5},{4,6},{5,7},{8,10},{9,11},{10,12},{11,13},... | collective-permute-start | bytes 1376264 | tf_op jit(solution)/shard_map/ppermute | solution.py:42
  72.8 5.7 %collective-permute-done.4.up1 = bf16[256,896]{1,0:T(8,128)(2,1)S(1)} collective-permute-done((bf16[256,896]{1,0:T(8,128)(2,1)S(1)}, bf16[256,896]{1,0:T(8,128)(2,1)S(1)}, u32[]{:S(2)}, u32[]{:S(2)}) %collective-permute-start.4) | collective-permute-done | bytes 458784 | tf_op jit(solution)/shard_map/ppermute | solution.py:42
  78.5 1.3 collective-permute-start.5
  80.5 1.1 pad_maximum_fusion.down
  81.6 2.7 %collective-permute-start.10 = (bf16[4,896,128]{2,1,0:T(8,128)(2,1)S(1)}, bf16[4,896,128]{2,1,0:T(8,128)(2,1)S(1)}, u32[]{:S(2)}, u32[]{:S(2)}) collective-permute-start(bf16[4,896,128]{2,1,0:T(8,128)(2,1)S(1)} %pad_maximum_fusion.down), channel_id=1, source_target_pairs={{0,1},{1,0},{2,3},{3,2},{4,5},{5,4},{6,7},{7,6},{8,9},{9,8},{10,11... | collective-permute-start | bytes 2752520 | tf_op jit(solution)/shard_map/ppermute | solution.py:47
  84.3 4.9 %collective-permute-done.5.up2 = bf16[256,896]{1,0:T(8,128)(2,1)S(1)} collective-permute-done((bf16[256,896]{1,0:T(8,128)(2,1)S(1)}, bf16[256,896]{1,0:T(8,128)(2,1)S(1)}, u32[]{:S(2)}, u32[]{:S(2)}) %collective-permute-start.5) | collective-permute-done | bytes 458784 | tf_op jit(solution)/shard_map/ppermute | solution.py:42
  89.2 1.3 collective-permute-start.8
  91.2 3.6 %shard_map.88.acts = f32[256,512]{1,0:T(8,128)S(1)} custom-call(s32[2]{0:T(128)S(1)} %copy-done.3, bf16[256,896]{1,0:T(8,128)(2,1)S(1)} %bitcast.35, bf16[256,896]{1,0:T(8,128)(2,1)S(1)} %collective-permute-done.4.up1, bf16[256,896]{1,0:T(8,128)(2,1)S(1)} %collective-permute-done.5.up2, bf16[256,896]{1,0:T(8,128)(2,1)S(1)} %collective-permute-done.6.down1, ...), custom_call_target="tpu_custom_call" | custom-call | flops 939524096 | bytes 3670016 | tf_op jit(solution)/shard_map/pallas_call | solution.py:83
  94.9 4.7 %collective-permute-done.8.up3 = bf16[256,896]{1,0:T(8,128)(2,1)S(1)} collective-permute-done((bf16[256,896]{1,0:T(8,128)(2,1)S(1)}, bf16[256,896]{1,0:T(8,128)(2,1)S(1)}, u32[]{:S(2)}, u32[]{:S(2)}) %collective-permute-start.8) | collective-permute-done | bytes 458784 | tf_op jit(solution)/shard_map/ppermute | solution.py:42
  99.6 2.2 %shard_map.89 = bf16[4,256,256]{2,1,0:T(8,128)(2,1)S(1)} custom-call(s32[2]{0:T(128)S(1)} %copy-done.3, f32[256,512]{1,0:T(8,128)S(1)} %shard_map.88.acts, bf16[256,896]{1,0:T(8,128)(2,1)S(1)} %collective-permute-done.8.up3, bf16[256,896]{1,0:T(8,128)(2,1)S(1)} %collective-permute-done.9.down3, bf16[3584,128]{1,0:T(8,128)(2,1)S(1)} %bitcast.25, ...), custom_call_target="tpu_custom_call" | custom-call | flops 234881024 | bytes 917504 | tf_op jit(solution)/shard_map/pallas_call | solution.py:83
  102.1 15.0 %all_to_all.30.hidden = bf16[4,256,256]{2,1,0:T(8,128)(2,1)S(1)} all-to-all(bf16[4,256,256]{2,1,0:T(8,128)(2,1)S(1)} %shard_map.89), channel_id=1, replica_groups={{0,2,4,6},{1,3,5,7},{8,10,12,14},{9,11,13,15},{16,18,20,22},{17,19,21,2..., dimensions={0} | all-to-all | bytes 1048576 | tf_op jit(solution)/shard_map/all_to_all | solution.py:31
  117.0 2.0 shard_map.90
  119.1 7.0 %all-to-all-start.2 = ((bf16[16,16,896]{2,1,0:T(8,128)(2,1)}), bf16[16,16,896]{2,1,0:T(8,128)(2,1)S(1)}, u32[]{:S(2)}, u32[]{:S(2)}) async-start(bf16[16,16,896]{2,1,0:T(8,128)(2,1)} %shard_map.90), calls=%async_computation.2 | async-start | bytes 917504 | tf_op jit(solution)/shard_map/all_to_all | solution.py:31
  126.1 2.7 %collective-permute-start.11 = (bf16[4,256,128]{2,1,0:T(8,128)(2,1)S(1)}, bf16[4,256,128]{2,1,0:T(8,128)(2,1)S(1)}, u32[]{:S(2)}, u32[]{:S(2)}) collective-permute-start(bf16[4,256,128]{2,1,0:T(8,128)(2,1)S(1)} %get-tuple-element.58), channel_id=1, source_target_pairs={{0,1},{1,0},{2,3},{3,2},{4,5},{5,4},{6,7},{7,6},{8,9},{9,8},{10,11... | collective-permute-start | bytes 786440 | tf_op jit(solution)/shard_map/ppermute | solution.py:62
  128.9 5.1 %collective-permute-start.12 = (bf16[4,256,128]{2,1,0:T(8,128)(2,1)S(1)}, bf16[4,256,128]{2,1,0:T(8,128)(2,1)S(1)}, u32[]{:S(2)}, u32[]{:S(2)}) collective-permute-start(bf16[4,256,128]{2,1,0:T(8,128)(2,1)S(1)} %get-tuple-element.57.own), channel_id=1, source_target_pairs={{0,256},{1,257},{2,258},{3,259},{4,260},{5,261},{6,262},{7,263},{8... | collective-permute-start | bytes 786440 | tf_op jit(solution)/shard_map/ppermute | solution.py:62
  134.0 2.9 %collective-permute-start.13 = (bf16[4,256,128]{2,1,0:T(8,128)(2,1)S(1)}, bf16[4,256,128]{2,1,0:T(8,128)(2,1)S(1)}, u32[]{:S(2)}, u32[]{:S(2)}) collective-permute-start(bf16[4,256,128]{2,1,0:T(8,128)(2,1)S(1)} %get-tuple-element.58), channel_id=1, source_target_pairs={{0,257},{1,256},{2,259},{3,258},{4,261},{5,260},{6,263},{7,262},{8... | collective-permute-start | bytes 786440 | tf_op jit(solution)/shard_map/ppermute | solution.py:62
  137.1 3.6 %collective-permute-done.12.mirrored = bf16[4,256,128]{2,1,0:T(8,128)(2,1)S(1)} collective-permute-done((bf16[4,256,128]{2,1,0:T(8,128)(2,1)S(1)}, bf16[4,256,128]{2,1,0:T(8,128)(2,1)S(1)}, u32[]{:S(2)}, u32[]{:S(2)}) %collective-permute-start.12) | collective-permute-done | bytes 262176 | tf_op jit(solution)/shard_map/ppermute | solution.py:62
  140.7 4.0 %collective-permute-done.13.opposite = bf16[4,256,128]{2,1,0:T(8,128)(2,1)S(1)} collective-permute-done((bf16[4,256,128]{2,1,0:T(8,128)(2,1)S(1)}, bf16[4,256,128]{2,1,0:T(8,128)(2,1)S(1)}, u32[]{:S(2)}, u32[]{:S(2)}) %collective-permute-start.13) | collective-permute-done | bytes 262176 | tf_op jit(solution)/shard_map/ppermute | solution.py:62
  145.6 1.9 shard_map.91
  147.5 31.2 %all_to_all.31 = bf16[16,16,896]{2,1,0:T(8,128)(2,1)S(1)} all-to-all(bf16[16,16,896]{2,1,0:T(8,128)(2,1)S(1)} %get-tuple-element.51), channel_id=1, replica_groups={{0,2,4,6,8,10,12,14,16,18,20,22,24,26,28,30},{1,3,5,7,9,11,13,15,17,19,..., dimensions={0} | all-to-all | bytes 917504 | tf_op jit(solution)/shard_map/all_to_all | solution.py:31
  178.9 13.8 %all_to_all.32.cotans = bf16[4,448,256]{2,1,0:T(8,128)(2,1)S(1)} all-to-all(bf16[4,448,256]{2,1,0:T(8,128)(2,1)S(1)} %shard_map.92), channel_id=1, replica_groups={{0,1,256,257},{2,3,258,259},{4,5,260,261},{6,7,262,263},{8,9,264,265},{..., dimensions={0} | all-to-all | bytes 1835008 | tf_op jit(solution)/shard_map/all_to_all | solution.py:31
  192.7 1.2 shard_map.93
  193.9 13.8 %all_to_all.33 = bf16[4,448,128]{2,1,0:T(8,128)(2,1)S(1)} all-to-all(bf16[4,448,128]{2,1,0:T(8,128)(2,1)S(1)} %shard_map.93), channel_id=1, replica_groups={{0,2,4,6},{1,3,5,7},{8,10,12,14},{9,11,13,15},{16,18,20,22},{17,19,21,2..., dimensions={0} | all-to-all | bytes 917504 | tf_op jit(solution)/shard_map/all_to_all | solution.py:31
  207.7 1.0 copy.9
  (32 shorter events, 4.5 us)
Async XLA Ops:
  0.6 19.1 %copy-start.4 = (s32[1,128,8]{1,2,0:T(8,128)S(1)}, s32[1,128,8]{1,2,0:T(8,128)}, u32[]{:S(2)}) copy-start(s32[1,128,8]{1,2,0:T(8,128)} %param.10) | copy-start | bytes 12292
  0.6 19.1 %copy-start.5 = (f32[1,128,8]{1,2,0:T(8,128)S(1)}, f32[1,128,8]{1,2,0:T(8,128)}, u32[]{:S(2)}) copy-start(f32[1,128,8]{1,2,0:T(8,128)} %param.11) | copy-start | bytes 12292
  0.6 19.1 %copy-start.2 = (bf16[1,128,3584]{2,1,0:T(8,128)(2,1)S(1)}, bf16[1,128,3584]{2,1,0:T(8,128)(2,1)}, u32[]{:S(2)}) copy-start(bf16[1,128,3584]{2,1,0:T(8,128)(2,1)} %param.9) | copy-start | bytes 2752516
  5.5 75.0 %copy-start.7 = (bf16[896,128]{1,0:T(8,128)(2,1)S(1)}, bf16[896,128]{1,0:T(8,128)(2,1)}, u32[]{:S(2)}) copy-start(bf16[896,128]{1,0:T(8,128)(2,1)} %get-tuple-element.43) | copy-start | bytes 688132
  5.5 61.4 %collective-permute-start = (bf16[2,3584,128]{2,1,0:T(8,128)(2,1)}, bf16[2,3584,128]{2,1,0:T(8,128)(2,1)}, u32[]{:S(2)}, u32[]{:S(2)}) collective-permute-start(bf16[2,3584,128]{2,1,0:T(8,128)(2,1)} %get-tuple-element.36), channel_id=1, source_target_pairs={{0,1},{1,0},{2,3},{3,2},{4,5},{5,4},{6,7},{7,6},{8,9},{9,8},{10,11... | collective-permute-start | bytes 5505032 | tf_op jit(solution)/shard_map/ppermute | solution.py:47
  8.8 58.1 %collective-permute-start.1 = (bf16[896,128]{1,0:T(8,128)(2,1)}, bf16[896,128]{1,0:T(8,128)(2,1)S(1)}, u32[]{:S(2)}, u32[]{:S(2)}) collective-permute-start(bf16[896,128]{1,0:T(8,128)(2,1)} %get-tuple-element.38), channel_id=1, source_target_pairs={{0,2},{1,3},{2,0},{3,1},{4,6},{5,7},{6,4},{7,5},{8,10},{9,11},{10,... | collective-permute-start | bytes 688136 | tf_op jit(solution)/shard_map/ppermute | solution.py:52
  12.6 54.3 %collective-permute-start.2 = (bf16[896,128]{1,0:T(8,128)(2,1)}, bf16[896,128]{1,0:T(8,128)(2,1)S(1)}, u32[]{:S(2)}, u32[]{:S(2)}) collective-permute-start(bf16[896,128]{1,0:T(8,128)(2,1)} %get-tuple-element.39), channel_id=1, source_target_pairs={{0,4},{1,5},{2,6},{3,7},{4,0},{5,1},{6,2},{7,3},{8,12},{9,13},{10,... | collective-permute-start | bytes 688136 | tf_op jit(solution)/shard_map/ppermute | solution.py:52
  17.8 49.1 %collective-permute-start.3 = (bf16[896,128]{1,0:T(8,128)(2,1)}, bf16[896,128]{1,0:T(8,128)(2,1)}, u32[]{:S(2)}, u32[]{:S(2)}) collective-permute-start(bf16[896,128]{1,0:T(8,128)(2,1)} %get-tuple-element.40), channel_id=1, source_target_pairs={{0,6},{1,7},{2,4},{3,5},{4,2},{5,3},{6,0},{7,1},{8,14},{9,15},{10,... | collective-permute-start | bytes 688136 | tf_op jit(solution)/shard_map/ppermute | solution.py:52
  20.5 70.7 %copy-start = (bf16[1,3584,128]{2,1,0:T(8,128)(2,1)S(1)}, bf16[1,3584,128]{2,1,0:T(8,128)(2,1)}, u32[]{:S(2)}) copy-start(bf16[1,3584,128]{2,1,0:T(8,128)(2,1)} %param.13) | copy-start | bytes 2752516
  20.5 70.7 %copy-start.1 = (bf16[1,3584,128]{2,1,0:T(8,128)(2,1)S(1)}, bf16[1,3584,128]{2,1,0:T(8,128)(2,1)}, u32[]{:S(2)}) copy-start(bf16[1,3584,128]{2,1,0:T(8,128)(2,1)} %param.14) | copy-start | bytes 2752516
  20.5 70.7 %copy-start.3 = (s32[2]{0:T(128)S(1)}, s32[2]{0:T(128)}, u32[]{:S(2)}) copy-start(s32[2]{0:T(128)} %pad_add_fusion.place_ref) | copy-start | bytes 28
  66.9 11.6 %collective-permute-start.4 = (bf16[256,896]{1,0:T(8,128)(2,1)S(1)}, bf16[256,896]{1,0:T(8,128)(2,1)S(1)}, u32[]{:S(2)}, u32[]{:S(2)}) collective-permute-start(bf16[256,896]{1,0:T(8,128)(2,1)S(1)} %bitcast.33), channel_id=1, source_target_pairs={{2,0},{3,1},{4,2},{5,3},{6,4},{7,5},{10,8},{11,9},{12,10},{13,11},... | collective-permute-start | bytes 1376264 | tf_op jit(solution)/shard_map/ppermute | solution.py:42
  68.2 11.6 %collective-permute-start.6 = (bf16[256,896]{1,0:T(8,128)(2,1)S(1)}, bf16[256,896]{1,0:T(8,128)(2,1)S(1)}, u32[]{:S(2)}, u32[]{:S(2)}) collective-permute-start(bf16[256,896]{1,0:T(8,128)(2,1)S(1)} %bitcast.34), channel_id=1, source_target_pairs={{0,2},{1,3},{2,4},{3,5},{4,6},{5,7},{8,10},{9,11},{10,12},{11,13},... | collective-permute-start | bytes 1376264 | tf_op jit(solution)/shard_map/ppermute | solution.py:42
  78.5 10.7 %collective-permute-start.5 = (bf16[256,896]{1,0:T(8,128)(2,1)S(1)}, bf16[256,896]{1,0:T(8,128)(2,1)S(1)}, u32[]{:S(2)}, u32[]{:S(2)}) collective-permute-start(bf16[256,896]{1,0:T(8,128)(2,1)S(1)} %collective-permute-done.4.up1), channel_id=1, source_target_pairs={{2,0},{3,1},{4,2},{5,3},{10,8},{11,9},{12,10},{13,11},{18,16},{19,... | collective-permute-start | bytes 1376264 | tf_op jit(solution)/shard_map/ppermute | solution.py:42
  79.8 10.7 %collective-permute-start.7 = (bf16[256,896]{1,0:T(8,128)(2,1)S(1)}, bf16[256,896]{1,0:T(8,128)(2,1)S(1)}, u32[]{:S(2)}, u32[]{:S(2)}) collective-permute-start(bf16[256,896]{1,0:T(8,128)(2,1)S(1)} %collective-permute-done.6.down1), channel_id=1, source_target_pairs={{2,4},{3,5},{4,6},{5,7},{10,12},{11,13},{12,14},{13,15},{18,20},{1... | collective-permute-start | bytes 1376264 | tf_op jit(solution)/shard_map/ppermute | solution.py:42
  81.6 20.5 %collective-permute-start.10 = (bf16[4,896,128]{2,1,0:T(8,128)(2,1)S(1)}, bf16[4,896,128]{2,1,0:T(8,128)(2,1)S(1)}, u32[]{:S(2)}, u32[]{:S(2)}) collective-permute-start(bf16[4,896,128]{2,1,0:T(8,128)(2,1)S(1)} %pad_maximum_fusion.down), channel_id=1, source_target_pairs={{0,1},{1,0},{2,3},{3,2},{4,5},{5,4},{6,7},{7,6},{8,9},{9,8},{10,11... | collective-permute-start | bytes 2752520 | tf_op jit(solution)/shard_map/ppermute | solution.py:47
  89.2 10.4 %collective-permute-start.8 = (bf16[256,896]{1,0:T(8,128)(2,1)S(1)}, bf16[256,896]{1,0:T(8,128)(2,1)S(1)}, u32[]{:S(2)}, u32[]{:S(2)}) collective-permute-start(bf16[256,896]{1,0:T(8,128)(2,1)S(1)} %collective-permute-done.5.up2), channel_id=1, source_target_pairs={{2,0},{3,1},{10,8},{11,9},{18,16},{19,17},{26,24},{27,25},{34,32},... | collective-permute-start | bytes 1376264 | tf_op jit(solution)/shard_map/ppermute | solution.py:42
  90.5 9.1 %collective-permute-start.9 = (bf16[256,896]{1,0:T(8,128)(2,1)S(1)}, bf16[256,896]{1,0:T(8,128)(2,1)S(1)}, u32[]{:S(2)}, u32[]{:S(2)}) collective-permute-start(bf16[256,896]{1,0:T(8,128)(2,1)S(1)} %collective-permute-done.7.down2), channel_id=1, source_target_pairs={{4,6},{5,7},{12,14},{13,15},{20,22},{21,23},{28,30},{29,31},{36,38... | collective-permute-start | bytes 1376264 | tf_op jit(solution)/shard_map/ppermute | solution.py:42
  117.0 28.5 %copy-start.6 = (f32[1,128]{1,0:T(1,128)S(1)}, f32[1,128]{1,0:T(1,128)}, u32[]{:S(2)}) copy-start(f32[1,128]{1,0:T(1,128)} %loss_ref.1) | copy-start | bytes 1540
  119.1 26.5 %all-to-all-start.2 = ((bf16[16,16,896]{2,1,0:T(8,128)(2,1)}), bf16[16,16,896]{2,1,0:T(8,128)(2,1)S(1)}, u32[]{:S(2)}, u32[]{:S(2)}) async-start(bf16[16,16,896]{2,1,0:T(8,128)(2,1)} %shard_map.90), calls=%async_computation.2 | async-start | bytes 917504 | tf_op jit(solution)/shard_map/all_to_all | solution.py:31
  126.1 11.0 %collective-permute-start.11 = (bf16[4,256,128]{2,1,0:T(8,128)(2,1)S(1)}, bf16[4,256,128]{2,1,0:T(8,128)(2,1)S(1)}, u32[]{:S(2)}, u32[]{:S(2)}) collective-permute-start(bf16[4,256,128]{2,1,0:T(8,128)(2,1)S(1)} %get-tuple-element.58), channel_id=1, source_target_pairs={{0,1},{1,0},{2,3},{3,2},{4,5},{5,4},{6,7},{7,6},{8,9},{9,8},{10,11... | collective-permute-start | bytes 786440 | tf_op jit(solution)/shard_map/ppermute | solution.py:62
  128.9 11.8 %collective-permute-start.12 = (bf16[4,256,128]{2,1,0:T(8,128)(2,1)S(1)}, bf16[4,256,128]{2,1,0:T(8,128)(2,1)S(1)}, u32[]{:S(2)}, u32[]{:S(2)}) collective-permute-start(bf16[4,256,128]{2,1,0:T(8,128)(2,1)S(1)} %get-tuple-element.57.own), channel_id=1, source_target_pairs={{0,256},{1,257},{2,258},{3,259},{4,260},{5,261},{6,262},{7,263},{8... | collective-permute-start | bytes 786440 | tf_op jit(solution)/shard_map/ppermute | solution.py:62
  134.0 10.7 %collective-permute-start.13 = (bf16[4,256,128]{2,1,0:T(8,128)(2,1)S(1)}, bf16[4,256,128]{2,1,0:T(8,128)(2,1)S(1)}, u32[]{:S(2)}, u32[]{:S(2)}) collective-permute-start(bf16[4,256,128]{2,1,0:T(8,128)(2,1)S(1)} %get-tuple-element.58), channel_id=1, source_target_pairs={{0,257},{1,256},{2,259},{3,258},{4,261},{5,260},{6,263},{7,262},{8... | collective-permute-start | bytes 786440 | tf_op jit(solution)/shard_map/ppermute | solution.py:62

commit v6 on v5

--- a/solution.py
+++ b/solution.py
@@ -219,7 +219,7 @@
 
 
 def grads_kernel(place_ref, cotans, own, across, mirrored, opposite, grads_ref):
-    mine = 2 * place_ref[1] + (place_ref[0] & 1)
+    mine = 2 * (place_ref[0] // SPLIT) + (place_ref[0] & 1)
     units = own.shape[2]
     total = None
     for flip, hidden in enumerate((own, across, mirrored, opposite)):
@@ -239,7 +239,7 @@
     quarter, eighth = width // QUADS, width // (2 * QUADS)
     place = lax.axis_index("expert")
     mirror = lax.axis_index("pipe") // (lax.axis_size("pipe") // 2)
-    place = jnp.stack([place, mirror])
+    place = (place % SPLIT + SPLIT * mirror).reshape(1)
     by_column, by_quad = columns(count), quads(count)
     blocks = count // 2
     held = blocks * CAP

time: 210 us -> 209 us (level)
  the two profiles are of different devices: /device:TPU:4 before, /device:TPU:2 now
where the time goes in v6:
time: 209 us; the launch traced here: 208 us
  blocking collectives  116 us (56%)
  starting transfers between devices  49 us (23%)
  waiting for transfers between devices  25.4 us (12%)
  Pallas kernels  15 us (7%)
    all_to_all x5, blocking collectives, exchange(): lax.all_to_all(blocks, axis, 0, 0, axis_index_groups=groups, tiled=True)  116 us
    pallas_call x8, Pallas kernels, call(): pl.pallas_call(body, out_shape=out_shape, in_specs=specs, out_specs=jax.t...  15 us
    ppermute x6, waiting for transfers between devices, pass_on(): return lax.ppermute(block, 'expert', route)  14.7 us
    ppermute x2, starting transfers between devices, neighbour(): return lax.ppermute(block, 'expert', [(i, i ^ 1) for i in range(count)])  11.3 us
    ppermute x3, starting transfers between devices, cross(): return lax.ppermute(block, ('pipe', 'expert'), route)  10.7 us
    ppermute x3, starting transfers between devices, swap(): lax.ppermute(block, 'expert', [(i, i ^ 2 * distance) for i in range(count)])  10.1 us
    ppermute x6, starting transfers between devices, pass_on(): return lax.ppermute(block, 'expert', route)  9.81 us
    ppermute x3, waiting for transfers between devices, cross(): return lax.ppermute(block, ('pipe', 'expert'), route)  8.44 us
  transfers between devices with their start and end apart: 15, of which 7 were waited for; matrix products, arithmetic and copies ran while one was open for 1% of the time, Pallas kernels for 3%

profile of v6, /device:TPU:2, one launch (start us, length us, event | category | flops | bytes accessed | tf_op | source)
XLA Modules:
  0.0 208.4 jit_solution(3081576327782548530)
XLA Ops:
  0.7 4.3 %shard_map.87 = (bf16[896,128]{1,0:T(8,128)(2,1)}, bf16[896,128]{1,0:T(8,128)(2,1)}, bf16[896,128]{1,0:T(8,128)(2,1)}, bf16[896,128]{1,0:T(8,128)(2,1)}, bf16[2,3584,128]{2,1,0:T(8,128)(2,1)}) custom-call(s32[1]{0:T(128)} %bitcast.5.place_ref, bf16[128,3584]{1,0:T(8,128)(2,1)} %bitcast.36, bf16[3584,128]{1,0:T(8,128)(2,1)} %bitcast.22, ...), custom_call_target="tpu_custom_call" | custom-call | bytes 5505024 | tf_op jit(solution)/shard_map/pallas_call | solution.py:83
  5.0 7.9 %collective-permute-start = (bf16[2,3584,128]{2,1,0:T(8,128)(2,1)}, bf16[2,3584,128]{2,1,0:T(8,128)(2,1)}, u32[]{:S(2)}, u32[]{:S(2)}) collective-permute-start(bf16[2,3584,128]{2,1,0:T(8,128)(2,1)} %get-tuple-element.36), channel_id=1, source_target_pairs={{0,1},{1,0},{2,3},{3,2},{4,5},{5,4},{6,7},{7,6},{8,9},{9,8},{10,11... | collective-permute-start | bytes 5505032 | tf_op jit(solution)/shard_map/ppermute | solution.py:47
  12.9 1.9 collective-permute-start.1
  14.8 1.9 collective-permute-start.2
  16.8 6.3 %collective-permute-start.3 = (bf16[896,128]{1,0:T(8,128)(2,1)}, bf16[896,128]{1,0:T(8,128)(2,1)}, u32[]{:S(2)}, u32[]{:S(2)}) collective-permute-start(bf16[896,128]{1,0:T(8,128)(2,1)} %get-tuple-element.40), channel_id=1, source_target_pairs={{0,6},{1,7},{2,4},{3,5},{4,2},{5,3},{6,0},{7,1},{8,14},{9,15},{10,... | collective-permute-start | bytes 688136 | tf_op jit(solution)/shard_map/ppermute | solution.py:52
  23.8 41.8 %conditional.1 = (bf16[16,16,896]{2,1,0:T(8,128)(2,1)S(1)}) conditional(s32[]{:T(128)} %convert_element_type.3, bf16[16,16,896]{2,1,0:T(8,128)(2,1)S(1)} %get-tuple-element.35, bf16[16,16,896]{2,1,0:T(8,128)(2,1)S(1)} %get-tuple-element.35), branch_computations={%region_0.1_spmd, %region_1.2_spmd} | conditional | bytes 917512 | solution.py:272
  23.8 41.8 %all_to_all.29 = bf16[16,16,896]{2,1,0:T(8,128)(2,1)S(1)} all-to-all(bf16[16,16,896]{2,1,0:T(8,128)(2,1)S(1)} %param.1), channel_id=1, replica_groups={{0,2,4,6,8,10,12,14,16,18,20,22,24,26,28,30},{1,3,5,7,9,11,13,15,17,19,..., dimensions={0} | all-to-all | bytes 917504 | tf_op jit(solution)/shard_map/cond/branch_1_fun/all_to_all | solution.py:31
  65.7 1.3 collective-permute-start.4
  67.0 4.6 %collective-permute-start.6 = (bf16[256,896]{1,0:T(8,128)(2,1)S(1)}, bf16[256,896]{1,0:T(8,128)(2,1)S(1)}, u32[]{:S(2)}, u32[]{:S(2)}) collective-permute-start(bf16[256,896]{1,0:T(8,128)(2,1)S(1)} %bitcast.33), channel_id=1, source_target_pairs={{0,2},{1,3},{2,4},{3,5},{4,6},{5,7},{8,10},{9,11},{10,12},{11,13},... | collective-permute-start | bytes 1376264 | tf_op jit(solution)/shard_map/ppermute | solution.py:42
  71.6 5.7 %collective-permute-done.4.up1 = bf16[256,896]{1,0:T(8,128)(2,1)S(1)} collective-permute-done((bf16[256,896]{1,0:T(8,128)(2,1)S(1)}, bf16[256,896]{1,0:T(8,128)(2,1)S(1)}, u32[]{:S(2)}, u32[]{:S(2)}) %collective-permute-start.4) | collective-permute-done | bytes 458784 | tf_op jit(solution)/shard_map/ppermute | solution.py:42
  77.3 1.3 collective-permute-start.5
  79.3 1.1 pad_maximum_fusion.down
  80.3 3.4 %collective-permute-start.10 = (bf16[4,896,128]{2,1,0:T(8,128)(2,1)S(1)}, bf16[4,896,128]{2,1,0:T(8,128)(2,1)S(1)}, u32[]{:S(2)}, u32[]{:S(2)}) collective-permute-start(bf16[4,896,128]{2,1,0:T(8,128)(2,1)S(1)} %pad_maximum_fusion.down), channel_id=1, source_target_pairs={{0,1},{1,0},{2,3},{3,2},{4,5},{5,4},{6,7},{7,6},{8,9},{9,8},{10,11... | collective-permute-start | bytes 2752520 | tf_op jit(solution)/shard_map/ppermute | solution.py:47
  83.7 4.2 %collective-permute-done.5.up2 = bf16[256,896]{1,0:T(8,128)(2,1)S(1)} collective-permute-done((bf16[256,896]{1,0:T(8,128)(2,1)S(1)}, bf16[256,896]{1,0:T(8,128)(2,1)S(1)}, u32[]{:S(2)}, u32[]{:S(2)}) %collective-permute-start.5) | collective-permute-done | bytes 458784 | tf_op jit(solution)/shard_map/ppermute | solution.py:42
  88.0 1.3 collective-permute-start.8
  90.0 3.6 %shard_map.88.acts = f32[256,512]{1,0:T(8,128)S(1)} custom-call(s32[1]{0:T(128)} %bitcast.5.place_ref, bf16[256,896]{1,0:T(8,128)(2,1)S(1)} %bitcast.34, bf16[256,896]{1,0:T(8,128)(2,1)S(1)} %collective-permute-done.4.up1, bf16[256,896]{1,0:T(8,128)(2,1)S(1)} %collective-permute-done.5.up2, bf16[256,896]{1,0:T(8,128)(2,1)S(1)} %collective-permute-done.6.down1, ...), custom_call_target="tpu_custom_call" | custom-call | flops 939524096 | bytes 3670016 | tf_op jit(solution)/shard_map/pallas_call | solution.py:83
  93.6 4.7 %collective-permute-done.8.up3 = bf16[256,896]{1,0:T(8,128)(2,1)S(1)} collective-permute-done((bf16[256,896]{1,0:T(8,128)(2,1)S(1)}, bf16[256,896]{1,0:T(8,128)(2,1)S(1)}, u32[]{:S(2)}, u32[]{:S(2)}) %collective-permute-start.8) | collective-permute-done | bytes 458784 | tf_op jit(solution)/shard_map/ppermute | solution.py:42
  98.3 2.2 %shard_map.89 = bf16[4,256,256]{2,1,0:T(8,128)(2,1)S(1)} custom-call(s32[1]{0:T(128)} %bitcast.5.place_ref, f32[256,512]{1,0:T(8,128)S(1)} %shard_map.88.acts, bf16[256,896]{1,0:T(8,128)(2,1)S(1)} %collective-permute-done.8.up3, bf16[256,896]{1,0:T(8,128)(2,1)S(1)} %collective-permute-done.9.down3, bf16[3584,128]{1,0:T(8,128)(2,1)S(1)} %bitcast.24, ...), custom_call_target="tpu_custom_call" | custom-call | flops 234881024 | bytes 917504 | tf_op jit(solution)/shard_map/pallas_call | solution.py:83
  100.8 15.0 %all_to_all.30.hidden = bf16[4,256,256]{2,1,0:T(8,128)(2,1)S(1)} all-to-all(bf16[4,256,256]{2,1,0:T(8,128)(2,1)S(1)} %shard_map.89), channel_id=1, replica_groups={{0,2,4,6},{1,3,5,7},{8,10,12,14},{9,11,13,15},{16,18,20,22},{17,19,21,2..., dimensions={0} | all-to-all | bytes 1048576 | tf_op jit(solution)/shard_map/all_to_all | solution.py:31
  115.8 1.5 shard_map.90
  117.3 7.0 %all-to-all-start.2 = ((bf16[16,16,896]{2,1,0:T(8,128)(2,1)}), bf16[16,16,896]{2,1,0:T(8,128)(2,1)S(1)}, u32[]{:S(2)}, u32[]{:S(2)}) async-start(bf16[16,16,896]{2,1,0:T(8,128)(2,1)} %shard_map.90), calls=%async_computation.2 | async-start | bytes 917504 | tf_op jit(solution)/shard_map/all_to_all | solution.py:31
  124.4 3.4 %collective-permute-start.11 = (bf16[4,256,128]{2,1,0:T(8,128)(2,1)S(1)}, bf16[4,256,128]{2,1,0:T(8,128)(2,1)S(1)}, u32[]{:S(2)}, u32[]{:S(2)}) collective-permute-start(bf16[4,256,128]{2,1,0:T(8,128)(2,1)S(1)} %get-tuple-element.58), channel_id=1, source_target_pairs={{0,1},{1,0},{2,3},{3,2},{4,5},{5,4},{6,7},{7,6},{8,9},{9,8},{10,11... | collective-permute-start | bytes 786440 | tf_op jit(solution)/shard_map/ppermute | solution.py:62
  127.8 5.1 %collective-permute-start.12 = (bf16[4,256,128]{2,1,0:T(8,128)(2,1)S(1)}, bf16[4,256,128]{2,1,0:T(8,128)(2,1)S(1)}, u32[]{:S(2)}, u32[]{:S(2)}) collective-permute-start(bf16[4,256,128]{2,1,0:T(8,128)(2,1)S(1)} %get-tuple-element.57.own), channel_id=1, source_target_pairs={{0,256},{1,257},{2,258},{3,259},{4,260},{5,261},{6,262},{7,263},{8... | collective-permute-start | bytes 786440 | tf_op jit(solution)/shard_map/ppermute | solution.py:62
  132.9 2.2 %collective-permute-start.13 = (bf16[4,256,128]{2,1,0:T(8,128)(2,1)S(1)}, bf16[4,256,128]{2,1,0:T(8,128)(2,1)S(1)}, u32[]{:S(2)}, u32[]{:S(2)}) collective-permute-start(bf16[4,256,128]{2,1,0:T(8,128)(2,1)S(1)} %get-tuple-element.58), channel_id=1, source_target_pairs={{0,257},{1,256},{2,259},{3,258},{4,261},{5,260},{6,263},{7,262},{8... | collective-permute-start | bytes 786440 | tf_op jit(solution)/shard_map/ppermute | solution.py:62
  135.1 4.4 %collective-permute-done.12.mirrored = bf16[4,256,128]{2,1,0:T(8,128)(2,1)S(1)} collective-permute-done((bf16[4,256,128]{2,1,0:T(8,128)(2,1)S(1)}, bf16[4,256,128]{2,1,0:T(8,128)(2,1)S(1)}, u32[]{:S(2)}, u32[]{:S(2)}) %collective-permute-start.12) | collective-permute-done | bytes 262176 | tf_op jit(solution)/shard_map/ppermute | solution.py:62
  139.6 4.0 %collective-permute-done.13.opposite = bf16[4,256,128]{2,1,0:T(8,128)(2,1)S(1)} collective-permute-done((bf16[4,256,128]{2,1,0:T(8,128)(2,1)S(1)}, bf16[4,256,128]{2,1,0:T(8,128)(2,1)S(1)}, u32[]{:S(2)}, u32[]{:S(2)}) %collective-permute-start.13) | collective-permute-done | bytes 262176 | tf_op jit(solution)/shard_map/ppermute | solution.py:62
  143.6 1.9 all-to-all-done.2.back
  145.5 2.0 shard_map.91
  147.5 30.2 %all_to_all.31 = bf16[16,16,896]{2,1,0:T(8,128)(2,1)S(1)} all-to-all(bf16[16,16,896]{2,1,0:T(8,128)(2,1)S(1)} %get-tuple-element.51), channel_id=1, replica_groups={{0,2,4,6,8,10,12,14,16,18,20,22,24,26,28,30},{1,3,5,7,9,11,13,15,17,19,..., dimensions={0} | all-to-all | bytes 917504 | tf_op jit(solution)/shard_map/all_to_all | solution.py:31
  177.9 14.8 %all_to_all.32.cotans = bf16[4,448,256]{2,1,0:T(8,128)(2,1)S(1)} all-to-all(bf16[4,448,256]{2,1,0:T(8,128)(2,1)S(1)} %shard_map.92), channel_id=1, replica_groups={{0,1,256,257},{2,3,258,259},{4,5,260,261},{6,7,262,263},{8,9,264,265},{..., dimensions={0} | all-to-all | bytes 1835008 | tf_op jit(solution)/shard_map/all_to_all | solution.py:31
  193.4 14.1 %all_to_all.33 = bf16[4,448,128]{2,1,0:T(8,128)(2,1)S(1)} all-to-all(bf16[4,448,128]{2,1,0:T(8,128)(2,1)S(1)} %shard_map.93), channel_id=1, replica_groups={{0,2,4,6},{1,3,5,7},{8,10,12,14},{9,11,13,15},{16,18,20,22},{17,19,21,2..., dimensions={0} | all-to-all | bytes 917504 | tf_op jit(solution)/shard_map/all_to_all | solution.py:31
  207.5 1.0 copy.9
  (29 shorter events, 3.4 us)
Async XLA Ops:
  0.6 22.4 %copy-start.3 = (s32[1,128,8]{1,2,0:T(8,128)S(1)}, s32[1,128,8]{1,2,0:T(8,128)}, u32[]{:S(2)}) copy-start(s32[1,128,8]{1,2,0:T(8,128)} %param.10) | copy-start | bytes 12292
  0.6 22.4 %copy-start.4 = (f32[1,128,8]{1,2,0:T(8,128)S(1)}, f32[1,128,8]{1,2,0:T(8,128)}, u32[]{:S(2)}) copy-start(f32[1,128,8]{1,2,0:T(8,128)} %param.11) | copy-start | bytes 12292
  0.7 22.4 %copy-start.2 = (bf16[1,128,3584]{2,1,0:T(8,128)(2,1)S(1)}, bf16[1,128,3584]{2,1,0:T(8,128)(2,1)}, u32[]{:S(2)}) copy-start(bf16[1,128,3584]{2,1,0:T(8,128)(2,1)} %param.9) | copy-start | bytes 2752516
  4.9 74.3 %copy-start.6 = (bf16[896,128]{1,0:T(8,128)(2,1)S(1)}, bf16[896,128]{1,0:T(8,128)(2,1)}, u32[]{:S(2)}) copy-start(bf16[896,128]{1,0:T(8,128)(2,1)} %get-tuple-element.43) | copy-start | bytes 688132
  5.0 60.7 %collective-permute-start = (bf16[2,3584,128]{2,1,0:T(8,128)(2,1)}, bf16[2,3584,128]{2,1,0:T(8,128)(2,1)}, u32[]{:S(2)}, u32[]{:S(2)}) collective-permute-start(bf16[2,3584,128]{2,1,0:T(8,128)(2,1)} %get-tuple-element.36), channel_id=1, source_target_pairs={{0,1},{1,0},{2,3},{3,2},{4,5},{5,4},{6,7},{7,6},{8,9},{9,8},{10,11... | collective-permute-start | bytes 5505032 | tf_op jit(solution)/shard_map/ppermute | solution.py:47
  12.9 52.7 %collective-permute-start.1 = (bf16[896,128]{1,0:T(8,128)(2,1)}, bf16[896,128]{1,0:T(8,128)(2,1)S(1)}, u32[]{:S(2)}, u32[]{:S(2)}) collective-permute-start(bf16[896,128]{1,0:T(8,128)(2,1)} %get-tuple-element.38), channel_id=1, source_target_pairs={{0,2},{1,3},{2,0},{3,1},{4,6},{5,7},{6,4},{7,5},{8,10},{9,11},{10,... | collective-permute-start | bytes 688136 | tf_op jit(solution)/shard_map/ppermute | solution.py:52
  14.8 50.8 %collective-permute-start.2 = (bf16[896,128]{1,0:T(8,128)(2,1)}, bf16[896,128]{1,0:T(8,128)(2,1)S(1)}, u32[]{:S(2)}, u32[]{:S(2)}) collective-permute-start(bf16[896,128]{1,0:T(8,128)(2,1)} %get-tuple-element.39), channel_id=1, source_target_pairs={{0,4},{1,5},{2,6},{3,7},{4,0},{5,1},{6,2},{7,3},{8,12},{9,13},{10,... | collective-permute-start | bytes 688136 | tf_op jit(solution)/shard_map/ppermute | solution.py:52
  16.8 48.9 %collective-permute-start.3 = (bf16[896,128]{1,0:T(8,128)(2,1)}, bf16[896,128]{1,0:T(8,128)(2,1)}, u32[]{:S(2)}, u32[]{:S(2)}) collective-permute-start(bf16[896,128]{1,0:T(8,128)(2,1)} %get-tuple-element.40), channel_id=1, source_target_pairs={{0,6},{1,7},{2,4},{3,5},{4,2},{5,3},{6,0},{7,1},{8,14},{9,15},{10,... | collective-permute-start | bytes 688136 | tf_op jit(solution)/shard_map/ppermute | solution.py:52
  23.8 66.2 %copy-start = (bf16[1,3584,128]{2,1,0:T(8,128)(2,1)S(1)}, bf16[1,3584,128]{2,1,0:T(8,128)(2,1)}, u32[]{:S(2)}) copy-start(bf16[1,3584,128]{2,1,0:T(8,128)(2,1)} %param.13) | copy-start | bytes 2752516
  23.8 66.2 %copy-start.1 = (bf16[1,3584,128]{2,1,0:T(8,128)(2,1)S(1)}, bf16[1,3584,128]{2,1,0:T(8,128)(2,1)}, u32[]{:S(2)}) copy-start(bf16[1,3584,128]{2,1,0:T(8,128)(2,1)} %param.14) | copy-start | bytes 2752516
  65.7 11.6 %collective-permute-start.4 = (bf16[256,896]{1,0:T(8,128)(2,1)S(1)}, bf16[256,896]{1,0:T(8,128)(2,1)S(1)}, u32[]{:S(2)}, u32[]{:S(2)}) collective-permute-start(bf16[256,896]{1,0:T(8,128)(2,1)S(1)} %bitcast.32), channel_id=1, source_target_pairs={{2,0},{3,1},{4,2},{5,3},{6,4},{7,5},{10,8},{11,9},{12,10},{13,11},... | collective-permute-start | bytes 1376264 | tf_op jit(solution)/shard_map/ppermute | solution.py:42
  67.0 11.6 %collective-permute-start.6 = (bf16[256,896]{1,0:T(8,128)(2,1)S(1)}, bf16[256,896]{1,0:T(8,128)(2,1)S(1)}, u32[]{:S(2)}, u32[]{:S(2)}) collective-permute-start(bf16[256,896]{1,0:T(8,128)(2,1)S(1)} %bitcast.33), channel_id=1, source_target_pairs={{0,2},{1,3},{2,4},{3,5},{4,6},{5,7},{8,10},{9,11},{10,12},{11,13},... | collective-permute-start | bytes 1376264 | tf_op jit(solution)/shard_map/ppermute | solution.py:42
  77.3 10.7 %collective-permute-start.5 = (bf16[256,896]{1,0:T(8,128)(2,1)S(1)}, bf16[256,896]{1,0:T(8,128)(2,1)S(1)}, u32[]{:S(2)}, u32[]{:S(2)}) collective-permute-start(bf16[256,896]{1,0:T(8,128)(2,1)S(1)} %collective-permute-done.4.up1), channel_id=1, source_target_pairs={{2,0},{3,1},{4,2},{5,3},{10,8},{11,9},{12,10},{13,11},{18,16},{19,... | collective-permute-start | bytes 1376264 | tf_op jit(solution)/shard_map/ppermute | solution.py:42
  78.6 10.7 %collective-permute-start.7 = (bf16[256,896]{1,0:T(8,128)(2,1)S(1)}, bf16[256,896]{1,0:T(8,128)(2,1)S(1)}, u32[]{:S(2)}, u32[]{:S(2)}) collective-permute-start(bf16[256,896]{1,0:T(8,128)(2,1)S(1)} %collective-permute-done.6.down1), channel_id=1, source_target_pairs={{2,4},{3,5},{4,6},{5,7},{10,12},{11,13},{12,14},{13,15},{18,20},{1... | collective-permute-start | bytes 1376264 | tf_op jit(solution)/shard_map/ppermute | solution.py:42
  80.3 20.5 %collective-permute-start.10 = (bf16[4,896,128]{2,1,0:T(8,128)(2,1)S(1)}, bf16[4,896,128]{2,1,0:T(8,128)(2,1)S(1)}, u32[]{:S(2)}, u32[]{:S(2)}) collective-permute-start(bf16[4,896,128]{2,1,0:T(8,128)(2,1)S(1)} %pad_maximum_fusion.down), channel_id=1, source_target_pairs={{0,1},{1,0},{2,3},{3,2},{4,5},{5,4},{6,7},{7,6},{8,9},{9,8},{10,11... | collective-permute-start | bytes 2752520 | tf_op jit(solution)/shard_map/ppermute | solution.py:47
  88.0 10.4 %collective-permute-start.8 = (bf16[256,896]{1,0:T(8,128)(2,1)S(1)}, bf16[256,896]{1,0:T(8,128)(2,1)S(1)}, u32[]{:S(2)}, u32[]{:S(2)}) collective-permute-start(bf16[256,896]{1,0:T(8,128)(2,1)S(1)} %collective-permute-done.5.up2), channel_id=1, source_target_pairs={{2,0},{3,1},{10,8},{11,9},{18,16},{19,17},{26,24},{27,25},{34,32},... | collective-permute-start | bytes 1376264 | tf_op jit(solution)/shard_map/ppermute | solution.py:42
  89.3 9.1 %collective-permute-start.9 = (bf16[256,896]{1,0:T(8,128)(2,1)S(1)}, bf16[256,896]{1,0:T(8,128)(2,1)S(1)}, u32[]{:S(2)}, u32[]{:S(2)}) collective-permute-start(bf16[256,896]{1,0:T(8,128)(2,1)S(1)} %collective-permute-done.7.down2), channel_id=1, source_target_pairs={{4,6},{5,7},{12,14},{13,15},{20,22},{21,23},{28,30},{29,31},{36,38... | collective-permute-start | bytes 1376264 | tf_op jit(solution)/shard_map/ppermute | solution.py:42
  115.8 29.7 %copy-start.5 = (f32[1,128]{1,0:T(1,128)S(1)}, f32[1,128]{1,0:T(1,128)}, u32[]{:S(2)}) copy-start(f32[1,128]{1,0:T(1,128)} %loss_ref.1) | copy-start | bytes 1540
  117.3 28.2 %all-to-all-start.2 = ((bf16[16,16,896]{2,1,0:T(8,128)(2,1)}), bf16[16,16,896]{2,1,0:T(8,128)(2,1)S(1)}, u32[]{:S(2)}, u32[]{:S(2)}) async-start(bf16[16,16,896]{2,1,0:T(8,128)(2,1)} %shard_map.90), calls=%async_computation.2 | async-start | bytes 917504 | tf_op jit(solution)/shard_map/all_to_all | solution.py:31
  124.4 10.7 %collective-permute-start.11 = (bf16[4,256,128]{2,1,0:T(8,128)(2,1)S(1)}, bf16[4,256,128]{2,1,0:T(8,128)(2,1)S(1)}, u32[]{:S(2)}, u32[]{:S(2)}) collective-permute-start(bf16[4,256,128]{2,1,0:T(8,128)(2,1)S(1)} %get-tuple-element.58), channel_id=1, source_target_pairs={{0,1},{1,0},{2,3},{3,2},{4,5},{5,4},{6,7},{7,6},{8,9},{9,8},{10,11... | collective-permute-start | bytes 786440 | tf_op jit(solution)/shard_map/ppermute | solution.py:62
  127.8 11.8 %collective-permute-start.12 = (bf16[4,256,128]{2,1,0:T(8,128)(2,1)S(1)}, bf16[4,256,128]{2,1,0:T(8,128)(2,1)S(1)}, u32[]{:S(2)}, u32[]{:S(2)}) collective-permute-start(bf16[4,256,128]{2,1,0:T(8,128)(2,1)S(1)} %get-tuple-element.57.own), channel_id=1, source_target_pairs={{0,256},{1,257},{2,258},{3,259},{4,260},{5,261},{6,262},{7,263},{8... | collective-permute-start | bytes 786440 | tf_op jit(solution)/shard_map/ppermute | solution.py:62
  132.9 10.7 %collective-permute-start.13 = (bf16[4,256,128]{2,1,0:T(8,128)(2,1)S(1)}, bf16[4,256,128]{2,1,0:T(8,128)(2,1)S(1)}, u32[]{:S(2)}, u32[]{:S(2)}) collective-permute-start(bf16[4,256,128]{2,1,0:T(8,128)(2,1)S(1)} %get-tuple-element.58), channel_id=1, source_target_pairs={{0,257},{1,256},{2,259},{3,258},{4,261},{5,260},{6,263},{7,262},{8... | collective-permute-start | bytes 786440 | tf_op jit(solution)/shard_map/ppermute | solution.py:62
